TPU v7x, 256 devices: a whole 4x4x8 slice. The times are simulated.
256 devices in a mesh: ctx: 16 (over y, x_hi, core), head: 16 (over z, x_lo).
Axes of the slice: x: 4 (x_hi: 2, x_lo: 2; x = x_hi * 2 + x_lo), y: 4, z: 8, core: 2. Of those that a mesh axis runs over, the one named last changes fastest.
Arguments:
- queries: bfloat16 [2048, 24576], P('ctx', 'head'), may hold values from -8 to 8
- kv_latent: bfloat16 [2048, 576], P('ctx'), may hold values from -7 to 7
- w_uk: bfloat16 [128, 512, 128], P('head'), may hold values from -0.25 to 0.25
- w_uv: bfloat16 [128, 512, 128], P('head'), may hold values from -0.25 to 0.25
- w_out: bfloat16 [16384, 7168], P('head', 'ctx'), may hold values from -0.046875 to 0.046875
- doc_lengths: int32 [8], replicated, may hold values from 1 to 1152, 2048 in all
Outputs:
- attn_out: bfloat16 [2048, 7168], P('ctx', 'head')
Inputs may be any that keep to these rules, and one draw needn't show every extreme that they name: `doc_lengths`: the lengths sum to 2048.
All inputs are finite; a program needn't handle non-finite values.
Results may differ from a plain program's by a relative error of at most 0.028.
Values may be sent and summed in bfloat16 or wider, within the bound.
No kernel may reach another device: no remote copies, remote signals or barrier semaphores. Data moves between devices by JAX's collectives and lax.ppermute only.
A program may use at most 128 MiB of HBM per device.

v0:
```python
import math

import jax
import jax.numpy as jnp
from jax import lax
from jax.sharding import PartitionSpec as P


def doc_index(positions, ends):
    return jnp.sum((positions[:, None] >= ends[None, :]).astype(jnp.int32), axis=1)


def body(queries, kv_latent, w_uk, w_uv, w_out, doc_lengths):
    rows_here = queries.shape[0]
    head_count, latent_width, nope_width = w_uk.shape
    rope_width = kv_latent.shape[1] - latent_width
    score_scale = 1.0 / math.sqrt(nope_width + rope_width)
    shaped = queries.reshape(rows_here, head_count, nope_width + rope_width)
    absorbed = jnp.einsum(
        "thn,hcn->htc", shaped[:, :, :nope_width], w_uk, preferred_element_type=jnp.float32
    ).astype(jnp.bfloat16)
    rope_part = jnp.transpose(shaped[:, :, nope_width:], (1, 0, 2))
    joined = jnp.concatenate([absorbed, rope_part], axis=2).reshape(
        head_count * rows_here, latent_width + rope_width
    )
    ends = jnp.cumsum(doc_lengths)
    query_pos = lax.axis_index("ctx") * rows_here + jnp.arange(rows_here, dtype=jnp.int32)
    query_doc = doc_index(query_pos, ends)

    def add_block(carry, block, block_start):
        key_pos = block_start + jnp.arange(block.shape[0], dtype=jnp.int32)
        key_doc = doc_index(key_pos, ends)
        visible = (key_pos[None, :] <= query_pos[:, None]) & (
            key_doc[None, :] == query_doc[:, None]
        )
        running, total, accum = carry
        scores = (
            jnp.einsum("qc,kc->qk", joined, block, preferred_element_type=jnp.float32) * score_scale
        )
        scores = scores.reshape(head_count, rows_here, block.shape[0])
        shown = jnp.where(visible[None], scores, -1e30)
        newest = jnp.maximum(running, jnp.max(shown, axis=2))
        weights = jnp.where(visible[None], jnp.exp(shown - newest[:, :, None]), 0.0)
        factor = jnp.exp(running - newest)
        total = total * factor + jnp.sum(weights, axis=2)
        products = jnp.dot(
            weights.astype(jnp.bfloat16).reshape(head_count * rows_here, block.shape[0]),
            block[:, :latent_width],
            preferred_element_type=jnp.float32,
        )
        accum = accum * factor[:, :, None] + products.reshape(head_count, rows_here, latent_width)
        return (newest, total, accum)

    initial = (
        jnp.full((head_count, rows_here), -1e30, jnp.float32),
        jnp.zeros((head_count, rows_here), jnp.float32),
        jnp.zeros((head_count, rows_here, latent_width), jnp.float32),
    )
    piece = lax.all_gather(kv_latent, "ctx", axis=0, tiled=True)
    piece_rows = piece.shape[0]
    width = math.gcd(piece_rows, 512)
    count = piece_rows // width
    blocks = piece.reshape(count, width, piece.shape[1])

    def scan_body(state, item):
        block, number = item
        return (add_block(state, block, number * width), None)

    result, unused = lax.scan(scan_body, initial, (blocks, jnp.arange(count, dtype=jnp.int32)))
    running, total, accum = result
    context = (accum / total[:, :, None]).astype(jnp.bfloat16)
    attended = jnp.einsum("htc,hcv->thv", context, w_uv, preferred_element_type=jnp.float32).astype(
        jnp.bfloat16
    )
    attended = attended.reshape(rows_here, head_count * w_uv.shape[2])
    partial_out = jnp.dot(
        attended,
        lax.all_gather(w_out, "ctx", axis=1, tiled=True),
        preferred_element_type=jnp.float32,
    )
    return lax.psum_scatter(
        partial_out.astype(jnp.bfloat16), "head", scatter_dimension=1, tiled=True
    )


def solution(mesh):
    placed = (
        P("ctx", "head"),
        P("ctx", None),
        P("head", None, None),
        P("head", None, None),
        P("head", "ctx"),
        P(),
    )
    return jax.shard_map(
        body, mesh=mesh, in_specs=placed, out_specs=P("ctx", "head"), check_vma=False
    )
```

profile of v0, /device:TPU:16, one launch (start us, length us, event | category | flops | bytes accessed | tf_op | source)
XLA Modules:
  0.0 260.3 jit_solution(15128621111904597557)
XLA Ops:
  6.5 0.7 all-gather.3.cloned.1.call-update
  7.3 0.7 all-gather.5.cloned.1.call-update
  8.1 1.2 copy.18
  9.3 0.2 copy.25
  9.5 0.2 reduce-window.8
  9.7 0.1 convert_reduce_fusion.1
  9.8 0.5 convolution_convert_fusion.1
  10.3 1.2 pad_maximum_fusion
  11.5 52.9 %all-gather.3.cloned.1.call-done = bf16[2048,576]{0,1:T(8,128)(2,1)} async-done(((bf16[128,576]{0,1:T(8,128)(2,1)}), bf16[2048,576]{0,1:T(8,128)(2,1)}) %all-gather.3.cloned.1.call-update) | async-done | bytes 2359312 | tf_op jit(solution)/shard_map/all_gather | solution.py:59
  64.4 4.3 %copy.17 = bf16[2048,576]{1,0:T(8,128)(2,1)} copy(bf16[2048,576]{0,1:T(8,128)(2,1)} %all-gather.3.cloned.1.call-done) | data formatting | bytes 4718592 | tf_op jit(solution)/shard_map/all_gather | solution.py:59
  68.8 54.4 %while.15 = (s32[]{:T(128)}, f32[8,128]{1,0:T(8,128)S(1)}, f32[8,128]{1,0:T(8,128)S(1)}, f32[8,128,512]{2,1,0:T(8,128)}, s32[4]{0:T(128)S(1)}, /*index=5*/s32[8]...) while((s32[]{:T(128)}, f32[8,128]{1,0:T(8,128)S(1)}, ...), condition=%wide.region_6.7_spmd.clone, body=%wide.region_2.6_spmd.clone.sunk | while | flops 1147359360 | bytes 20197096 | solution.py:69
  68.8 0.6 dynamic_slice.14
  70.1 0.2 compare_and_fusion.2
  70.3 0.2 broadcast_in_dim.61
  70.6 1.2 dynamic-slice_bitcast_fusion.2
  71.7 4.0 %fusion.25 = (f32[1024]{0:T(1024)S(1)}, f32[512,1024]{1,0:T(8,128)}) fusion(pred[64,8,8,128]{3,2,1,0:T(8,128)(4,1)S(1)} %bitcast.92, bf16[512,576]{1,0:T(8,128)(2,1)S(1)} %dynamic-slice_bitcast_fusion.2, bf16[1024,576]{1,0:T(8,128)(2,1)} %get-tuple-element.229), kind=kOutput, calls=%fused_computation.5.clone.1 | convolution fusion | flops 605551616 | bytes 4395008 | tf_op jit(solution)/shard_map/while/body/eval_jaxpr/qc,kc->qk/dot_general | solution.py:38
  75.7 2.3 fusion.27
  78.0 0.5 copy.38
  78.6 3.2 %fusion.28 = f32[8,128,512]{2,1,0:T(8,128)} fusion(f32[8,128,512]{2,1,0:T(8,128)} %get-tuple-element.211, bf16[8,128,512]{2,1,0:T(8,128)(2,1)S(1)} %bitcast.91, f32[8,128]{1,0:T(8,128)S(1)} %get-tuple-element.194, pred[]{:T(512)S(6)} %compare.3, bf16[512,576]{1,0:T(8,128)(2,1)} %copy-done.1), kind=kOutput, calls=%fused_computation.3.clone.1 | convolution fusion | flops 538443776 | bytes 5771265 | tf_op jit(solution)/shard_map/while/body/eval_jaxpr/dot_general | solution.py:46
  81.8 0.6 dynamic_slice.14
  83.0 0.1 convert_reduce_fusion.3
  83.1 0.2 compare_and_fusion.2
  83.3 0.2 broadcast_in_dim.61
  83.6 1.2 dynamic-slice_bitcast_fusion.2
  84.7 4.0 %fusion.25 = (f32[1024]{0:T(1024)S(1)}, f32[512,1024]{1,0:T(8,128)}) fusion(pred[64,8,8,128]{3,2,1,0:T(8,128)(4,1)S(1)} %bitcast.92, bf16[512,576]{1,0:T(8,128)(2,1)S(1)} %dynamic-slice_bitcast_fusion.2, bf16[1024,576]{1,0:T(8,128)(2,1)} %get-tuple-element.229), kind=kOutput, calls=%fused_computation.5.clone.1 | convolution fusion | flops 605551616 | bytes 4395008 | tf_op jit(solution)/shard_map/while/body/eval_jaxpr/qc,kc->qk/dot_general | solution.py:38
  88.7 2.3 fusion.27
  91.0 0.5 copy.38
  91.6 3.8 %fusion.28 = f32[8,128,512]{2,1,0:T(8,128)} fusion(f32[8,128,512]{2,1,0:T(8,128)} %get-tuple-element.211, bf16[8,128,512]{2,1,0:T(8,128)(2,1)S(1)} %bitcast.91, f32[8,128]{1,0:T(8,128)S(1)} %get-tuple-element.194, pred[]{:T(512)S(6)} %compare.3, bf16[512,576]{1,0:T(8,128)(2,1)} %copy-done.1), kind=kOutput, calls=%fused_computation.3.clone.1 | convolution fusion | flops 538443776 | bytes 5771265 | tf_op jit(solution)/shard_map/while/body/eval_jaxpr/dot_general | solution.py:46
  95.5 0.6 dynamic_slice.14
  96.8 0.2 compare_and_fusion.2
  97.0 0.2 broadcast_in_dim.61
  97.3 1.2 dynamic-slice_bitcast_fusion.2
  98.4 4.0 %fusion.25 = (f32[1024]{0:T(1024)S(1)}, f32[512,1024]{1,0:T(8,128)}) fusion(pred[64,8,8,128]{3,2,1,0:T(8,128)(4,1)S(1)} %bitcast.92, bf16[512,576]{1,0:T(8,128)(2,1)S(1)} %dynamic-slice_bitcast_fusion.2, bf16[1024,576]{1,0:T(8,128)(2,1)} %get-tuple-element.229), kind=kOutput, calls=%fused_computation.5.clone.1 | convolution fusion | flops 605551616 | bytes 4395008 | tf_op jit(solution)/shard_map/while/body/eval_jaxpr/qc,kc->qk/dot_general | solution.py:38
  102.4 2.3 fusion.27
  104.7 0.5 copy.38
  105.3 3.8 %fusion.28 = f32[8,128,512]{2,1,0:T(8,128)} fusion(f32[8,128,512]{2,1,0:T(8,128)} %get-tuple-element.211, bf16[8,128,512]{2,1,0:T(8,128)(2,1)S(1)} %bitcast.91, f32[8,128]{1,0:T(8,128)S(1)} %get-tuple-element.194, pred[]{:T(512)S(6)} %compare.3, bf16[512,576]{1,0:T(8,128)(2,1)} %copy-done.1), kind=kOutput, calls=%fused_computation.3.clone.1 | convolution fusion | flops 538443776 | bytes 5771265 | tf_op jit(solution)/shard_map/while/body/eval_jaxpr/dot_general | solution.py:46
  109.1 0.6 dynamic_slice.14
  110.5 0.2 compare_and_fusion.2
  110.7 0.2 broadcast_in_dim.61
  110.9 1.2 dynamic-slice_bitcast_fusion.2
  112.1 4.3 %fusion.25 = (f32[1024]{0:T(1024)S(1)}, f32[512,1024]{1,0:T(8,128)}) fusion(pred[64,8,8,128]{3,2,1,0:T(8,128)(4,1)S(1)} %bitcast.92, bf16[512,576]{1,0:T(8,128)(2,1)S(1)} %dynamic-slice_bitcast_fusion.2, bf16[1024,576]{1,0:T(8,128)(2,1)} %get-tuple-element.229), kind=kOutput, calls=%fused_computation.5.clone.1 | convolution fusion | flops 605551616 | bytes 4395008 | tf_op jit(solution)/shard_map/while/body/eval_jaxpr/qc,kc->qk/dot_general | solution.py:38
  116.4 2.4 fusion.27
  118.8 0.5 copy.38
  119.3 3.8 %fusion.28 = f32[8,128,512]{2,1,0:T(8,128)} fusion(f32[8,128,512]{2,1,0:T(8,128)} %get-tuple-element.211, bf16[8,128,512]{2,1,0:T(8,128)(2,1)S(1)} %bitcast.91, f32[8,128]{1,0:T(8,128)S(1)} %get-tuple-element.194, pred[]{:T(512)S(6)} %compare.3, bf16[512,576]{1,0:T(8,128)(2,1)} %copy-done.1), kind=kOutput, calls=%fused_computation.3.clone.1 | convolution fusion | flops 538443776 | bytes 5771265 | tf_op jit(solution)/shard_map/while/body/eval_jaxpr/dot_general | solution.py:46
  123.2 2.5 convolution_convert_fusion.2
  125.7 44.0 %all-gather.5.cloned.1.call-done = bf16[1024,7168]{0,1:T(8,128)(2,1)} async-done(((bf16[1024,448]{0,1:T(8,128)(2,1)}), bf16[1024,7168]{0,1:T(8,128)(2,1)}) %all-gather.5.cloned.1.call-update) | async-done | bytes 14680080 | tf_op jit(solution)/shard_map/all_gather | solution.py:78
  169.7 10.4 %convolution_convert_fusion = bf16[128,7168]{0,1:T(8,128)(2,1)} fusion(bf16[1024,7168]{0,1:T(8,128)(2,1)} %all-gather.5.cloned.1.call-done, bf16[128,1024]{0,1:T(8,128)(2,1)S(1)} %bitcast.101), kind=kOutput, calls=%fused_computation.18 | convolution fusion | flops 1879965696 | bytes 16777216 | tf_op jit(solution)/shard_map/dot_general | solution.py:76
  180.1 73.6 %reduce-scatter.2.cloned.1.call-done = bf16[128,448]{0,1:T(8,128)(2,1)} async-done(((bf16[128,7168]{0,1:T(8,128)(2,1)}), bf16[128,448]{0,1:T(8,128)(2,1)}) %reduce-scatter.2.cloned.1.call-update) | async-done | bytes 114704 | tf_op jit(solution)/shard_map/reduce_scatter | solution.py:81
  (45 shorter events, 0.5 us)
Async XLA Ops:
  6.5 3.3 %copy-start = (bf16[8,512,128]{2,1,0:T(8,128)(2,1)S(1)}, bf16[8,512,128]{2,1,0:T(8,128)(2,1)}, u32[]{:S(2)}) copy-start(bf16[8,512,128]{2,1,0:T(8,128)(2,1)} %param.10) | copy-start | bytes 3145732
  6.5 3.0 %copy-start.2 = (s32[8]{0:T(128)S(1)}, s32[8]{0:T(128)}, u32[]{:S(2)}) copy-start(s32[8]{0:T(128)} %param.13) | copy-start | bytes 100
  6.5 57.9 %all-gather.3.cloned.1.call-start = ((), (), s32[]{:S(2)}) async-start(), calls=%async_computation.1 | async-start | bytes 2506752 | tf_op jit(solution)/shard_map/all_gather | solution.py:59
  7.3 162.4 %all-gather.5.cloned.1.call-start = ((), (), s32[]{:S(2)}) async-start(), calls=%async_computation.2 | async-start | bytes 15597568 | tf_op jit(solution)/shard_map/all_gather | solution.py:78
  8.0 245.7 %reduce-scatter.2.cloned.1.call-start = ((), (), s32[]{:S(2)}) async-start(), calls=%async_computation.3 | async-start | bytes 1949696 | tf_op jit(solution)/shard_map/reduce_scatter | solution.py:81
  71.7 4.0 %copy-start.1 = (bf16[512,576]{1,0:T(8,128)(2,1)}, bf16[512,576]{1,0:T(8,128)(2,1)S(1)}, u32[]{:S(2)}) copy-start(bf16[512,576]{1,0:T(8,128)(2,1)S(1)} %dynamic-slice_bitcast_fusion.2) | copy-start | bytes 1769476 | tf_op jit(solution)/shard_map/while
  84.7 4.0 %copy-start.1 = (bf16[512,576]{1,0:T(8,128)(2,1)}, bf16[512,576]{1,0:T(8,128)(2,1)S(1)}, u32[]{:S(2)}) copy-start(bf16[512,576]{1,0:T(8,128)(2,1)S(1)} %dynamic-slice_bitcast_fusion.2) | copy-start | bytes 1769476 | tf_op jit(solution)/shard_map/while
  98.4 4.0 %copy-start.1 = (bf16[512,576]{1,0:T(8,128)(2,1)}, bf16[512,576]{1,0:T(8,128)(2,1)S(1)}, u32[]{:S(2)}) copy-start(bf16[512,576]{1,0:T(8,128)(2,1)S(1)} %dynamic-slice_bitcast_fusion.2) | copy-start | bytes 1769476 | tf_op jit(solution)/shard_map/while
  112.1 4.3 %copy-start.1 = (bf16[512,576]{1,0:T(8,128)(2,1)}, bf16[512,576]{1,0:T(8,128)(2,1)S(1)}, u32[]{:S(2)}) copy-start(bf16[512,576]{1,0:T(8,128)(2,1)S(1)} %dynamic-slice_bitcast_fusion.2) | copy-start | bytes 1769476 | tf_op jit(solution)/shard_map/while
Sparse Core Ops, SparseCore 0:
  10.0 54.3 all-gather.2
  67.2 102.4 all-gather.4
  180.2 73.4 reduce-scatter.1
where the time goes:
time: 261 us; the launch traced here: 260 us
  waiting for transfers between devices  172 us (66%)
  matrix products  44.3 us (17%)
  local copies, waits for them, and re-layouts  15.9 us (6%)
  between operations  13.2 us (5%)
  other arithmetic  12 us (5%)
  loops' own time  2.76 us (1%)
    reduce_scatter x1, waiting for transfers between devices, body(): lax.psum_scatter(partial_out.astype(jnp.bfloat16), 'head', scatter_dimens...  73.6 us
    all_gather x1, waiting for transfers between devices, body(): piece = lax.all_gather(kv_latent, 'ctx', axis=0, tiled=True)  52.9 us
    all_gather x1, waiting for transfers between devices, body(): lax.all_gather(w_out, 'ctx', axis=1, tiled=True)  44 us
    dot_general x4, matrix products, add_block(): jnp.einsum('qc,kc->qk', joined, block, preferred_element_type=jnp.float32)  16.3 us
    dot_general x4, matrix products, add_block(): jnp.dot(weights.astype(jnp.bfloat16).reshape(head_count * rows_here, bloc...  14.6 us
    dot_general x1, matrix products, body(): jnp.dot(attended, lax.all_gather(w_out, 'ctx', axis=1, tiled=True), prefe...  10.4 us
    convert_element_type x4, other arithmetic, add_block(): weights.astype(jnp.bfloat16).reshape(head_count * rows_here, block.shape[0])  9.24 us
  transfers between devices with their start and end apart: 3, of which 3 were waited for; matrix products, arithmetic and copies ran while one was open for 24% of the time, Pallas kernels for 0%

commit v1 on v0

v1 whole, which is shorter than its diff:
```python
import functools
import math

import jax
import jax.numpy as jnp
from jax import lax
from jax.experimental import pallas as pl
from jax.experimental.pallas import tpu as pltpu
from jax.sharding import PartitionSpec as P

AXES = ("ctx", "head")
VMEM = pltpu.MemorySpace.VMEM
SMEM = pltpu.MemorySpace.SMEM
NEVER = -1e30


def index_of(y, xh, core, z, xl):
    return ((y * 2 + xh) * 2 + core) * 16 + z * 2 + xl


PLACES = [
    (y, xh, core, z, xl)
    for y in range(4)
    for xh in range(2)
    for core in range(2)
    for z in range(8)
    for xl in range(2)
]


def send(value, target):
    pairs = []
    for place in PLACES:
        goal = target(*place)
        if goal is not None:
            pairs.append((index_of(*place), index_of(*goal)))
    return lax.ppermute(value, AXES, pairs)


def other_core(y, xh, core, z, xl):
    return (y, xh, 1 - core, z, xl)


def other_lo(y, xh, core, z, xl):
    return (y, xh, core, z, 1 - xl)


def absorb_kernel(q_ref, w_uk_ref, qc_ref, qr_ref):
    heads, rows = w_uk_ref.shape[0], q_ref.shape[0]
    for h in range(heads):
        nope = q_ref[:, h * 192 : h * 192 + 128]
        qc_ref[h * rows : (h + 1) * rows, :] = lax.dot_general(
            nope, w_uk_ref[h], (((1,), (1,)), ((), ())), preferred_element_type=jnp.float32
        ).astype(jnp.bfloat16)
        qr_ref[h * rows : (h + 1) * rows, :] = q_ref[:, h * 192 + 128 : (h + 1) * 192]


def attend_kernel(info_ref, qc_ref, qr_ref, w_uv_ref, *rest):
    units = (len(rest) - 5) // 2
    blocks = rest[: 2 * units]
    out_ref, kv_ref, scores_ref, accum_ref, sems = rest[2 * units :]
    rows, latent = qc_ref.shape
    heads = w_uv_ref.shape[0]
    tokens = rows // heads
    query_base = info_ref[8]
    copies = []
    for u in range(units):
        for half in range(2):
            copies.append(
                pltpu.make_async_copy(
                    blocks[2 * u + half],
                    kv_ref.at[u, :, pl.ds(half * 128, 128)],
                    sems.at[2 * u + half],
                )
            )
    for copy in copies:
        copy.start()
    query_pos = query_base + lax.broadcasted_iota(jnp.int32, (tokens, 1), 0)
    start = jnp.zeros((tokens, 1), jnp.int32)
    first = jnp.int32(0)
    end = jnp.int32(0)
    for k in range(8):
        end = end + info_ref[k]
        start = jnp.where(query_pos >= end, end, start)
        first = jnp.where(query_base >= end, end, first)
    for copy in copies:
        copy.wait()
    lane = lax.broadcasted_iota(jnp.int32, (1, 256), 1)
    scale = 1.0 / math.sqrt(192.0) * math.log2(math.e)

    def seen(u):
        base = info_ref[16 + u]
        return (base <= query_base + tokens - 1) & (base + 256 > first)

    def base_of(u):
        return info_ref[16 + u], info_ref[32 + u]

    def look(u, highest):
        def yes():
            base, flip = base_of(u)
            key_pos = base + jnp.where(flip > 0, lax.rem(lane + 128, 256), lane)
            visible = (key_pos <= query_pos) & (key_pos >= start)
            s = jnp.dot(qc_ref[...], kv_ref[u, :latent, :], preferred_element_type=jnp.float32)
            s = s + jnp.dot(qr_ref[...], kv_ref[u, latent:, :], preferred_element_type=jnp.float32)
            s = jnp.where(visible[None], s.reshape(heads, tokens, 256), NEVER)
            scores_ref[u] = s.reshape(rows, 256)
            top = jnp.maximum(s[:, :, :128], s[:, :, 128:]).reshape(rows, 128)
            return jnp.maximum(highest, top)

        return lax.cond(seen(u), yes, lambda: highest)

    highest = lax.fori_loop(0, units, look, jnp.full((rows, 128), NEVER, jnp.float32))
    peak = jnp.max(highest, axis=1, keepdims=True) * scale
    accum_ref[...] = jnp.zeros_like(accum_ref)

    def gather(u, total):
        def yes():
            p = jnp.exp2(scores_ref[u] * scale - peak)
            accum_ref[...] += lax.dot_general(
                p.astype(jnp.bfloat16),
                kv_ref[u, :latent, :],
                (((1,), (1,)), ((), ())),
                preferred_element_type=jnp.float32,
            )
            return total + p[:, :128] + p[:, 128:]

        return lax.cond(seen(u), yes, lambda: total)

    total = lax.fori_loop(0, units, gather, jnp.zeros((rows, 128), jnp.float32))
    inverse = 1.0 / jnp.sum(total, axis=1, keepdims=True)
    for h in range(heads):
        context = (
            accum_ref[h * tokens : (h + 1) * tokens, :] * inverse[h * tokens : (h + 1) * tokens]
        ).astype(jnp.bfloat16)
        out_ref[:, h * 128 : (h + 1) * 128] = jnp.dot(
            context, w_uv_ref[h], preferred_element_type=jnp.float32
        ).astype(jnp.bfloat16)


def whole(space):
    return pl.BlockSpec(memory_space=space)


def body(queries, kv_latent, w_uk, w_uv, w_out, doc_lengths):
    rows = queries.shape[0]
    heads, latent, nope = w_uk.shape
    ctx = lax.axis_index("ctx")
    head = lax.axis_index("head")
    y, xh, core = ctx // 4, (ctx // 2) % 2, ctx % 2
    z, xl = head // 2, head % 2
    width = w_out.shape[1]

    mine = kv_latent.T

    def from_y(step, flip):
        def target(ty, txh, tcore, tz, txl):
            if ty + step > 3:
                return None
            if flip:
                return (ty + step, 1 - txh, tcore, tz, 1 - txl)
            return (ty + step, txh, tcore, tz, txl)

        return target

    got = [mine, send(mine, lambda ty, txh, tcore, tz, txl: (ty, 1 - txh, tcore, tz, 1 - txl))]
    for step in (1, 2):
        got.append(send(mine, from_y(step, False)))
        got.append(send(mine, from_y(step, True)))

    def farthest(ty, txh, tcore, tz, txl):
        if (ty, txh, tcore) == (0, 1, 1):
            return (3, 0, 0, tz, 1 - txl)
        return None

    far = send(mine, farthest)
    theirs = [send(block, other_core) for block in got]
    blocks = []
    bases = []
    for number, (a, b) in enumerate(zip(got, theirs)):
        step, flip = number // 2, number % 2
        blocks.extend([a, b])
        source = y - step
        source_xh = xh if flip == 0 else 1 - xh
        base = jnp.where(source < 0, 1 << 20, source * 512 + source_xh * 256)
        bases.append(base)
    blocks.extend([far, far])
    bases.append(jnp.where((y == 3) & (xh == 0) & (core == 0), 256, 1 << 20))
    units = len(bases)
    flips = [core] * (units - 1) + [0]
    info = jnp.concatenate(
        [
            doc_lengths,
            jnp.stack([ctx * rows] + [0] * 7).astype(jnp.int32),
            jnp.stack(bases + [0] * (16 - units)).astype(jnp.int32),
            jnp.stack(flips + [0] * (16 - units)).astype(jnp.int32),
        ]
    )

    w_own = w_out.T
    w_got = []
    for s in range(2):

        def target(ty, a, c, tz, xx, s=s):
            return (ty, xx ^ s, a, tz, c)

        w_got.append(send(w_own, target))
    w_theirs = [send(block, other_core) for block in w_got]

    qc, qr = pl.pallas_call(
        absorb_kernel,
        out_shape=(
            jax.ShapeDtypeStruct((heads * rows, latent), jnp.bfloat16),
            jax.ShapeDtypeStruct((heads * rows, 64), jnp.bfloat16),
        ),
        in_specs=[whole(VMEM), whole(VMEM)],
        out_specs=(whole(VMEM), whole(VMEM)),
        compiler_params=pltpu.CompilerParams(vmem_limit_bytes=32 << 20),
        name="absorb",
    )(queries, w_uk)

    values = pl.pallas_call(
        attend_kernel,
        out_shape=jax.ShapeDtypeStruct((rows, heads * 128), jnp.bfloat16),
        in_specs=[whole(SMEM)] + [whole(VMEM)] * 3 + [whole(pl.ANY)] * (2 * units),
        out_specs=whole(VMEM),
        scratch_shapes=[
            pltpu.VMEM((units, latent + 64, 256), jnp.bfloat16),
            pltpu.VMEM((units, heads * rows, 256), jnp.float32),
            pltpu.VMEM((heads * rows, latent), jnp.float32),
            pltpu.SemaphoreType.DMA((2 * units,)),
        ],
        compiler_params=pltpu.CompilerParams(vmem_limit_bytes=48 << 20),
        name="attend",
    )(info, qc, qr, w_uv, *blocks)

    def shifted(step):
        return lambda ty, txh, tcore, tz, txl: ((ty + step) % 4, txh, tcore, tz, txl)

    near = [values] + [send(values, shifted(step)) for step in (1, 2, 3)]
    across = [send(block, other_lo) for block in near]
    own_x = jnp.concatenate(near, axis=0)
    other_x = jnp.concatenate(across, axis=0)
    same = (xh ^ xl) == 0
    x0 = jnp.where(same, own_x, other_x)
    x1 = jnp.where(same, other_x, own_x)

    def times(w0, w1):
        dims = (((1,), (1,)), ((), ()))
        return lax.dot_general(
            x0, w0, dims, preferred_element_type=jnp.float32
        ) + lax.dot_general(x1, w1, dims, preferred_element_type=jnp.float32)

    here = times(w_got[0], w_got[1]).astype(jnp.bfloat16)
    there = times(w_theirs[0], w_theirs[1]).astype(jnp.bfloat16)
    first = core == 0
    partial = jnp.concatenate(
        [jnp.where(first, here, there), jnp.where(first, there, here)], axis=1
    )

    half = rows // 2

    def piece(goal):
        b, d = goal // 2, goal % 2
        at = ((y - b) % 4) * rows + d * half
        return lax.dynamic_slice_in_dim(partial, at, half, axis=0)

    total = piece(z).astype(jnp.float32)
    for step in range(1, 8):
        arrived = send(
            piece((z + step) % 8),
            lambda ty, txh, tcore, tz, txl, step=step: (ty, txh, tcore, (tz + step) % 8, txl),
        )
        total = total + arrived.astype(jnp.float32)
    total = total.astype(jnp.bfloat16)

    even = (z % 2) == 0
    left, right = total[:, :width], total[:, width:]
    out = []
    for s in range(2):

        def target(ty, txh, tcore, tz, txl, s=s):
            b, d = tz // 2, tz % 2
            return (b, txh, tcore, 2 * ty + (d ^ s), txl)

        chosen = jnp.where(even, left, right) if s == 0 else jnp.where(even, right, left)
        out.append(send(chosen, target))
    return jnp.where(
        even,
        jnp.concatenate([out[0], out[1]], axis=0),
        jnp.concatenate([out[1], out[0]], axis=0),
    )


def solution(mesh):
    placed = (
        P("ctx", "head"),
        P("ctx", None),
        P("head", None, None),
        P("head", None, None),
        P("head", "ctx"),
        P(),
    )
    return jax.shard_map(
        body, mesh=mesh, in_specs=placed, out_specs=P("ctx", "head"), check_vma=False
    )
```

time: 261 us -> 158 us (0.61)
  the two profiles are of different devices: /device:TPU:16 before, /device:TPU:24 now
where the time goes in v1:
time: 158 us
  waiting for transfers between devices  67.8 us (43%)
  starting transfers between devices  62 us (39%)
  Pallas kernels  10.8 us (7%)
  matrix products  7.5 us (5%)
  local copies, waits for them, and re-layouts  6.74 us (4%)
  other arithmetic  2.4 us (2%)
    ppermute x32, waiting for transfers between devices, send(): return lax.ppermute(value, AXES, pairs)  67.8 us
    ppermute x32, starting transfers between devices, send(): return lax.ppermute(value, AXES, pairs)  62 us
    pallas_call x1, Pallas kernels, body(): pl.pallas_call(attend_kernel, out_shape=jax.ShapeDtypeStruct((rows, heads...  10.4 us
    unnamed x25, local copies, waits for them, and re-layouts  6.61 us
    dot_general x2, matrix products, times(): lax.dot_general(x1, w1, dims, preferred_element_type=jnp.float32)  3.9 us
    dot_general x2, matrix products, times(): lax.dot_general(x0, w0, dims, preferred_element_type=jnp.float32)  3.59 us
  transfers between devices with their start and end apart: 32, of which 16 were waited for; matrix products, arithmetic and copies ran while one was open for 4% of the time, Pallas kernels for 7%

profile of v1, /device:TPU:24, one launch (start us, length us, event | category | flops | bytes accessed | tf_op | source)
XLA Modules:
  0.0 157.5 jit_solution(17823610615984482526)
XLA Ops:
  0.0 1.4 collective-permute-start.9
  1.4 2.8 %collective-permute-start.1 = (bf16[576,128]{1,0:T(8,128)(2,1)}, bf16[576,128]{1,0:T(8,128)(2,1)S(1)}, u32[]{:S(2)}, u32[]{:S(2)}) collective-permute-start(bf16[576,128]{1,0:T(8,128)(2,1)} %bitcast.16), channel_id=1, source_target_pairs={{0,33},{1,32},{2,35},{3,34},{4,37},{5,36},{6,39},{7,38},{8,41},{9,... | collective-permute-start | bytes 442376 | tf_op jit(solution)/shard_map/ppermute | solution.py:37
  4.3 1.3 collective-permute-start.3
  5.6 1.3 collective-permute-start.5
  6.9 1.3 collective-permute-start.7
  8.2 3.8 %collective-permute-done.9.rest_10_ = bf16[576,128]{1,0:T(8,128)(2,1)S(1)} collective-permute-done((bf16[576,128]{1,0:T(8,128)(2,1)}, bf16[576,128]{1,0:T(8,128)(2,1)S(1)}, u32[]{:S(2)}, u32[]{:S(2)}) %collective-permute-start.9) | collective-permute-done | bytes 147488 | tf_op jit(solution)/shard_map/ppermute | solution.py:37
  11.9 1.3 collective-permute-start.11
  13.3 1.7 %collective-permute-done.5.rest_6_ = bf16[576,128]{1,0:T(8,128)(2,1)S(1)} collective-permute-done((bf16[576,128]{1,0:T(8,128)(2,1)}, bf16[576,128]{1,0:T(8,128)(2,1)S(1)}, u32[]{:S(2)}, u32[]{:S(2)}) %collective-permute-start.5) | collective-permute-done | bytes 147488 | tf_op jit(solution)/shard_map/ppermute | solution.py:37
  15.7 1.3 collective-permute-done.7.rest_8_
  17.0 0.7 copy-done.6
  18.1 3.8 %collective-permute-done.11.rest_12_.rest_13_ = bf16[576,128]{1,0:T(8,128)(2,1)S(1)} collective-permute-done((bf16[576,128]{1,0:T(8,128)(2,1)}, bf16[576,128]{1,0:T(8,128)(2,1)S(1)}, u32[]{:S(2)}, u32[]{:S(2)}) %collective-permute-start.11) | collective-permute-done | bytes 147488 | tf_op jit(solution)/shard_map/ppermute | solution.py:37
  21.9 0.6 copy-done.8
  23.1 1.2 copy-done.1
  24.3 1.0 copy-done.2
  26.2 0.9 copy-done.5
  27.1 0.9 copy-done.7
  28.1 0.9 copy-done.9
  29.0 10.4 %attend.1 = bf16[128,1024]{1,0:T(8,128)(2,1)S(1)} custom-call(s32[48]{0:T(128)S(1)} %concatenate.18.info_ref, bf16[1024,512]{1,0:T(8,128)(2,1)S(1)} %get-tuple-element.7.qc_ref, bf16[1024,64]{1,0:T(8,128)(2,1)S(1)} %get-tuple-element.8.qr_ref, bf16[8,512,128]{2,1,0:T(8,128)(2,1)S(1)} %copy-done, bf16[576,128]{1,0:T(8,128)(2,1)S(1)} %bitcast.22, ...), custom_call_target="tpu_custom_call" | custom-call | tf_op jit(solution)/shard_map/attend/pallas_call | solution.py:221
  39.4 1.8 %collective-permute-start.19 = (bf16[448,1024]{1,0:T(8,128)(2,1)}, bf16[448,1024]{1,0:T(8,128)(2,1)S(1)}, u32[]{:S(2)}, u32[]{:S(2)}) collective-permute-start(bf16[448,1024]{1,0:T(8,128)(2,1)} %bitcast.10), channel_id=1, source_target_pairs={{0,0},{1,32},{2,2},{3,34},{4,4},{5,36},{6,6},{7,38},{8,8},{9,40},{... | collective-permute-start | bytes 2752520 | tf_op jit(solution)/shard_map/ppermute | solution.py:37
  41.3 1.5 collective-permute-start.13
  42.8 5.8 %collective-permute-done.15 = bf16[128,1024]{1,0:T(8,128)(2,1)S(1)} collective-permute-done((bf16[128,1024]{1,0:T(8,128)(2,1)S(1)}, bf16[128,1024]{1,0:T(8,128)(2,1)S(1)}, u32[]{:S(2)}, u32[]{:S(2)}) %collective-permute-start.15) | collective-permute-done | bytes 262176 | tf_op jit(solution)/shard_map/ppermute | solution.py:37
  49.2 3.9 %collective-permute-start.16 = (bf16[128,1024]{1,0:T(8,128)(2,1)}, bf16[128,1024]{1,0:T(8,128)(2,1)S(1)}, u32[]{:S(2)}, u32[]{:S(2)}) collective-permute-start(bf16[128,1024]{1,0:T(8,128)(2,1)} %collective-permute-done.12), channel_id=1, source_target_pairs={{0,1},{1,0},{2,3},{3,2},{4,5},{5,4},{6,7},{7,6},{8,9},{9,8},{10,11... | collective-permute-start | bytes 786440 | tf_op jit(solution)/shard_map/ppermute | solution.py:37
  53.1 2.1 %collective-permute-start.17 = (bf16[128,1024]{1,0:T(8,128)(2,1)}, bf16[128,1024]{1,0:T(8,128)(2,1)S(1)}, u32[]{:S(2)}, u32[]{:S(2)}) collective-permute-start(bf16[128,1024]{1,0:T(8,128)(2,1)} %collective-permute-done.13), channel_id=1, source_target_pairs={{0,1},{1,0},{2,3},{3,2},{4,5},{5,4},{6,7},{7,6},{8,9},{9,8},{10,11... | collective-permute-start | bytes 786440 | tf_op jit(solution)/shard_map/ppermute | solution.py:37
  55.2 2.6 %collective-permute-done.14 = bf16[128,1024]{1,0:T(8,128)(2,1)} collective-permute-done((bf16[128,1024]{1,0:T(8,128)(2,1)S(1)}, bf16[128,1024]{1,0:T(8,128)(2,1)}, u32[]{:S(2)}, u32[]{:S(2)}) %collective-permute-start.14) | collective-permute-done | bytes 262176 | tf_op jit(solution)/shard_map/ppermute | solution.py:37
  57.8 1.6 collective-permute-start.18
  59.4 1.1 collective-permute-done.16
  60.5 5.4 %collective-permute-start.22 = (bf16[448,1024]{1,0:T(8,128)(2,1)}, bf16[448,1024]{1,0:T(8,128)(2,1)S(1)}, u32[]{:S(2)}, u32[]{:S(2)}) collective-permute-start(bf16[448,1024]{1,0:T(8,128)(2,1)} %collective-permute-done.20), channel_id=1, source_target_pairs={{0,16},{1,17},{2,18},{3,19},{4,20},{5,21},{6,22},{7,23},{8,24},{9,... | collective-permute-start | bytes 2752520 | tf_op jit(solution)/shard_map/ppermute | solution.py:37
  66.2 5.6 %collective-permute-done.18 = bf16[128,1024]{1,0:T(8,128)(2,1)S(1)} collective-permute-done((bf16[128,1024]{1,0:T(8,128)(2,1)}, bf16[128,1024]{1,0:T(8,128)(2,1)S(1)}, u32[]{:S(2)}, u32[]{:S(2)}) %collective-permute-start.18) | collective-permute-done | bytes 262176 | tf_op jit(solution)/shard_map/ppermute | solution.py:37
  71.8 2.5 %collective-permute-start.21 = (bf16[448,1024]{1,0:T(8,128)(2,1)S(1)}, bf16[448,1024]{1,0:T(8,128)(2,1)S(1)}, u32[]{:S(2)}, u32[]{:S(2)}) collective-permute-start(bf16[448,1024]{1,0:T(8,128)(2,1)S(1)} %collective-permute-done.19), channel_id=1, source_target_pairs={{0,16},{1,17},{2,18},{3,19},{4,20},{5,21},{6,22},{7,23},{8,24},{9,... | collective-permute-start | bytes 2752520 | tf_op jit(solution)/shard_map/ppermute | solution.py:37
  74.3 2.1 %fusion.3 = f32[512,448]{0,1:T(8,128)S(1)} fusion(bf16[448,1024]{1,0:T(8,128)(2,1)} %collective-permute-done.20, bf16[512,1024]{1,0:T(8,128)(2,1)S(1)} %constant_dynamic-update-slice_fusion, pred[]{:T(512)S(6)} %eq.46, bf16[128,1024]{1,0:T(8,128)(2,1)} %collective-permute-done.14, bf16[128,1024]{1,0:T(8,128)(2,1)} %collective-permute-done.13, ...), kind=kOutput, calls=%fused_computation.27 | convolution fusion | flops 474480640 | bytes 3932161 | tf_op jit(solution)/shard_map/dot_general | solution.py:251
  76.4 1.8 %fusion = bf16[512,448]{0,1:T(8,128)(2,1)S(1)} fusion(f32[512,448]{0,1:T(8,128)S(1)} %fusion.3, bf16[448,1024]{1,0:T(8,128)(2,1)S(1)} %collective-permute-done.19, bf16[512,1024]{1,0:T(8,128)(2,1)S(1)} %constant_dynamic-update-slice_fusion, pred[]{:T(512)S(6)} %eq.46, bf16[128,1024]{1,0:T(8,128)(2,1)} %collective-permute-done.14, ...), kind=kOutput, calls=%fused_computation.18 | convolution fusion | flops 474939392 | bytes 4390913 | tf_op jit(solution)/shard_map/dot_general | solution.py:249
  78.2 1.8 %fusion.2 = f32[512,448]{0,1:T(8,128)S(1)} fusion(bf16[448,1024]{1,0:T(8,128)(2,1)S(1)} %collective-permute-done.22, bf16[512,1024]{1,0:T(8,128)(2,1)S(1)} %constant_dynamic-update-slice_fusion, pred[]{:T(512)S(6)} %eq.46, bf16[128,1024]{1,0:T(8,128)(2,1)} %collective-permute-done.14, bf16[128,1024]{1,0:T(8,128)(2,1)} %collective-permute-done.13, ...), kind=kOutput, calls=%fused_computation.26 | convolution fusion | flops 474480640 | bytes 3932161 | tf_op jit(solution)/shard_map/dot_general | solution.py:251
  80.0 1.8 %broadcast_select_fusion.2 = (bf16[512,448]{0,1:T(8,128)(2,1)S(1)}, bf16[512,448]{0,1:T(8,128)(2,1)S(1)}) fusion(bf16[512,448]{0,1:T(8,128)(2,1)S(1)} %fusion, pred[]{:T(512)S(6)} %eq.45, f32[512,448]{0,1:T(8,128)S(1)} %fusion.2, bf16[448,1024]{1,0:T(8,128)(2,1)S(1)} %collective-permute-done.21, ...), kind=kOutput, calls=%fused_computation.24 | convolution fusion | flops 475398144 | bytes 5308418 | tf_op jit(solution)/shard_map/dot_general | solution.py:249
  82.3 2.0 %collective-permute-start.23 = (bf16[64,896]{0,1:T(8,128)(2,1)S(1)}, bf16[64,896]{0,1:T(8,128)(2,1)S(1)}, u32[]{:S(2)}, u32[]{:S(2)}) collective-permute-start(bf16[64,896]{0,1:T(8,128)(2,1)S(1)} %get-tuple-element.9), channel_id=1, source_target_pairs={{0,2},{1,3},{2,4},{3,5},{4,6},{5,7},{6,8},{7,9},{8,10},{9,11},{10,... | collective-permute-start | bytes 344072 | tf_op jit(solution)/shard_map/ppermute | solution.py:37
  84.3 3.3 %collective-permute-start.24 = (bf16[64,896]{0,1:T(8,128)(2,1)S(1)}, bf16[64,896]{0,1:T(8,128)(2,1)S(1)}, u32[]{:S(2)}, u32[]{:S(2)}) collective-permute-start(bf16[64,896]{0,1:T(8,128)(2,1)S(1)} %get-tuple-element.10), channel_id=1, source_target_pairs={{0,4},{1,5},{2,6},{3,7},{4,8},{5,9},{6,10},{7,11},{8,12},{9,13},{1... | collective-permute-start | bytes 344072 | tf_op jit(solution)/shard_map/ppermute | solution.py:37
  87.6 4.1 %collective-permute-start.25 = (bf16[64,896]{0,1:T(8,128)(2,1)S(1)}, bf16[64,896]{0,1:T(8,128)(2,1)S(1)}, u32[]{:S(2)}, u32[]{:S(2)}) collective-permute-start(bf16[64,896]{0,1:T(8,128)(2,1)S(1)} %get-tuple-element.11), channel_id=1, source_target_pairs={{0,6},{1,7},{2,8},{3,9},{4,10},{5,11},{6,12},{7,13},{8,14},{9,15},... | collective-permute-start | bytes 344072 | tf_op jit(solution)/shard_map/ppermute | solution.py:37
  92.2 4.9 %collective-permute-start.27 = (bf16[64,896]{0,1:T(8,128)(2,1)S(1)}, bf16[64,896]{0,1:T(8,128)(2,1)S(1)}, u32[]{:S(2)}, u32[]{:S(2)}) collective-permute-start(bf16[64,896]{0,1:T(8,128)(2,1)S(1)} %get-tuple-element.13), channel_id=1, source_target_pairs={{0,10},{1,11},{2,12},{3,13},{4,14},{5,15},{6,0},{7,1},{8,2},{9,3},... | collective-permute-start | bytes 344072 | tf_op jit(solution)/shard_map/ppermute | solution.py:37
  97.1 0.8 fusion.4
  97.9 4.2 %collective-permute-start.28 = (bf16[64,896]{0,1:T(8,128)(2,1)S(1)}, bf16[64,896]{0,1:T(8,128)(2,1)S(1)}, u32[]{:S(2)}, u32[]{:S(2)}) collective-permute-start(bf16[64,896]{0,1:T(8,128)(2,1)S(1)} %get-tuple-element.14), channel_id=1, source_target_pairs={{0,12},{1,13},{2,14},{3,15},{4,0},{5,1},{6,2},{7,3},{8,4},{9,5},{1... | collective-permute-start | bytes 344072 | tf_op jit(solution)/shard_map/ppermute | solution.py:37
  102.1 5.1 %collective-permute-done.24 = bf16[64,896]{0,1:T(8,128)(2,1)S(1)} collective-permute-done((bf16[64,896]{0,1:T(8,128)(2,1)S(1)}, bf16[64,896]{0,1:T(8,128)(2,1)S(1)}, u32[]{:S(2)}, u32[]{:S(2)}) %collective-permute-start.24) | collective-permute-done | bytes 114720 | tf_op jit(solution)/shard_map/ppermute | solution.py:37
  107.2 2.7 %collective-permute-start.29 = (bf16[64,896]{0,1:T(8,128)(2,1)}, bf16[64,896]{0,1:T(8,128)(2,1)S(1)}, u32[]{:S(2)}, u32[]{:S(2)}) collective-permute-start(bf16[64,896]{0,1:T(8,128)(2,1)} %fusion.4), channel_id=1, source_target_pairs={{0,14},{1,15},{2,0},{3,1},{4,2},{5,3},{6,4},{7,5},{8,6},{9,7},{10,... | collective-permute-start | bytes 344072 | tf_op jit(solution)/shard_map/ppermute | solution.py:37
  109.9 13.8 %collective-permute-done.25 = bf16[64,896]{0,1:T(8,128)(2,1)S(1)} collective-permute-done((bf16[64,896]{0,1:T(8,128)(2,1)S(1)}, bf16[64,896]{0,1:T(8,128)(2,1)S(1)}, u32[]{:S(2)}, u32[]{:S(2)}) %collective-permute-start.25) | collective-permute-done | bytes 114720 | tf_op jit(solution)/shard_map/ppermute | solution.py:37
  123.7 6.8 %collective-permute-done.28 = bf16[64,896]{0,1:T(8,128)(2,1)S(1)} collective-permute-done((bf16[64,896]{0,1:T(8,128)(2,1)S(1)}, bf16[64,896]{0,1:T(8,128)(2,1)S(1)}, u32[]{:S(2)}, u32[]{:S(2)}) %collective-permute-start.28) | collective-permute-done | bytes 114720 | tf_op jit(solution)/shard_map/ppermute | solution.py:37
  130.6 2.6 %collective-permute-done.29 = bf16[64,896]{0,1:T(8,128)(2,1)S(1)} collective-permute-done((bf16[64,896]{0,1:T(8,128)(2,1)}, bf16[64,896]{0,1:T(8,128)(2,1)S(1)}, u32[]{:S(2)}, u32[]{:S(2)}) %collective-permute-start.29) | collective-permute-done | bytes 114720 | tf_op jit(solution)/shard_map/ppermute | solution.py:37
  133.5 2.8 %collective-permute-start.30 = (bf16[64,448]{0,1:T(8,128)(2,1)S(1)}, bf16[64,448]{0,1:T(8,128)(2,1)S(1)}, u32[]{:S(2)}, u32[]{:S(2)}) collective-permute-start(bf16[64,448]{0,1:T(8,128)(2,1)S(1)} %get-tuple-element.17), channel_id=1, source_target_pairs={{0,0},{1,1},{2,2},{3,3},{4,64},{5,65},{6,66},{7,67},{8,128},{9,129... | collective-permute-start | bytes 172040 | tf_op jit(solution)/shard_map/ppermute | solution.py:37
  136.3 7.6 %collective-permute-start.31 = (bf16[64,448]{0,1:T(8,128)(2,1)S(1)}, bf16[64,448]{0,1:T(8,128)(2,1)S(1)}, u32[]{:S(2)}, u32[]{:S(2)}) collective-permute-start(bf16[64,448]{0,1:T(8,128)(2,1)S(1)} %get-tuple-element.18), channel_id=1, source_target_pairs={{0,2},{1,3},{2,0},{3,1},{4,66},{5,67},{6,64},{7,65},{8,130},{9,131... | collective-permute-start | bytes 172040 | tf_op jit(solution)/shard_map/ppermute | solution.py:37
  144.4 12.3 %collective-permute-done.31 = bf16[64,448]{0,1:T(8,128)(2,1)S(1)} collective-permute-done((bf16[64,448]{0,1:T(8,128)(2,1)S(1)}, bf16[64,448]{0,1:T(8,128)(2,1)S(1)}, u32[]{:S(2)}, u32[]{:S(2)}) %collective-permute-start.31) | collective-permute-done | bytes 57376 | tf_op jit(solution)/shard_map/ppermute | solution.py:37
  156.7 0.8 maximum_select_fusion
  (57 shorter events, 5.5 us)
Async XLA Ops:
  0.0 26.1 %copy-start = (bf16[8,512,128]{2,1,0:T(8,128)(2,1)S(1)}, bf16[8,512,128]{2,1,0:T(8,128)(2,1)}, u32[]{:S(2)}) copy-start(bf16[8,512,128]{2,1,0:T(8,128)(2,1)} %w_uv_ref.1) | copy-start | bytes 3145732
  0.0 11.9 %collective-permute-start.9 = (bf16[576,128]{1,0:T(8,128)(2,1)}, bf16[576,128]{1,0:T(8,128)(2,1)S(1)}, u32[]{:S(2)}, u32[]{:S(2)}) collective-permute-start(bf16[576,128]{1,0:T(8,128)(2,1)} %bitcast.15), channel_id=1, source_target_pairs={{0,161},{1,160},{2,163},{3,162},{4,165},{5,164},{6,167},{7,166},{8... | collective-permute-start | bytes 442376 | tf_op jit(solution)/shard_map/ppermute | solution.py:37
  1.4 10.5 %collective-permute-start.1 = (bf16[576,128]{1,0:T(8,128)(2,1)}, bf16[576,128]{1,0:T(8,128)(2,1)S(1)}, u32[]{:S(2)}, u32[]{:S(2)}) collective-permute-start(bf16[576,128]{1,0:T(8,128)(2,1)} %bitcast.16), channel_id=1, source_target_pairs={{0,33},{1,32},{2,35},{3,34},{4,37},{5,36},{6,39},{7,38},{8,41},{9,... | collective-permute-start | bytes 442376 | tf_op jit(solution)/shard_map/ppermute | solution.py:37
  4.3 9.0 %collective-permute-start.3 = (bf16[576,128]{1,0:T(8,128)(2,1)}, bf16[576,128]{1,0:T(8,128)(2,1)S(1)}, u32[]{:S(2)}, u32[]{:S(2)}) collective-permute-start(bf16[576,128]{1,0:T(8,128)(2,1)} %bitcast.17), channel_id=1, source_target_pairs={{0,64},{1,65},{2,66},{3,67},{4,68},{5,69},{6,70},{7,71},{8,72},{9,... | collective-permute-start | bytes 442376 | tf_op jit(solution)/shard_map/ppermute | solution.py:37
  5.6 9.5 %collective-permute-start.5 = (bf16[576,128]{1,0:T(8,128)(2,1)}, bf16[576,128]{1,0:T(8,128)(2,1)S(1)}, u32[]{:S(2)}, u32[]{:S(2)}) collective-permute-start(bf16[576,128]{1,0:T(8,128)(2,1)} %bitcast.18), channel_id=1, source_target_pairs={{0,97},{1,96},{2,99},{3,98},{4,101},{5,100},{6,103},{7,102},{8,105... | collective-permute-start | bytes 442376 | tf_op jit(solution)/shard_map/ppermute | solution.py:37
  6.9 10.1 %collective-permute-start.7 = (bf16[576,128]{1,0:T(8,128)(2,1)}, bf16[576,128]{1,0:T(8,128)(2,1)S(1)}, u32[]{:S(2)}, u32[]{:S(2)}) collective-permute-start(bf16[576,128]{1,0:T(8,128)(2,1)} %bitcast.19), channel_id=1, source_target_pairs={{0,128},{1,129},{2,130},{3,131},{4,132},{5,133},{6,134},{7,135},{8... | collective-permute-start | bytes 442376 | tf_op jit(solution)/shard_map/ppermute | solution.py:37
  11.9 5.0 %collective-permute-start = (bf16[576,128]{1,0:T(8,128)(2,1)}, bf16[576,128]{1,0:T(8,128)(2,1)S(1)}, u32[]{:S(2)}, u32[]{:S(2)}) collective-permute-start(bf16[576,128]{1,0:T(8,128)(2,1)} %bitcast.20), channel_id=1, source_target_pairs={{0,16},{1,17},{2,18},{3,19},{4,20},{5,21},{6,22},{7,23},{8,24},{9,... | collective-permute-start | bytes 442376 | tf_op jit(solution)/shard_map/ppermute | solution.py:37
  11.9 10.0 %collective-permute-start.11 = (bf16[576,128]{1,0:T(8,128)(2,1)}, bf16[576,128]{1,0:T(8,128)(2,1)S(1)}, u32[]{:S(2)}, u32[]{:S(2)}) collective-permute-start(bf16[576,128]{1,0:T(8,128)(2,1)} %bitcast.21), channel_id=1, source_target_pairs={{48,193},{49,192},{50,195},{51,194},{52,197},{53,196},{54,199},{55... | collective-permute-start | bytes 442376 | tf_op jit(solution)/shard_map/ppermute | solution.py:37
  13.2 8.7 %collective-permute-start.10 = (bf16[576,128]{1,0:T(8,128)(2,1)S(1)}, bf16[576,128]{1,0:T(8,128)(2,1)S(1)}, u32[]{:S(2)}, u32[]{:S(2)}) collective-permute-start(bf16[576,128]{1,0:T(8,128)(2,1)S(1)} %collective-permute-done.9.rest_10_), channel_id=1, source_target_pairs={{0,16},{1,17},{2,18},{3,19},{4,20},{5,21},{6,22},{7,23},{8,24},{9,... | collective-permute-start | bytes 442376 | tf_op jit(solution)/shard_map/ppermute | solution.py:37
  15.1 45.5 %collective-permute-start.20 = (bf16[448,1024]{1,0:T(8,128)(2,1)}, bf16[448,1024]{1,0:T(8,128)(2,1)}, u32[]{:S(2)}, u32[]{:S(2)}) collective-permute-start(bf16[448,1024]{1,0:T(8,128)(2,1)} %bitcast.10), channel_id=1, source_target_pairs={{0,32},{1,0},{2,34},{3,2},{4,36},{5,4},{6,38},{7,6},{8,40},{9,8},{... | collective-permute-start | bytes 2752520 | tf_op jit(solution)/shard_map/ppermute | solution.py:37
  16.9 9.2 %copy-start.4 = (bf16[576,128]{1,0:T(8,128)(2,1)}, bf16[576,128]{1,0:T(8,128)(2,1)S(1)}, u32[]{:S(2)}) copy-start(bf16[576,128]{1,0:T(8,128)(2,1)S(1)} %collective-permute-done.7.rest_8_) | copy-start | bytes 442372
  17.0 9.1 %collective-permute-start.2 = (bf16[576,128]{1,0:T(8,128)(2,1)S(1)}, bf16[576,128]{1,0:T(8,128)(2,1)}, u32[]{:S(2)}, u32[]{:S(2)}) collective-permute-start(bf16[576,128]{1,0:T(8,128)(2,1)S(1)} %collective-permute-done.1.rest_2_), channel_id=1, source_target_pairs={{0,16},{1,17},{2,18},{3,19},{4,20},{5,21},{6,22},{7,23},{8,24},{9,... | collective-permute-start | bytes 442376 | tf_op jit(solution)/shard_map/ppermute | solution.py:37
  17.0 0.7 copy-start.6
  17.6 8.4 %collective-permute-start.4 = (bf16[576,128]{1,0:T(8,128)(2,1)S(1)}, bf16[576,128]{1,0:T(8,128)(2,1)}, u32[]{:S(2)}, u32[]{:S(2)}) collective-permute-start(bf16[576,128]{1,0:T(8,128)(2,1)S(1)} %collective-permute-done.3.rest_4_), channel_id=1, source_target_pairs={{0,16},{1,17},{2,18},{3,19},{4,20},{5,21},{6,22},{7,23},{8,24},{9,... | collective-permute-start | bytes 442376 | tf_op jit(solution)/shard_map/ppermute | solution.py:37
  21.9 4.2 %collective-permute-start.6 = (bf16[576,128]{1,0:T(8,128)(2,1)S(1)}, bf16[576,128]{1,0:T(8,128)(2,1)}, u32[]{:S(2)}, u32[]{:S(2)}) collective-permute-start(bf16[576,128]{1,0:T(8,128)(2,1)S(1)} %collective-permute-done.5.rest_6_), channel_id=1, source_target_pairs={{0,16},{1,17},{2,18},{3,19},{4,20},{5,21},{6,22},{7,23},{8,24},{9,... | collective-permute-start | bytes 442376 | tf_op jit(solution)/shard_map/ppermute | solution.py:37
  21.9 0.6 copy-start.8
  22.6 3.5 %collective-permute-start.8 = (bf16[576,128]{1,0:T(8,128)(2,1)S(1)}, bf16[576,128]{1,0:T(8,128)(2,1)}, u32[]{:S(2)}, u32[]{:S(2)}) collective-permute-start(bf16[576,128]{1,0:T(8,128)(2,1)S(1)} %collective-permute-done.7.rest_8_), channel_id=1, source_target_pairs={{0,16},{1,17},{2,18},{3,19},{4,20},{5,21},{6,22},{7,23},{8,24},{9,... | collective-permute-start | bytes 442376 | tf_op jit(solution)/shard_map/ppermute | solution.py:37
  23.1 1.2 copy-start.1
  24.3 1.0 copy-start.2
  25.3 0.7 copy-start.10
  25.3 0.9 copy-start.3
  26.2 0.9 copy-start.5
  27.1 0.9 copy-start.7
  28.1 0.9 copy-start.9
  39.3 9.3 %collective-permute-start.15 = (bf16[128,1024]{1,0:T(8,128)(2,1)S(1)}, bf16[128,1024]{1,0:T(8,128)(2,1)S(1)}, u32[]{:S(2)}, u32[]{:S(2)}) collective-permute-start(bf16[128,1024]{1,0:T(8,128)(2,1)S(1)} %attend.1), channel_id=1, source_target_pairs={{0,1},{1,0},{2,3},{3,2},{4,5},{5,4},{6,7},{7,6},{8,9},{9,8},{10,11... | collective-permute-start | bytes 786440 | tf_op jit(solution)/shard_map/ppermute | solution.py:37
  39.4 32.3 %collective-permute-start.19 = (bf16[448,1024]{1,0:T(8,128)(2,1)}, bf16[448,1024]{1,0:T(8,128)(2,1)S(1)}, u32[]{:S(2)}, u32[]{:S(2)}) collective-permute-start(bf16[448,1024]{1,0:T(8,128)(2,1)} %bitcast.10), channel_id=1, source_target_pairs={{0,0},{1,32},{2,2},{3,34},{4,4},{5,36},{6,6},{7,38},{8,8},{9,40},{... | collective-permute-start | bytes 2752520 | tf_op jit(solution)/shard_map/ppermute | solution.py:37
  41.3 7.9 %collective-permute-start.12 = (bf16[128,1024]{1,0:T(8,128)(2,1)S(1)}, bf16[128,1024]{1,0:T(8,128)(2,1)}, u32[]{:S(2)}, u32[]{:S(2)}) collective-permute-start(bf16[128,1024]{1,0:T(8,128)(2,1)S(1)} %attend.1), channel_id=1, source_target_pairs={{0,64},{1,65},{2,66},{3,67},{4,68},{5,69},{6,70},{7,71},{8,72},{9,... | collective-permute-start | bytes 786440 | tf_op jit(solution)/shard_map/ppermute | solution.py:37
  41.3 11.8 %collective-permute-start.13 = (bf16[128,1024]{1,0:T(8,128)(2,1)S(1)}, bf16[128,1024]{1,0:T(8,128)(2,1)}, u32[]{:S(2)}, u32[]{:S(2)}) collective-permute-start(bf16[128,1024]{1,0:T(8,128)(2,1)S(1)} %attend.1), channel_id=1, source_target_pairs={{0,128},{1,129},{2,130},{3,131},{4,132},{5,133},{6,134},{7,135},{8... | collective-permute-start | bytes 786440 | tf_op jit(solution)/shard_map/ppermute | solution.py:37
  48.6 9.2 %collective-permute-start.14 = (bf16[128,1024]{1,0:T(8,128)(2,1)S(1)}, bf16[128,1024]{1,0:T(8,128)(2,1)}, u32[]{:S(2)}, u32[]{:S(2)}) collective-permute-start(bf16[128,1024]{1,0:T(8,128)(2,1)S(1)} %attend.1), channel_id=1, source_target_pairs={{0,192},{1,193},{2,194},{3,195},{4,196},{5,197},{6,198},{7,199},{8... | collective-permute-start | bytes 786440 | tf_op jit(solution)/shard_map/ppermute | solution.py:37
  49.2 11.3 %collective-permute-start.16 = (bf16[128,1024]{1,0:T(8,128)(2,1)}, bf16[128,1024]{1,0:T(8,128)(2,1)S(1)}, u32[]{:S(2)}, u32[]{:S(2)}) collective-permute-start(bf16[128,1024]{1,0:T(8,128)(2,1)} %collective-permute-done.12), channel_id=1, source_target_pairs={{0,1},{1,0},{2,3},{3,2},{4,5},{5,4},{6,7},{7,6},{8,9},{9,8},{10,11... | collective-permute-start | bytes 786440 | tf_op jit(solution)/shard_map/ppermute | solution.py:37
  53.1 13.0 %collective-permute-start.17 = (bf16[128,1024]{1,0:T(8,128)(2,1)}, bf16[128,1024]{1,0:T(8,128)(2,1)S(1)}, u32[]{:S(2)}, u32[]{:S(2)}) collective-permute-start(bf16[128,1024]{1,0:T(8,128)(2,1)} %collective-permute-done.13), channel_id=1, source_target_pairs={{0,1},{1,0},{2,3},{3,2},{4,5},{5,4},{6,7},{7,6},{8,9},{9,8},{10,11... | collective-permute-start | bytes 786440 | tf_op jit(solution)/shard_map/ppermute | solution.py:37
  57.8 14.0 %collective-permute-start.18 = (bf16[128,1024]{1,0:T(8,128)(2,1)}, bf16[128,1024]{1,0:T(8,128)(2,1)S(1)}, u32[]{:S(2)}, u32[]{:S(2)}) collective-permute-start(bf16[128,1024]{1,0:T(8,128)(2,1)} %collective-permute-done.14), channel_id=1, source_target_pairs={{0,1},{1,0},{2,3},{3,2},{4,5},{5,4},{6,7},{7,6},{8,9},{9,8},{10,11... | collective-permute-start | bytes 786440 | tf_op jit(solution)/shard_map/ppermute | solution.py:37
  60.5 17.6 %collective-permute-start.22 = (bf16[448,1024]{1,0:T(8,128)(2,1)}, bf16[448,1024]{1,0:T(8,128)(2,1)S(1)}, u32[]{:S(2)}, u32[]{:S(2)}) collective-permute-start(bf16[448,1024]{1,0:T(8,128)(2,1)} %collective-permute-done.20), channel_id=1, source_target_pairs={{0,16},{1,17},{2,18},{3,19},{4,20},{5,21},{6,22},{7,23},{8,24},{9,... | collective-permute-start | bytes 2752520 | tf_op jit(solution)/shard_map/ppermute | solution.py:37
  71.8 8.2 %collective-permute-start.21 = (bf16[448,1024]{1,0:T(8,128)(2,1)S(1)}, bf16[448,1024]{1,0:T(8,128)(2,1)S(1)}, u32[]{:S(2)}, u32[]{:S(2)}) collective-permute-start(bf16[448,1024]{1,0:T(8,128)(2,1)S(1)} %collective-permute-done.19), channel_id=1, source_target_pairs={{0,16},{1,17},{2,18},{3,19},{4,20},{5,21},{6,22},{7,23},{8,24},{9,... | collective-permute-start | bytes 2752520 | tf_op jit(solution)/shard_map/ppermute | solution.py:37
  82.3 15.6 %collective-permute-start.23 = (bf16[64,896]{0,1:T(8,128)(2,1)S(1)}, bf16[64,896]{0,1:T(8,128)(2,1)S(1)}, u32[]{:S(2)}, u32[]{:S(2)}) collective-permute-start(bf16[64,896]{0,1:T(8,128)(2,1)S(1)} %get-tuple-element.9), channel_id=1, source_target_pairs={{0,2},{1,3},{2,4},{3,5},{4,6},{5,7},{6,8},{7,9},{8,10},{9,11},{10,... | collective-permute-start | bytes 344072 | tf_op jit(solution)/shard_map/ppermute | solution.py:37
  84.3 22.9 %collective-permute-start.24 = (bf16[64,896]{0,1:T(8,128)(2,1)S(1)}, bf16[64,896]{0,1:T(8,128)(2,1)S(1)}, u32[]{:S(2)}, u32[]{:S(2)}) collective-permute-start(bf16[64,896]{0,1:T(8,128)(2,1)S(1)} %get-tuple-element.10), channel_id=1, source_target_pairs={{0,4},{1,5},{2,6},{3,7},{4,8},{5,9},{6,10},{7,11},{8,12},{9,13},{1... | collective-permute-start | bytes 344072 | tf_op jit(solution)/shard_map/ppermute | solution.py:37
  87.6 36.2 %collective-permute-start.25 = (bf16[64,896]{0,1:T(8,128)(2,1)S(1)}, bf16[64,896]{0,1:T(8,128)(2,1)S(1)}, u32[]{:S(2)}, u32[]{:S(2)}) collective-permute-start(bf16[64,896]{0,1:T(8,128)(2,1)S(1)} %get-tuple-element.11), channel_id=1, source_target_pairs={{0,6},{1,7},{2,8},{3,9},{4,10},{5,11},{6,12},{7,13},{8,14},{9,15},... | collective-permute-start | bytes 344072 | tf_op jit(solution)/shard_map/ppermute | solution.py:37
  91.6 32.1 %collective-permute-start.26 = (bf16[64,896]{0,1:T(8,128)(2,1)S(1)}, bf16[64,896]{0,1:T(8,128)(2,1)S(1)}, u32[]{:S(2)}, u32[]{:S(2)}) collective-permute-start(bf16[64,896]{0,1:T(8,128)(2,1)S(1)} %get-tuple-element.12), channel_id=1, source_target_pairs={{0,8},{1,9},{2,10},{3,11},{4,12},{5,13},{6,14},{7,15},{8,0},{9,1},... | collective-permute-start | bytes 344072 | tf_op jit(solution)/shard_map/ppermute | solution.py:37
  92.2 31.6 %collective-permute-start.27 = (bf16[64,896]{0,1:T(8,128)(2,1)S(1)}, bf16[64,896]{0,1:T(8,128)(2,1)S(1)}, u32[]{:S(2)}, u32[]{:S(2)}) collective-permute-start(bf16[64,896]{0,1:T(8,128)(2,1)S(1)} %get-tuple-element.13), channel_id=1, source_target_pairs={{0,10},{1,11},{2,12},{3,13},{4,14},{5,15},{6,0},{7,1},{8,2},{9,3},... | collective-permute-start | bytes 344072 | tf_op jit(solution)/shard_map/ppermute | solution.py:37
  97.9 32.6 %collective-permute-start.28 = (bf16[64,896]{0,1:T(8,128)(2,1)S(1)}, bf16[64,896]{0,1:T(8,128)(2,1)S(1)}, u32[]{:S(2)}, u32[]{:S(2)}) collective-permute-start(bf16[64,896]{0,1:T(8,128)(2,1)S(1)} %get-tuple-element.14), channel_id=1, source_target_pairs={{0,12},{1,13},{2,14},{3,15},{4,0},{5,1},{6,2},{7,3},{8,4},{9,5},{1... | collective-permute-start | bytes 344072 | tf_op jit(solution)/shard_map/ppermute | solution.py:37
  107.2 26.0 %collective-permute-start.29 = (bf16[64,896]{0,1:T(8,128)(2,1)}, bf16[64,896]{0,1:T(8,128)(2,1)S(1)}, u32[]{:S(2)}, u32[]{:S(2)}) collective-permute-start(bf16[64,896]{0,1:T(8,128)(2,1)} %fusion.4), channel_id=1, source_target_pairs={{0,14},{1,15},{2,0},{3,1},{4,2},{5,3},{6,4},{7,5},{8,6},{9,7},{10,... | collective-permute-start | bytes 344072 | tf_op jit(solution)/shard_map/ppermute | solution.py:37
  133.5 10.9 %collective-permute-start.30 = (bf16[64,448]{0,1:T(8,128)(2,1)S(1)}, bf16[64,448]{0,1:T(8,128)(2,1)S(1)}, u32[]{:S(2)}, u32[]{:S(2)}) collective-permute-start(bf16[64,448]{0,1:T(8,128)(2,1)S(1)} %get-tuple-element.17), channel_id=1, source_target_pairs={{0,0},{1,1},{2,2},{3,3},{4,64},{5,65},{6,66},{7,67},{8,128},{9,129... | collective-permute-start | bytes 172040 | tf_op jit(solution)/shard_map/ppermute | solution.py:37
  136.3 20.4 %collective-permute-start.31 = (bf16[64,448]{0,1:T(8,128)(2,1)S(1)}, bf16[64,448]{0,1:T(8,128)(2,1)S(1)}, u32[]{:S(2)}, u32[]{:S(2)}) collective-permute-start(bf16[64,448]{0,1:T(8,128)(2,1)S(1)} %get-tuple-element.18), channel_id=1, source_target_pairs={{0,2},{1,3},{2,0},{3,1},{4,66},{5,67},{6,64},{7,65},{8,130},{9,131... | collective-permute-start | bytes 172040 | tf_op jit(solution)/shard_map/ppermute | solution.py:37

commit v2 on v1

v2 whole, which is shorter than its diff:
```python
import math

import jax
import jax.numpy as jnp
from jax import lax
from jax.experimental import pallas as pl
from jax.experimental.pallas import tpu as pltpu
from jax.sharding import PartitionSpec as P

AXES = ("ctx", "head")
VMEM = pltpu.MemorySpace.VMEM
SMEM = pltpu.MemorySpace.SMEM
NEVER = -1e30


def index_of(y, xh, core, z, xl):
    return ((y * 2 + xh) * 2 + core) * 16 + z * 2 + xl


PLACES = [
    (y, xh, core, z, xl)
    for y in range(4)
    for xh in range(2)
    for core in range(2)
    for z in range(8)
    for xl in range(2)
]


def send(value, target):
    pairs = []
    for place in PLACES:
        goal = target(*place)
        if goal is not None:
            pairs.append((index_of(*place), index_of(*goal)))
    return lax.ppermute(value, AXES, pairs)


def other_core(y, xh, core, z, xl):
    return (y, xh, 1 - core, z, xl)


def other_lo(y, xh, core, z, xl):
    return (y, xh, core, z, 1 - xl)


def after(value, earlier):
    return lax.optimization_barrier((value, earlier))[0]


def absorb_kernel(q_ref, w_uk_ref, qc_ref, qr_ref):
    heads, rows = w_uk_ref.shape[0], q_ref.shape[0]
    for h in range(heads):
        nope = q_ref[:, h * 192 : h * 192 + 128]
        qc_ref[h * rows : (h + 1) * rows, :] = lax.dot_general(
            nope, w_uk_ref[h], (((1,), (1,)), ((), ())), preferred_element_type=jnp.float32
        ).astype(jnp.bfloat16)
        qr_ref[h * rows : (h + 1) * rows, :] = q_ref[:, h * 192 + 128 : (h + 1) * 192]


def place_here():
    ctx, head = lax.axis_index("ctx"), lax.axis_index("head")
    return ctx // 4, lax.rem(ctx // 2, 2), lax.rem(ctx, 2), head // 2, lax.rem(head, 2)


def attend_kernel(lengths_ref, qc_ref, qr_ref, w_uv_any, *rest):
    blocks = rest[:13]
    out_ref, kv_ref, scores_ref, accum_ref, highest_ref, total_ref, w_uv_ref, sems = rest[13:]
    y, xh, core, _, _ = place_here()
    rows, latent = qc_ref.shape
    heads = w_uv_ref.shape[0]
    tokens = rows // heads
    units = kv_ref.shape[0]
    query_base = lax.axis_index("ctx") * tokens
    for u in range(units):
        for half in range(2):
            pltpu.make_async_copy(
                blocks[min(2 * u + half, 12)],
                kv_ref.at[u, :, pl.ds(half * 128, 128)],
                sems.at[2 * u + half],
            ).start()
    w_uv_copy = pltpu.make_async_copy(w_uv_any, w_uv_ref, sems.at[2 * units])
    w_uv_copy.start()
    query_pos = query_base + lax.broadcasted_iota(jnp.int32, (tokens, 1), 0)
    start = jnp.zeros((tokens, 1), jnp.int32)
    first = jnp.int32(0)
    end = jnp.int32(0)
    for k in range(8):
        end = end + lengths_ref[k]
        start = jnp.where(query_pos >= end, end, start)
        first = jnp.where(query_base >= end, end, first)
    lane = lax.broadcasted_iota(jnp.int32, (1, 256), 1)
    scale = 1.0 / math.sqrt(192.0) * math.log2(math.e)

    def base_of(u):
        source = y - u // 2
        source_xh = jnp.where(lax.rem(u, 2) == 0, xh, 1 - xh)
        base = jnp.where(source < 0, 1 << 20, source * 512 + source_xh * 256)
        last = jnp.where((y == 3) & (xh == 0) & (core == 0), 256, 1 << 20)
        return jnp.where(u == units - 1, last, base)

    def seen(u):
        base = base_of(u)
        return (base <= query_base + tokens - 1) & (base + 256 > first)

    def look(u, fresh):
        base, flip = base_of(u), jnp.where(u == units - 1, 0, core)
        key_pos = base + jnp.where(flip > 0, lax.rem(lane + 128, 256), lane)
        visible = (key_pos <= query_pos) & (key_pos >= start)
        s = jnp.dot(qc_ref[...], kv_ref[u, :latent, :], preferred_element_type=jnp.float32)
        s = s + jnp.dot(qr_ref[...], kv_ref[u, latent:, :], preferred_element_type=jnp.float32)
        s = jnp.where(visible[None], s.reshape(heads, tokens, 256), NEVER)
        scores_ref[u] = s.reshape(rows, 256)
        top = jnp.maximum(s[:, :, :128], s[:, :, 128:]).reshape(rows, 128)
        highest_ref[...] = top if fresh else jnp.maximum(highest_ref[...], top)

    def wait(u):
        for half in range(2):
            pltpu.make_async_copy(
                blocks[0], kv_ref.at[u, :, pl.ds(half * 128, 128)], sems.at[2 * u + half]
            ).wait()

    wait(0)
    look(0, True)

    @pl.loop(1, units)
    def _(u):
        wait(u)

        @pl.when(seen(u))
        def _():
            look(u, False)

    highest_ref[:, :1] = jnp.max(highest_ref[...], axis=1, keepdims=True) * scale

    def gather(u, fresh):
        p = jnp.exp2(scores_ref[u] * scale - highest_ref[:, :1])
        product = lax.dot_general(
            p.astype(jnp.bfloat16),
            kv_ref[u, :latent, :],
            (((1,), (1,)), ((), ())),
            preferred_element_type=jnp.float32,
        )
        both = p[:, :128] + p[:, 128:]
        accum_ref[...] = product if fresh else accum_ref[...] + product
        total_ref[...] = both if fresh else total_ref[...] + both

    gather(0, True)

    @pl.loop(1, units)
    def _(u):
        @pl.when(seen(u))
        def _():
            gather(u, False)

    w_uv_copy.wait()
    inverse = 1.0 / jnp.sum(total_ref[...], axis=1, keepdims=True)
    for h in range(heads):
        context = (
            accum_ref[h * tokens : (h + 1) * tokens, :] * inverse[h * tokens : (h + 1) * tokens]
        ).astype(jnp.bfloat16)
        out_ref[:, h * 128 : (h + 1) * 128] = jnp.dot(
            context, w_uv_ref[h], preferred_element_type=jnp.float32
        ).astype(jnp.bfloat16)


def project_kernel(*rest):
    sources = rest[:16]
    own_ref, up_ref, down_ref, far_up_ref, far_down_ref, up2_ref, down2_ref = rest[16:23]
    x_ref, w_ref, sems = rest[23:]
    y, xh, core, z, xl = place_here()
    b, d = z // 2, lax.rem(z, 2)

    def x_copy(number):
        part, g = number // 4, number % 4
        at = pl.multiple_of(lax.rem(y - g - b + 8, 4) * 128, 128)
        return pltpu.make_async_copy(
            sources[number],
            x_ref.at[pl.ds(at, 128), pl.ds(part * 1024, 1024)],
            sems.at[number],
        )

    def w_copy(source, order, part):
        return pltpu.make_async_copy(
            source,
            w_ref.at[order, :, pl.ds(part * 1024, 1024)],
            sems.at[8 + 2 * order + part],
        )

    near_order, far_order = lax.rem(xh + d, 2), lax.rem(1 - xh + d, 2)
    kinds = ((near_order, 0), (near_order, 1), (far_order, 1), (far_order, 0))
    for turn in range(2):

        @pl.when(lax.rem(core + xl, 2) == turn)
        def fetch(turn=turn):
            for kind, (order, part) in enumerate(kinds):
                w_copy(sources[8 + 4 * turn + kind], order, part).start()

    for number in range(8):
        x_copy(number).start()
    for number in range(8):
        x_copy(number).wait()
    pieces = []
    for order in range(2):
        for part in range(2):
            w_copy(sources[8], order, part).wait()
        sums = lax.dot_general(
            w_ref[order], x_ref[...], (((1,), (1,)), ((), ())), preferred_element_type=jnp.float32
        ).astype(jnp.bfloat16)
        parts = [sums[:, j * 128 : (j + 1) * 128] for j in range(4)]
        if order == 0:
            own_ref[...], up2_ref[...] = parts[0], parts[1]
            far_up_ref[...], far_down_ref[...] = parts[2][:224], parts[2][224:]
            down2_ref[...] = parts[3]
        else:
            for turn in range(2):

                @pl.when(d == turn)
                def store(turn=turn):
                    for j in range(4):
                        step = (2 * j + 1 - 2 * turn) % 8
                        ref = up_ref if step < 4 else down_ref
                        ref[0 if step in (3, 5) else 1] = parts[j]


def whole(space):
    return pl.BlockSpec(memory_space=space)


def body(queries, kv_latent, w_uk, w_uv, w_out, doc_lengths):
    rows = queries.shape[0]
    heads, latent, nope = w_uk.shape
    width = w_out.shape[1]

    mine = kv_latent.T

    def from_y(step, flip):
        def target(ty, txh, tcore, tz, txl):
            if ty + step > 3:
                return None
            if flip:
                return (ty + step, 1 - txh, tcore, tz, 1 - txl)
            return (ty + step, txh, tcore, tz, txl)

        return target

    def farthest(ty, txh, tcore, tz, txl):
        if (ty, txh, tcore) == (0, 1, 1):
            return (3, 0, 0, tz, 1 - txl)
        return None

    got = [mine, send(mine, from_y(0, True))]
    for step in (1, 2):
        got.extend([send(mine, from_y(step, False)), send(mine, from_y(step, True))])
    far = send(mine, farthest)
    qc, qr = pl.pallas_call(
        absorb_kernel,
        out_shape=(
            jax.ShapeDtypeStruct((heads * rows, latent), jnp.bfloat16),
            jax.ShapeDtypeStruct((heads * rows, 64), jnp.bfloat16),
        ),
        in_specs=[whole(VMEM), whole(VMEM)],
        out_specs=(whole(VMEM), whole(VMEM)),
        compiler_params=pltpu.CompilerParams(vmem_limit_bytes=8 << 20),
        name="absorb",
    )(queries, w_uk)

    blocks = []
    for block in got[:4]:
        blocks.extend([block, send(block, other_core)])
    for block in after(got[4:], (qc, qr)):
        blocks.extend([block, send(block, other_core)])
    blocks.append(far)
    units = len(got) + 1

    def only(test, goal):
        return lambda *at: goal(*at) if test(*at) else None

    def same(ty, h, c, tz, x):
        return c == x

    def differs(ty, h, c, tz, x):
        return c != x

    def around(ty, h, c, tz, x):
        return (ty, 1 - h, 1 - c, tz, x) if c == x else (ty, h, c, tz, 1 - x)

    def across_x(ty, h, c, tz, x):
        return (ty, 1 - h, 1 - c, tz, 1 - x)

    w_own = w_out.T
    w_a = send(w_own, around)
    w_b = send(after(w_own, got), only(differs, across_x))
    w_a_other = send(after(w_a, blocks), other_core)
    w_own_other = send(after(w_own, blocks), only(same, other_core))

    def shifted(step):
        return lambda ty, txh, tcore, tz, txl: ((ty + step) % 4, txh, tcore, tz, txl)

    qc = after(qc, (w_a_other, w_own_other))
    values = pl.pallas_call(
        attend_kernel,
        out_shape=jax.ShapeDtypeStruct((rows, heads * 128), jnp.bfloat16),
        in_specs=[whole(SMEM)] + [whole(VMEM)] * 2 + [whole(pl.ANY)] * 14,
        out_specs=whole(VMEM),
        scratch_shapes=[
            pltpu.VMEM((units, latent + 64, 256), jnp.bfloat16),
            pltpu.VMEM((units, heads * rows, 256), jnp.float32),
            pltpu.VMEM((heads * rows, latent), jnp.float32),
            pltpu.VMEM((heads * rows, 128), jnp.float32),
            pltpu.VMEM((heads * rows, 128), jnp.float32),
            pltpu.VMEM((heads, latent, 128), jnp.bfloat16),
            pltpu.SemaphoreType.DMA((2 * units + 1,)),
        ],
        compiler_params=pltpu.CompilerParams(vmem_limit_bytes=26 << 20),
        name="attend",
    )(doc_lengths, qc, qr, w_uv, *blocks)

    near = [values] + [send(values, shifted(step)) for step in (1, 2, 3)]
    neighbour = send(values, other_lo)
    w_b_other = send(after(w_b, (near, neighbour)), only(differs, other_core))
    w_same = [w_own, w_a, w_b_other, w_a_other]
    w_cross = [w_own_other, w_a_other, w_b, w_a]
    across = [
        neighbour,
        send(neighbour, shifted(1)),
        send(near[2], other_lo),
        send(neighbour, shifted(3)),
    ]

    def result(*shape):
        return jax.ShapeDtypeStruct(shape, jnp.bfloat16)

    own, up, down, far_up, far_down, up2, down2 = pl.pallas_call(
        project_kernel,
        out_shape=[
            result(width, rows),
            result(2, width, rows),
            result(2, width, rows),
            result(width // 2, rows),
            result(width // 2, rows),
            result(width, rows),
            result(width, rows),
        ],
        in_specs=[whole(pl.ANY)] * 16,
        out_specs=[whole(VMEM)] * 7,
        scratch_shapes=[
            pltpu.VMEM((4 * rows, 2048), jnp.bfloat16),
            pltpu.VMEM((2, width, 2048), jnp.bfloat16),
            pltpu.SemaphoreType.DMA((12,)),
        ],
        compiler_params=pltpu.CompilerParams(vmem_limit_bytes=20 << 20),
        name="project",
    )(*near, *across, *w_same, *w_cross)

    def along(step):
        return lambda ty, txh, tcore, tz, txl: (ty, txh, tcore, (tz + step) % 8, txl)

    def wide(value):
        return value.astype(jnp.float32)

    from_far_low = send(far_up, along(2))
    from_far_high = send(far_down, along(6))
    from_low = send(up, along(1))
    from_high = send(down, along(7))
    up_sum = wide(up2) + wide(from_low[0]) + jnp.pad(wide(from_far_low), ((0, width // 2), (0, 0)))
    down_sum = (
        wide(down2) + wide(from_high[0]) + jnp.pad(wide(from_far_high), ((width // 2, 0), (0, 0)))
    )
    total = wide(own) + wide(from_low[1]) + wide(from_high[1])
    total = total + wide(send(up_sum.astype(jnp.bfloat16), along(2)))
    total = total + wide(send(down_sum.astype(jnp.bfloat16), along(6)))
    total = total.astype(jnp.bfloat16)

    def final(ty, txh, tcore, tz, txl):
        return (tz // 2, txh, tcore, 2 * ty + tz % 2, txl)

    return send(total, final).T


def solution(mesh):
    placed = (
        P("ctx", "head"),
        P("ctx", None),
        P("head", None, None),
        P("head", None, None),
        P("head", "ctx"),
        P(),
    )
    return jax.shard_map(
        body, mesh=mesh, in_specs=placed, out_specs=P("ctx", "head"), check_vma=False
    )
```

time: 158 us -> 113 us (0.72)
  the two profiles are of different devices: /device:TPU:24 before, /device:TPU:16 now
where the time goes in v2:
time: 113 us; the launch traced here: 111 us
  starting transfers between devices  52.4 us (46%)
  waiting for transfers between devices  44.7 us (40%)
  Pallas kernels  10.7 us (9%)
  local copies, waits for them, and re-layouts  2.89 us (3%)
    ppermute x31, starting transfers between devices, send(): return lax.ppermute(value, AXES, pairs)  52.4 us
    ppermute x31, waiting for transfers between devices, send(): return lax.ppermute(value, AXES, pairs)  44.7 us
    pallas_call x1, Pallas kernels, body(): pl.pallas_call(attend_kernel, out_shape=jax.ShapeDtypeStruct((rows, heads...  7.36 us
    pallas_call x1, Pallas kernels, body(): pl.pallas_call(project_kernel, out_shape=[result(width, rows), result(2,...  2.95 us
    unnamed x13, local copies, waits for them, and re-layouts  2.89 us
  transfers between devices with their start and end apart: 31, of which 17 were waited for; matrix products, arithmetic and copies ran while one was open for 0% of the time, Pallas kernels for 7%

profile of v2, /device:TPU:16, one launch (start us, length us, event | category | flops | bytes accessed | tf_op | source)
XLA Modules:
  0.0 111.1 jit_solution(8279885378371884240)
XLA Ops:
  0.0 2.5 %collective-permute-start = (bf16[448,1024]{1,0:T(8,128)(2,1)}, bf16[448,1024]{1,0:T(8,128)(2,1)S(1)}, u32[]{:S(2)}, u32[]{:S(2)}) collective-permute-start(bf16[448,1024]{1,0:T(8,128)(2,1)} %bitcast.23), channel_id=1, source_target_pairs={{0,48},{1,0},{2,50},{3,2},{4,52},{5,4},{6,54},{7,6},{8,56},{9,8},{... | collective-permute-start | bytes 2752520 | tf_op jit(solution)/shard_map/ppermute | solution.py:36
  2.5 0.7 collective-permute-start.12
  3.1 1.3 %collective-permute-start.9 = (bf16[576,128]{1,0:T(8,128)(2,1)}, bf16[576,128]{1,0:T(8,128)(2,1)S(1)}, u32[]{:S(2)}, u32[]{:S(2)}) collective-permute-start(bf16[576,128]{1,0:T(8,128)(2,1)} %bitcast.28), channel_id=1, source_target_pairs={{0,161},{1,160},{2,163},{3,162},{4,165},{5,164},{6,167},{7,166},{8... | collective-permute-start | bytes 442376 | tf_op jit(solution)/shard_map/ppermute | solution.py:36
  4.4 1.3 %collective-permute-start.8 = (bf16[576,128]{1,0:T(8,128)(2,1)}, bf16[576,128]{1,0:T(8,128)(2,1)S(1)}, u32[]{:S(2)}, u32[]{:S(2)}) collective-permute-start(bf16[576,128]{1,0:T(8,128)(2,1)} %bitcast.29), channel_id=1, source_target_pairs={{0,128},{1,129},{2,130},{3,131},{4,132},{5,133},{6,134},{7,135},{8... | collective-permute-start | bytes 442376 | tf_op jit(solution)/shard_map/ppermute | solution.py:36
  5.7 3.8 %collective-permute-start.6 = (bf16[576,128]{1,0:T(8,128)(2,1)}, bf16[576,128]{1,0:T(8,128)(2,1)S(1)}, u32[]{:S(2)}, u32[]{:S(2)}) collective-permute-start(bf16[576,128]{1,0:T(8,128)(2,1)} %bitcast.30), channel_id=1, source_target_pairs={{0,97},{1,96},{2,99},{3,98},{4,101},{5,100},{6,103},{7,102},{8,105... | collective-permute-start | bytes 442376 | tf_op jit(solution)/shard_map/ppermute | solution.py:36
  9.5 9.7 %collective-permute-start.4 = (bf16[576,128]{1,0:T(8,128)(2,1)}, bf16[576,128]{1,0:T(8,128)(2,1)S(1)}, u32[]{:S(2)}, u32[]{:S(2)}) collective-permute-start(bf16[576,128]{1,0:T(8,128)(2,1)} %bitcast.31), channel_id=1, source_target_pairs={{0,64},{1,65},{2,66},{3,67},{4,68},{5,69},{6,70},{7,71},{8,72},{9,... | collective-permute-start | bytes 442376 | tf_op jit(solution)/shard_map/ppermute | solution.py:36
  19.2 1.1 collective-permute-start.2
  20.3 1.6 %collective-permute-start.1 = (bf16[576,128]{1,0:T(8,128)(2,1)}, bf16[576,128]{1,0:T(8,128)(2,1)S(1)}, u32[]{:S(2)}, u32[]{:S(2)}) collective-permute-start(bf16[576,128]{1,0:T(8,128)(2,1)} %bitcast.33), channel_id=1, source_target_pairs={{0,16},{1,17},{2,18},{3,19},{4,20},{5,21},{6,22},{7,23},{8,24},{9,... | collective-permute-start | bytes 442376 | tf_op jit(solution)/shard_map/ppermute | solution.py:36
  21.9 2.4 %collective-permute-done.6.rest_6_ = bf16[576,128]{1,0:T(8,128)(2,1)S(1)} collective-permute-done((bf16[576,128]{1,0:T(8,128)(2,1)}, bf16[576,128]{1,0:T(8,128)(2,1)S(1)}, u32[]{:S(2)}, u32[]{:S(2)}) %collective-permute-start.6) | collective-permute-done | bytes 147488 | tf_op jit(solution)/shard_map/ppermute | solution.py:36
  24.3 1.2 %copy-done.1 = bf16[8,512,128]{2,1,0:T(8,128)(2,1)S(1)} copy-done((bf16[8,512,128]{2,1,0:T(8,128)(2,1)S(1)}, bf16[8,512,128]{2,1,0:T(8,128)(2,1)}, u32[]{:S(2)}) %copy-start.1) | copy-done | bytes 1048600
  25.6 1.0 copy-done.3
  26.6 0.4 absorb.1
  27.0 0.6 collective-permute-start.10
  27.6 0.1 collective-permute-start.5
  27.8 0.4 collective-permute-start.3
  28.2 0.1 collective-permute-start.11
  28.3 0.7 collective-permute-done.5.rest_5_
  29.0 0.2 collective-permute-done.3.rest_3_
  29.2 0.3 collective-permute-done.11.rest_11_
  29.5 2.2 %collective-permute-start.14 = (bf16[448,1024]{1,0:T(8,128)(2,1)}, bf16[448,1024]{1,0:T(8,128)(2,1)S(1)}, u32[]{:S(2)}, u32[]{:S(2)}) collective-permute-start(bf16[448,1024]{1,0:T(8,128)(2,1)} %bitcast.24), channel_id=1, source_target_pairs={{0,16},{2,18},{4,20},{6,22},{8,24},{10,26},{12,28},{14,30},{17,1},... | collective-permute-start | bytes 2752520 | tf_op jit(solution)/shard_map/ppermute | solution.py:36
  31.8 0.7 collective-permute-start.22
  32.5 1.4 %collective-permute-done.14.rest_12_ = bf16[448,1024]{1,0:T(8,128)(2,1)S(1)} collective-permute-done((bf16[448,1024]{1,0:T(8,128)(2,1)}, bf16[448,1024]{1,0:T(8,128)(2,1)S(1)}, u32[]{:S(2)}, u32[]{:S(2)}) %collective-permute-start.14) | collective-permute-done | bytes 917536 | tf_op jit(solution)/shard_map/ppermute | solution.py:36
  33.9 1.1 collective-permute-done.13.rest_11_.rest_13_
  35.0 7.4 %attend.1.rest_0_ = bf16[128,1024]{1,0:T(8,128)(2,1)S(1)} custom-call(s32[8]{0:T(128)S(1)} %copy-done.5, bf16[1024,512]{1,0:T(8,128)(2,1)S(1)} %get-tuple-element.27.qc_ref, bf16[1024,64]{1,0:T(8,128)(2,1)S(1)} %get-tuple-element.22.qr_ref, bf16[8,512,128]{2,1,0:T(8,128)(2,1)S(1)} %copy-done, bf16[576,128]{1,0:T(8,128)(2,1)S(1)} %bitcast.34, ...), custom_call_target="tpu_custom_call" | custom-call | tf_op jit(solution)/shard_map/attend/pallas_call | solution.py:301
  42.5 0.1 collective-permute-start.17
  42.7 2.1 %collective-permute-start.15 = (bf16[128,1024]{1,0:T(8,128)(2,1)S(1)}, bf16[128,1024]{1,0:T(8,128)(2,1)S(1)}, u32[]{:S(2)}, u32[]{:S(2)}) collective-permute-start(bf16[128,1024]{1,0:T(8,128)(2,1)S(1)} %attend.1.rest_0_), channel_id=1, source_target_pairs={{0,64},{1,65},{2,66},{3,67},{4,68},{5,69},{6,70},{7,71},{8,72},{9,... | collective-permute-start | bytes 786440 | tf_op jit(solution)/shard_map/ppermute | solution.py:36
  44.8 6.8 %collective-permute-done.18.rest_4_ = bf16[128,1024]{1,0:T(8,128)(2,1)S(1)} collective-permute-done((bf16[128,1024]{1,0:T(8,128)(2,1)S(1)}, bf16[128,1024]{1,0:T(8,128)(2,1)S(1)}, u32[]{:S(2)}, u32[]{:S(2)}) %collective-permute-start.18) | collective-permute-done | bytes 262176 | tf_op jit(solution)/shard_map/ppermute | solution.py:36
  51.7 1.7 %collective-permute-done.16.rest_2_ = bf16[128,1024]{1,0:T(8,128)(2,1)S(1)} collective-permute-done((bf16[128,1024]{1,0:T(8,128)(2,1)S(1)}, bf16[128,1024]{1,0:T(8,128)(2,1)S(1)}, u32[]{:S(2)}, u32[]{:S(2)}) %collective-permute-start.16) | collective-permute-done | bytes 262176 | tf_op jit(solution)/shard_map/ppermute | solution.py:36
  53.5 5.2 %collective-permute-done.15.rest_1_ = bf16[128,1024]{1,0:T(8,128)(2,1)S(1)} collective-permute-done((bf16[128,1024]{1,0:T(8,128)(2,1)S(1)}, bf16[128,1024]{1,0:T(8,128)(2,1)S(1)}, u32[]{:S(2)}, u32[]{:S(2)}) %collective-permute-start.15) | collective-permute-done | bytes 262176 | tf_op jit(solution)/shard_map/ppermute | solution.py:36
  58.6 1.5 %collective-permute-start.23 = (bf16[448,1024]{1,0:T(8,128)(2,1)S(1)}, bf16[448,1024]{1,0:T(8,128)(2,1)S(1)}, u32[]{:S(2)}, u32[]{:S(2)}) collective-permute-start(bf16[448,1024]{1,0:T(8,128)(2,1)S(1)} %collective-permute-done.22.rest_14_), channel_id=1, source_target_pairs={{1,17},{3,19},{5,21},{7,23},{9,25},{11,27},{13,29},{15,31},{16,0},... | collective-permute-start | bytes 2752520 | tf_op jit(solution)/shard_map/ppermute | solution.py:36
  60.1 1.1 collective-permute-start.21
  61.1 1.1 collective-permute-start.19
  62.2 2.1 %collective-permute-start.20 = (bf16[128,1024]{1,0:T(8,128)(2,1)S(1)}, bf16[128,1024]{1,0:T(8,128)(2,1)S(1)}, u32[]{:S(2)}, u32[]{:S(2)}) collective-permute-start(bf16[128,1024]{1,0:T(8,128)(2,1)S(1)} %collective-permute-done.16.rest_2_), channel_id=1, source_target_pairs={{0,1},{1,0},{2,3},{3,2},{4,5},{5,4},{6,7},{7,6},{8,9},{9,8},{10,11... | collective-permute-start | bytes 786440 | tf_op jit(solution)/shard_map/ppermute | solution.py:36
  64.3 4.9 %collective-permute-done.21.rest_7_ = bf16[128,1024]{1,0:T(8,128)(2,1)S(1)} collective-permute-done((bf16[128,1024]{1,0:T(8,128)(2,1)S(1)}, bf16[128,1024]{1,0:T(8,128)(2,1)S(1)}, u32[]{:S(2)}, u32[]{:S(2)}) %collective-permute-start.21) | collective-permute-done | bytes 262176 | tf_op jit(solution)/shard_map/ppermute | solution.py:36
  69.1 1.1 %collective-permute-done.19.rest_5_ = bf16[128,1024]{1,0:T(8,128)(2,1)S(1)} collective-permute-done((bf16[128,1024]{1,0:T(8,128)(2,1)S(1)}, bf16[128,1024]{1,0:T(8,128)(2,1)S(1)}, u32[]{:S(2)}, u32[]{:S(2)}) %collective-permute-start.19) | collective-permute-done | bytes 262176 | tf_op jit(solution)/shard_map/ppermute | solution.py:36
  70.2 0.8 collective-permute-done.20.rest_6_
  71.0 3.0 %project.1 = (bf16[448,128]{1,0:T(8,128)(2,1)S(1)}, bf16[2,448,128]{2,1,0:T(8,128)(2,1)S(1)}, bf16[2,448,128]{2,1,0:T(8,128)(2,1)S(1)}, bf16[224,128]{1,0:T(8,12...) custom-call(bf16[128,1024]{1,0:T(8,128)(2,1)S(1)} %attend.1.rest_0_, ...), custom_call_target="tpu_custom_call" | custom-call | tf_op jit(solution)/shard_map/project/pallas_call | solution.py:334
  74.0 2.0 %collective-permute-start.24 = (bf16[2,448,128]{2,1,0:T(8,128)(2,1)S(1)}, bf16[2,448,128]{2,1,0:T(8,128)(2,1)S(1)}, u32[]{:S(2)}, u32[]{:S(2)}) collective-permute-start(bf16[2,448,128]{2,1,0:T(8,128)(2,1)S(1)} %get-tuple-element.31), channel_id=1, source_target_pairs={{0,2},{1,3},{2,4},{3,5},{4,6},{5,7},{6,8},{7,9},{8,10},{9,11},{10,... | collective-permute-start | bytes 688136 | tf_op jit(solution)/shard_map/ppermute | solution.py:36
  76.0 3.3 %collective-permute-start.26 = (bf16[224,128]{1,0:T(8,128)(2,1)S(1)}, bf16[224,128]{1,0:T(8,128)(2,1)S(1)}, u32[]{:S(2)}, u32[]{:S(2)}) collective-permute-start(bf16[224,128]{1,0:T(8,128)(2,1)S(1)} %get-tuple-element.34), channel_id=1, source_target_pairs={{0,4},{1,5},{2,6},{3,7},{4,8},{5,9},{6,10},{7,11},{8,12},{9,13},{1... | collective-permute-start | bytes 172040 | tf_op jit(solution)/shard_map/ppermute | solution.py:36
  79.2 2.1 %collective-permute-start.28 = (bf16[224,128]{1,0:T(8,128)(2,1)S(1)}, bf16[224,128]{1,0:T(8,128)(2,1)S(1)}, u32[]{:S(2)}, u32[]{:S(2)}) collective-permute-start(bf16[224,128]{1,0:T(8,128)(2,1)S(1)} %get-tuple-element.36), channel_id=1, source_target_pairs={{0,12},{1,13},{2,14},{3,15},{4,0},{5,1},{6,2},{7,3},{8,4},{9,5},{1... | collective-permute-start | bytes 172040 | tf_op jit(solution)/shard_map/ppermute | solution.py:36
  81.4 1.5 %collective-permute-start.25 = (bf16[2,448,128]{2,1,0:T(8,128)(2,1)S(1)}, bf16[2,448,128]{2,1,0:T(8,128)(2,1)S(1)}, u32[]{:S(2)}, u32[]{:S(2)}) collective-permute-start(bf16[2,448,128]{2,1,0:T(8,128)(2,1)S(1)} %get-tuple-element.32), channel_id=1, source_target_pairs={{0,14},{1,15},{2,0},{3,1},{4,2},{5,3},{6,4},{7,5},{8,6},{9,7},{10,... | collective-permute-start | bytes 688136 | tf_op jit(solution)/shard_map/ppermute | solution.py:36
  82.9 5.5 %collective-permute-done.26 = bf16[224,128]{1,0:T(8,128)(2,1)S(1)} collective-permute-done((bf16[224,128]{1,0:T(8,128)(2,1)S(1)}, bf16[224,128]{1,0:T(8,128)(2,1)S(1)}, u32[]{:S(2)}, u32[]{:S(2)}) %collective-permute-start.26) | collective-permute-done | bytes 57376 | tf_op jit(solution)/shard_map/ppermute | solution.py:36
  88.6 1.2 %collective-permute-done.25 = bf16[2,448,128]{2,1,0:T(8,128)(2,1)S(1)} collective-permute-done((bf16[2,448,128]{2,1,0:T(8,128)(2,1)S(1)}, bf16[2,448,128]{2,1,0:T(8,128)(2,1)S(1)}, u32[]{:S(2)}, u32[]{:S(2)}) %collective-permute-start.25) | collective-permute-done | bytes 229408 | tf_op jit(solution)/shard_map/ppermute | solution.py:36
  89.9 3.0 %collective-permute-start.29 = (bf16[448,128]{1,0:T(8,128)(2,1)S(1)}, bf16[448,128]{1,0:T(8,128)(2,1)S(1)}, u32[]{:S(2)}, u32[]{:S(2)}) collective-permute-start(bf16[448,128]{1,0:T(8,128)(2,1)S(1)} %fusion.1), channel_id=1, source_target_pairs={{0,12},{1,13},{2,14},{3,15},{4,0},{5,1},{6,2},{7,3},{8,4},{9,5},{1... | collective-permute-start | bytes 344072 | tf_op jit(solution)/shard_map/ppermute | solution.py:36
  92.9 4.4 %collective-permute-done.27 = bf16[448,128]{1,0:T(8,128)(2,1)S(1)} collective-permute-done((bf16[448,128]{1,0:T(8,128)(2,1)S(1)}, bf16[448,128]{1,0:T(8,128)(2,1)S(1)}, u32[]{:S(2)}, u32[]{:S(2)}) %collective-permute-start.27) | collective-permute-done | bytes 114720 | tf_op jit(solution)/shard_map/ppermute | solution.py:36
  97.3 6.3 %collective-permute-start.30 = (bf16[448,128]{1,0:T(8,128)(2,1)S(1)}, bf16[448,128]{1,0:T(8,128)(2,1)S(1)}, u32[]{:S(2)}, u32[]{:S(2)}) collective-permute-start(bf16[448,128]{1,0:T(8,128)(2,1)S(1)} %fusion.6), channel_id=1, source_target_pairs={{0,0},{1,1},{2,2},{3,3},{4,64},{5,65},{6,66},{7,67},{8,128},{9,129... | collective-permute-start | bytes 344072 | tf_op jit(solution)/shard_map/ppermute | solution.py:36
  103.6 6.8 %collective-permute-done.30 = bf16[448,128]{1,0:T(8,128)(2,1)S(1)} collective-permute-done((bf16[448,128]{1,0:T(8,128)(2,1)S(1)}, bf16[448,128]{1,0:T(8,128)(2,1)S(1)}, u32[]{:S(2)}, u32[]{:S(2)}) %collective-permute-start.30) | collective-permute-done | bytes 114720 | tf_op jit(solution)/shard_map/ppermute | solution.py:36
  110.4 0.6 copy.8
  (33 shorter events, 0.6 us)
Async XLA Ops:
  0.0 35.0 %copy-start = (bf16[8,512,128]{2,1,0:T(8,128)(2,1)S(1)}, bf16[8,512,128]{2,1,0:T(8,128)(2,1)}, u32[]{:S(2)}) copy-start(bf16[8,512,128]{2,1,0:T(8,128)(2,1)} %w_uv_any.1) | copy-start | bytes 3145732
  0.0 31.7 %collective-permute-start = (bf16[448,1024]{1,0:T(8,128)(2,1)}, bf16[448,1024]{1,0:T(8,128)(2,1)S(1)}, u32[]{:S(2)}, u32[]{:S(2)}) collective-permute-start(bf16[448,1024]{1,0:T(8,128)(2,1)} %bitcast.23), channel_id=1, source_target_pairs={{0,48},{1,0},{2,50},{3,2},{4,52},{5,4},{6,54},{7,6},{8,56},{9,8},{... | collective-permute-start | bytes 2752520 | tf_op jit(solution)/shard_map/ppermute | solution.py:36
  2.5 7.0 %collective-permute-start.12 = (bf16[576,128]{1,0:T(8,128)(2,1)}, bf16[576,128]{1,0:T(8,128)(2,1)S(1)}, u32[]{:S(2)}, u32[]{:S(2)}) collective-permute-start(bf16[576,128]{1,0:T(8,128)(2,1)} %bitcast.27), channel_id=1, source_target_pairs={{48,193},{49,192},{50,195},{51,194},{52,197},{53,196},{54,199},{55... | collective-permute-start | bytes 442376 | tf_op jit(solution)/shard_map/ppermute | solution.py:36
  3.1 16.1 %collective-permute-start.9 = (bf16[576,128]{1,0:T(8,128)(2,1)}, bf16[576,128]{1,0:T(8,128)(2,1)S(1)}, u32[]{:S(2)}, u32[]{:S(2)}) collective-permute-start(bf16[576,128]{1,0:T(8,128)(2,1)} %bitcast.28), channel_id=1, source_target_pairs={{0,161},{1,160},{2,163},{3,162},{4,165},{5,164},{6,167},{7,166},{8... | collective-permute-start | bytes 442376 | tf_op jit(solution)/shard_map/ppermute | solution.py:36
  4.4 15.9 %collective-permute-start.8 = (bf16[576,128]{1,0:T(8,128)(2,1)}, bf16[576,128]{1,0:T(8,128)(2,1)S(1)}, u32[]{:S(2)}, u32[]{:S(2)}) collective-permute-start(bf16[576,128]{1,0:T(8,128)(2,1)} %bitcast.29), channel_id=1, source_target_pairs={{0,128},{1,129},{2,130},{3,131},{4,132},{5,133},{6,134},{7,135},{8... | collective-permute-start | bytes 442376 | tf_op jit(solution)/shard_map/ppermute | solution.py:36
  5.7 18.6 %collective-permute-start.6 = (bf16[576,128]{1,0:T(8,128)(2,1)}, bf16[576,128]{1,0:T(8,128)(2,1)S(1)}, u32[]{:S(2)}, u32[]{:S(2)}) collective-permute-start(bf16[576,128]{1,0:T(8,128)(2,1)} %bitcast.30), channel_id=1, source_target_pairs={{0,97},{1,96},{2,99},{3,98},{4,101},{5,100},{6,103},{7,102},{8,105... | collective-permute-start | bytes 442376 | tf_op jit(solution)/shard_map/ppermute | solution.py:36
  9.5 17.5 %collective-permute-start.4 = (bf16[576,128]{1,0:T(8,128)(2,1)}, bf16[576,128]{1,0:T(8,128)(2,1)S(1)}, u32[]{:S(2)}, u32[]{:S(2)}) collective-permute-start(bf16[576,128]{1,0:T(8,128)(2,1)} %bitcast.31), channel_id=1, source_target_pairs={{0,64},{1,65},{2,66},{3,67},{4,68},{5,69},{6,70},{7,71},{8,72},{9,... | collective-permute-start | bytes 442376 | tf_op jit(solution)/shard_map/ppermute | solution.py:36
  19.2 8.4 %collective-permute-start.2 = (bf16[576,128]{1,0:T(8,128)(2,1)}, bf16[576,128]{1,0:T(8,128)(2,1)S(1)}, u32[]{:S(2)}, u32[]{:S(2)}) collective-permute-start(bf16[576,128]{1,0:T(8,128)(2,1)} %bitcast.32), channel_id=1, source_target_pairs={{0,33},{1,32},{2,35},{3,34},{4,37},{5,36},{6,39},{7,38},{8,41},{9,... | collective-permute-start | bytes 442376 | tf_op jit(solution)/shard_map/ppermute | solution.py:36
  20.3 7.5 %collective-permute-start.1 = (bf16[576,128]{1,0:T(8,128)(2,1)}, bf16[576,128]{1,0:T(8,128)(2,1)S(1)}, u32[]{:S(2)}, u32[]{:S(2)}) collective-permute-start(bf16[576,128]{1,0:T(8,128)(2,1)} %bitcast.33), channel_id=1, source_target_pairs={{0,16},{1,17},{2,18},{3,19},{4,20},{5,21},{6,22},{7,23},{8,24},{9,... | collective-permute-start | bytes 442376 | tf_op jit(solution)/shard_map/ppermute | solution.py:36
  24.3 3.8 %collective-permute-start.7 = (bf16[576,128]{1,0:T(8,128)(2,1)S(1)}, bf16[576,128]{1,0:T(8,128)(2,1)S(1)}, u32[]{:S(2)}, u32[]{:S(2)}) collective-permute-start(bf16[576,128]{1,0:T(8,128)(2,1)S(1)} %collective-permute-done.6.rest_6_), channel_id=1, source_target_pairs={{0,16},{1,17},{2,18},{3,19},{4,20},{5,21},{6,22},{7,23},{8,24},{9,... | collective-permute-start | bytes 442376 | tf_op jit(solution)/shard_map/ppermute | solution.py:36
  24.3 1.2 %copy-start.1 = (bf16[8,512,128]{2,1,0:T(8,128)(2,1)S(1)}, bf16[8,512,128]{2,1,0:T(8,128)(2,1)}, u32[]{:S(2)}) copy-start(bf16[8,512,128]{2,1,0:T(8,128)(2,1)} %w_uk_ref.1) | copy-start | bytes 3145732
  25.6 1.0 copy-start.3
  26.6 8.5 %copy-start.4 = (bf16[128,576]{0,1:T(8,128)(2,1)S(1)}, bf16[128,576]{0,1:T(8,128)(2,1)}, u32[]{:S(2)}) copy-start(bf16[128,576]{0,1:T(8,128)(2,1)} %param.7) | copy-start | bytes 442372
  27.0 8.0 %copy-start.5 = (s32[8]{0:T(128)S(1)}, s32[8]{0:T(128)}, u32[]{:S(2)}) copy-start(s32[8]{0:T(128)} %lengths_ref.1) | copy-start | bytes 100
  27.0 44.0 %copy-start.2 = (bf16[1024,448]{0,1:T(8,128)(2,1)S(1)}, bf16[1024,448]{0,1:T(8,128)(2,1)}, u32[]{:S(2)}) copy-start(bf16[1024,448]{0,1:T(8,128)(2,1)} %param.10) | copy-start | bytes 2752516
  27.0 2.2 %collective-permute-start.10 = (bf16[576,128]{1,0:T(8,128)(2,1)S(1)}, bf16[576,128]{1,0:T(8,128)(2,1)S(1)}, u32[]{:S(2)}, u32[]{:S(2)}) collective-permute-start(bf16[576,128]{1,0:T(8,128)(2,1)S(1)} %collective-permute-done.8.rest_8_), channel_id=1, source_target_pairs={{0,16},{1,17},{2,18},{3,19},{4,20},{5,21},{6,22},{7,23},{8,24},{9,... | collective-permute-start | bytes 442376 | tf_op jit(solution)/shard_map/ppermute | solution.py:36
  27.6 1.4 %collective-permute-start.5 = (bf16[576,128]{1,0:T(8,128)(2,1)S(1)}, bf16[576,128]{1,0:T(8,128)(2,1)S(1)}, u32[]{:S(2)}, u32[]{:S(2)}) collective-permute-start(bf16[576,128]{1,0:T(8,128)(2,1)S(1)} %collective-permute-done.4.rest_4_), channel_id=1, source_target_pairs={{0,16},{1,17},{2,18},{3,19},{4,20},{5,21},{6,22},{7,23},{8,24},{9,... | collective-permute-start | bytes 442376 | tf_op jit(solution)/shard_map/ppermute | solution.py:36
  27.8 1.5 %collective-permute-start.3 = (bf16[576,128]{1,0:T(8,128)(2,1)S(1)}, bf16[576,128]{1,0:T(8,128)(2,1)S(1)}, u32[]{:S(2)}, u32[]{:S(2)}) collective-permute-start(bf16[576,128]{1,0:T(8,128)(2,1)S(1)} %collective-permute-done.2.rest_2_), channel_id=1, source_target_pairs={{0,16},{1,17},{2,18},{3,19},{4,20},{5,21},{6,22},{7,23},{8,24},{9,... | collective-permute-start | bytes 442376 | tf_op jit(solution)/shard_map/ppermute | solution.py:36
  28.2 1.4 %collective-permute-start.11 = (bf16[576,128]{1,0:T(8,128)(2,1)S(1)}, bf16[576,128]{1,0:T(8,128)(2,1)S(1)}, u32[]{:S(2)}, u32[]{:S(2)}) collective-permute-start(bf16[576,128]{1,0:T(8,128)(2,1)S(1)} %collective-permute-done.9.rest_10_), channel_id=1, source_target_pairs={{0,16},{1,17},{2,18},{3,19},{4,20},{5,21},{6,22},{7,23},{8,24},{9,... | collective-permute-start | bytes 442376 | tf_op jit(solution)/shard_map/ppermute | solution.py:36
  29.5 4.4 %collective-permute-start.14 = (bf16[448,1024]{1,0:T(8,128)(2,1)}, bf16[448,1024]{1,0:T(8,128)(2,1)S(1)}, u32[]{:S(2)}, u32[]{:S(2)}) collective-permute-start(bf16[448,1024]{1,0:T(8,128)(2,1)} %bitcast.24), channel_id=1, source_target_pairs={{0,16},{2,18},{4,20},{6,22},{8,24},{10,26},{12,28},{14,30},{17,1},... | collective-permute-start | bytes 2752520 | tf_op jit(solution)/shard_map/ppermute | solution.py:36
  31.7 3.3 %collective-permute-start.13 = (bf16[448,1024]{1,0:T(8,128)(2,1)S(1)}, bf16[448,1024]{1,0:T(8,128)(2,1)S(1)}, u32[]{:S(2)}, u32[]{:S(2)}) collective-permute-start(bf16[448,1024]{1,0:T(8,128)(2,1)S(1)} %collective-permute-done.rest_9_.rest_15_), channel_id=1, source_target_pairs={{0,16},{1,17},{2,18},{3,19},{4,20},{5,21},{6,22},{7,23},{8,24},{9,... | collective-permute-start | bytes 2752520 | tf_op jit(solution)/shard_map/ppermute | solution.py:36
  31.8 13.0 %collective-permute-start.22 = (bf16[448,1024]{1,0:T(8,128)(2,1)}, bf16[448,1024]{1,0:T(8,128)(2,1)S(1)}, u32[]{:S(2)}, u32[]{:S(2)}) collective-permute-start(bf16[448,1024]{1,0:T(8,128)(2,1)} %bitcast.25), channel_id=1, source_target_pairs={{1,48},{3,50},{5,52},{7,54},{9,56},{11,58},{13,60},{15,62},{16,33}... | collective-permute-start | bytes 2752520 | tf_op jit(solution)/shard_map/ppermute | solution.py:36
  42.4 9.2 %collective-permute-start.18 = (bf16[128,1024]{1,0:T(8,128)(2,1)S(1)}, bf16[128,1024]{1,0:T(8,128)(2,1)S(1)}, u32[]{:S(2)}, u32[]{:S(2)}) collective-permute-start(bf16[128,1024]{1,0:T(8,128)(2,1)S(1)} %attend.1.rest_0_), channel_id=1, source_target_pairs={{0,1},{1,0},{2,3},{3,2},{4,5},{5,4},{6,7},{7,6},{8,9},{9,8},{10,11... | collective-permute-start | bytes 786440 | tf_op jit(solution)/shard_map/ppermute | solution.py:36
  42.5 9.2 %collective-permute-start.17 = (bf16[128,1024]{1,0:T(8,128)(2,1)S(1)}, bf16[128,1024]{1,0:T(8,128)(2,1)S(1)}, u32[]{:S(2)}, u32[]{:S(2)}) collective-permute-start(bf16[128,1024]{1,0:T(8,128)(2,1)S(1)} %attend.1.rest_0_), channel_id=1, source_target_pairs={{0,192},{1,193},{2,194},{3,195},{4,196},{5,197},{6,198},{7,199},{8... | collective-permute-start | bytes 786440 | tf_op jit(solution)/shard_map/ppermute | solution.py:36
  42.6 10.8 %collective-permute-start.16 = (bf16[128,1024]{1,0:T(8,128)(2,1)S(1)}, bf16[128,1024]{1,0:T(8,128)(2,1)S(1)}, u32[]{:S(2)}, u32[]{:S(2)}) collective-permute-start(bf16[128,1024]{1,0:T(8,128)(2,1)S(1)} %attend.1.rest_0_), channel_id=1, source_target_pairs={{0,128},{1,129},{2,130},{3,131},{4,132},{5,133},{6,134},{7,135},{8... | collective-permute-start | bytes 786440 | tf_op jit(solution)/shard_map/ppermute | solution.py:36
  42.7 15.9 %collective-permute-start.15 = (bf16[128,1024]{1,0:T(8,128)(2,1)S(1)}, bf16[128,1024]{1,0:T(8,128)(2,1)S(1)}, u32[]{:S(2)}, u32[]{:S(2)}) collective-permute-start(bf16[128,1024]{1,0:T(8,128)(2,1)S(1)} %attend.1.rest_0_), channel_id=1, source_target_pairs={{0,64},{1,65},{2,66},{3,67},{4,68},{5,69},{6,70},{7,71},{8,72},{9,... | collective-permute-start | bytes 786440 | tf_op jit(solution)/shard_map/ppermute | solution.py:36
  58.6 12.4 %collective-permute-start.23 = (bf16[448,1024]{1,0:T(8,128)(2,1)S(1)}, bf16[448,1024]{1,0:T(8,128)(2,1)S(1)}, u32[]{:S(2)}, u32[]{:S(2)}) collective-permute-start(bf16[448,1024]{1,0:T(8,128)(2,1)S(1)} %collective-permute-done.22.rest_14_), channel_id=1, source_target_pairs={{1,17},{3,19},{5,21},{7,23},{9,25},{11,27},{13,29},{15,31},{16,0},... | collective-permute-start | bytes 2752520 | tf_op jit(solution)/shard_map/ppermute | solution.py:36
  60.1 9.0 %collective-permute-start.21 = (bf16[128,1024]{1,0:T(8,128)(2,1)S(1)}, bf16[128,1024]{1,0:T(8,128)(2,1)S(1)}, u32[]{:S(2)}, u32[]{:S(2)}) collective-permute-start(bf16[128,1024]{1,0:T(8,128)(2,1)S(1)} %collective-permute-done.18.rest_4_), channel_id=1, source_target_pairs={{0,192},{1,193},{2,194},{3,195},{4,196},{5,197},{6,198},{7,199},{8... | collective-permute-start | bytes 786440 | tf_op jit(solution)/shard_map/ppermute | solution.py:36
  61.1 9.1 %collective-permute-start.19 = (bf16[128,1024]{1,0:T(8,128)(2,1)S(1)}, bf16[128,1024]{1,0:T(8,128)(2,1)S(1)}, u32[]{:S(2)}, u32[]{:S(2)}) collective-permute-start(bf16[128,1024]{1,0:T(8,128)(2,1)S(1)} %collective-permute-done.18.rest_4_), channel_id=1, source_target_pairs={{0,64},{1,65},{2,66},{3,67},{4,68},{5,69},{6,70},{7,71},{8,72},{9,... | collective-permute-start | bytes 786440 | tf_op jit(solution)/shard_map/ppermute | solution.py:36
  62.2 8.8 %collective-permute-start.20 = (bf16[128,1024]{1,0:T(8,128)(2,1)S(1)}, bf16[128,1024]{1,0:T(8,128)(2,1)S(1)}, u32[]{:S(2)}, u32[]{:S(2)}) collective-permute-start(bf16[128,1024]{1,0:T(8,128)(2,1)S(1)} %collective-permute-done.16.rest_2_), channel_id=1, source_target_pairs={{0,1},{1,0},{2,3},{3,2},{4,5},{5,4},{6,7},{7,6},{8,9},{9,8},{10,11... | collective-permute-start | bytes 786440 | tf_op jit(solution)/shard_map/ppermute | solution.py:36
  74.0 14.5 %collective-permute-start.24 = (bf16[2,448,128]{2,1,0:T(8,128)(2,1)S(1)}, bf16[2,448,128]{2,1,0:T(8,128)(2,1)S(1)}, u32[]{:S(2)}, u32[]{:S(2)}) collective-permute-start(bf16[2,448,128]{2,1,0:T(8,128)(2,1)S(1)} %get-tuple-element.31), channel_id=1, source_target_pairs={{0,2},{1,3},{2,4},{3,5},{4,6},{5,7},{6,8},{7,9},{8,10},{9,11},{10,... | collective-permute-start | bytes 688136 | tf_op jit(solution)/shard_map/ppermute | solution.py:36
  76.0 12.5 %collective-permute-start.26 = (bf16[224,128]{1,0:T(8,128)(2,1)S(1)}, bf16[224,128]{1,0:T(8,128)(2,1)S(1)}, u32[]{:S(2)}, u32[]{:S(2)}) collective-permute-start(bf16[224,128]{1,0:T(8,128)(2,1)S(1)} %get-tuple-element.34), channel_id=1, source_target_pairs={{0,4},{1,5},{2,6},{3,7},{4,8},{5,9},{6,10},{7,11},{8,12},{9,13},{1... | collective-permute-start | bytes 172040 | tf_op jit(solution)/shard_map/ppermute | solution.py:36
  79.2 9.4 %collective-permute-start.28 = (bf16[224,128]{1,0:T(8,128)(2,1)S(1)}, bf16[224,128]{1,0:T(8,128)(2,1)S(1)}, u32[]{:S(2)}, u32[]{:S(2)}) collective-permute-start(bf16[224,128]{1,0:T(8,128)(2,1)S(1)} %get-tuple-element.36), channel_id=1, source_target_pairs={{0,12},{1,13},{2,14},{3,15},{4,0},{5,1},{6,2},{7,3},{8,4},{9,5},{1... | collective-permute-start | bytes 172040 | tf_op jit(solution)/shard_map/ppermute | solution.py:36
  81.4 8.4 %collective-permute-start.25 = (bf16[2,448,128]{2,1,0:T(8,128)(2,1)S(1)}, bf16[2,448,128]{2,1,0:T(8,128)(2,1)S(1)}, u32[]{:S(2)}, u32[]{:S(2)}) collective-permute-start(bf16[2,448,128]{2,1,0:T(8,128)(2,1)S(1)} %get-tuple-element.32), channel_id=1, source_target_pairs={{0,14},{1,15},{2,0},{3,1},{4,2},{5,3},{6,4},{7,5},{8,6},{9,7},{10,... | collective-permute-start | bytes 688136 | tf_op jit(solution)/shard_map/ppermute | solution.py:36
  88.5 8.7 %collective-permute-start.27 = (bf16[448,128]{1,0:T(8,128)(2,1)S(1)}, bf16[448,128]{1,0:T(8,128)(2,1)S(1)}, u32[]{:S(2)}, u32[]{:S(2)}) collective-permute-start(bf16[448,128]{1,0:T(8,128)(2,1)S(1)} %fusion.3), channel_id=1, source_target_pairs={{0,4},{1,5},{2,6},{3,7},{4,8},{5,9},{6,10},{7,11},{8,12},{9,13},{1... | collective-permute-start | bytes 344072 | tf_op jit(solution)/shard_map/ppermute | solution.py:36
  89.9 7.4 %collective-permute-start.29 = (bf16[448,128]{1,0:T(8,128)(2,1)S(1)}, bf16[448,128]{1,0:T(8,128)(2,1)S(1)}, u32[]{:S(2)}, u32[]{:S(2)}) collective-permute-start(bf16[448,128]{1,0:T(8,128)(2,1)S(1)} %fusion.1), channel_id=1, source_target_pairs={{0,12},{1,13},{2,14},{3,15},{4,0},{5,1},{6,2},{7,3},{8,4},{9,5},{1... | collective-permute-start | bytes 344072 | tf_op jit(solution)/shard_map/ppermute | solution.py:36
  97.3 13.1 %collective-permute-start.30 = (bf16[448,128]{1,0:T(8,128)(2,1)S(1)}, bf16[448,128]{1,0:T(8,128)(2,1)S(1)}, u32[]{:S(2)}, u32[]{:S(2)}) collective-permute-start(bf16[448,128]{1,0:T(8,128)(2,1)S(1)} %fusion.6), channel_id=1, source_target_pairs={{0,0},{1,1},{2,2},{3,3},{4,64},{5,65},{6,66},{7,67},{8,128},{9,129... | collective-permute-start | bytes 344072 | tf_op jit(solution)/shard_map/ppermute | solution.py:36

commit v3 on v2

--- a/solution.py
+++ b/solution.py
@@ -297,7 +297,7 @@
     def shifted(step):
         return lambda ty, txh, tcore, tz, txl: ((ty + step) % 4, txh, tcore, tz, txl)
 
-    qc = after(qc, (w_a_other, w_own_other))
+    qc = after(qc, w_a_other)
     values = pl.pallas_call(
         attend_kernel,
         out_shape=jax.ShapeDtypeStruct((rows, heads * 128), jnp.bfloat16),
@@ -315,6 +315,8 @@
         compiler_params=pltpu.CompilerParams(vmem_limit_bytes=26 << 20),
         name="attend",
     )(doc_lengths, qc, qr, w_uv, *blocks)
+
+    values = after(values, w_own_other)
 
     near = [values] + [send(values, shifted(step)) for step in (1, 2, 3)]
     neighbour = send(values, other_lo)
@@ -359,10 +361,11 @@
     def wide(value):
         return value.astype(jnp.float32)
 
+    from_low = send(up, along(1))
+    from_high = send(down, along(7))
+    far_up, far_down = after((far_up, far_down), (up, down))
     from_far_low = send(far_up, along(2))
     from_far_high = send(far_down, along(6))
-    from_low = send(up, along(1))
-    from_high = send(down, along(7))
     up_sum = wide(up2) + wide(from_low[0]) + jnp.pad(wide(from_far_low), ((0, width // 2), (0, 0)))
     down_sum = (
         wide(down2) + wide(from_high[0]) + jnp.pad(wide(from_far_high), ((width // 2, 0), (0, 0)))

time: 113 us -> 111 us (0.982)
  starting transfers between devices: 52.4 us -> 50.9 us
  waiting for transfers between devices: 44.7 us -> 45.9 us
    ppermute x31, starting transfers between devices: 52.4 us -> 50.9 us  [send(): return lax.ppermute(value, AXES, pairs)]
    ppermute x31, waiting for transfers between devices: 44.7 us -> 45.9 us  [send(): return lax.ppermute(value, AXES, pairs)]
  transfers between devices with their start and end apart: 31 -> 31, of which waited for: 17 -> 16; matrix products, arithmetic and copies ran while one was open for 0% -> 0% of each run, Pallas kernels for 7% -> 6%
where the time goes in v3:
time: 111 us; the launch traced here: 110 us
  starting transfers between devices  50.9 us (46%)
  waiting for transfers between devices  45.9 us (41%)
  Pallas kernels  9.72 us (9%)
  local copies, waits for them, and re-layouts  2.89 us (3%)
    ppermute x31, starting transfers between devices, send(): return lax.ppermute(value, AXES, pairs)  50.9 us
    ppermute x31, waiting for transfers between devices, send(): return lax.ppermute(value, AXES, pairs)  45.9 us
    pallas_call x1, Pallas kernels, body(): pl.pallas_call(attend_kernel, out_shape=jax.ShapeDtypeStruct((rows, heads...  6.33 us
    pallas_call x1, Pallas kernels, body(): pl.pallas_call(project_kernel, out_shape=[result(width, rows), result(2,...  2.96 us
    unnamed x13, local copies, waits for them, and re-layouts  2.89 us
  transfers between devices with their start and end apart: 31, of which 16 were waited for; matrix products, arithmetic and copies ran while one was open for 0% of the time, Pallas kernels for 6%

profile of v3, /device:TPU:16, one launch (start us, length us, event | category | flops | bytes accessed | tf_op | source)
XLA Modules:
  0.0 109.8 jit_solution(2481246618479943620)
XLA Ops:
  0.0 2.5 %collective-permute-start = (bf16[448,1024]{1,0:T(8,128)(2,1)}, bf16[448,1024]{1,0:T(8,128)(2,1)S(1)}, u32[]{:S(2)}, u32[]{:S(2)}) collective-permute-start(bf16[448,1024]{1,0:T(8,128)(2,1)} %bitcast.23), channel_id=1, source_target_pairs={{0,48},{1,0},{2,50},{3,2},{4,52},{5,4},{6,54},{7,6},{8,56},{9,8},{... | collective-permute-start | bytes 2752520 | tf_op jit(solution)/shard_map/ppermute | solution.py:36
  2.5 0.7 collective-permute-start.12
  3.1 1.3 %collective-permute-start.9 = (bf16[576,128]{1,0:T(8,128)(2,1)}, bf16[576,128]{1,0:T(8,128)(2,1)S(1)}, u32[]{:S(2)}, u32[]{:S(2)}) collective-permute-start(bf16[576,128]{1,0:T(8,128)(2,1)} %bitcast.28), channel_id=1, source_target_pairs={{0,161},{1,160},{2,163},{3,162},{4,165},{5,164},{6,167},{7,166},{8... | collective-permute-start | bytes 442376 | tf_op jit(solution)/shard_map/ppermute | solution.py:36
  4.4 1.3 %collective-permute-start.8 = (bf16[576,128]{1,0:T(8,128)(2,1)}, bf16[576,128]{1,0:T(8,128)(2,1)S(1)}, u32[]{:S(2)}, u32[]{:S(2)}) collective-permute-start(bf16[576,128]{1,0:T(8,128)(2,1)} %bitcast.29), channel_id=1, source_target_pairs={{0,128},{1,129},{2,130},{3,131},{4,132},{5,133},{6,134},{7,135},{8... | collective-permute-start | bytes 442376 | tf_op jit(solution)/shard_map/ppermute | solution.py:36
  5.7 3.8 %collective-permute-start.6 = (bf16[576,128]{1,0:T(8,128)(2,1)}, bf16[576,128]{1,0:T(8,128)(2,1)S(1)}, u32[]{:S(2)}, u32[]{:S(2)}) collective-permute-start(bf16[576,128]{1,0:T(8,128)(2,1)} %bitcast.30), channel_id=1, source_target_pairs={{0,97},{1,96},{2,99},{3,98},{4,101},{5,100},{6,103},{7,102},{8,105... | collective-permute-start | bytes 442376 | tf_op jit(solution)/shard_map/ppermute | solution.py:36
  9.5 9.7 %collective-permute-start.4 = (bf16[576,128]{1,0:T(8,128)(2,1)}, bf16[576,128]{1,0:T(8,128)(2,1)S(1)}, u32[]{:S(2)}, u32[]{:S(2)}) collective-permute-start(bf16[576,128]{1,0:T(8,128)(2,1)} %bitcast.31), channel_id=1, source_target_pairs={{0,64},{1,65},{2,66},{3,67},{4,68},{5,69},{6,70},{7,71},{8,72},{9,... | collective-permute-start | bytes 442376 | tf_op jit(solution)/shard_map/ppermute | solution.py:36
  19.2 1.1 collective-permute-start.2
  20.3 1.6 %collective-permute-start.1 = (bf16[576,128]{1,0:T(8,128)(2,1)}, bf16[576,128]{1,0:T(8,128)(2,1)S(1)}, u32[]{:S(2)}, u32[]{:S(2)}) collective-permute-start(bf16[576,128]{1,0:T(8,128)(2,1)} %bitcast.33), channel_id=1, source_target_pairs={{0,16},{1,17},{2,18},{3,19},{4,20},{5,21},{6,22},{7,23},{8,24},{9,... | collective-permute-start | bytes 442376 | tf_op jit(solution)/shard_map/ppermute | solution.py:36
  21.9 2.4 %collective-permute-done.6.rest_6_ = bf16[576,128]{1,0:T(8,128)(2,1)S(1)} collective-permute-done((bf16[576,128]{1,0:T(8,128)(2,1)}, bf16[576,128]{1,0:T(8,128)(2,1)S(1)}, u32[]{:S(2)}, u32[]{:S(2)}) %collective-permute-start.6) | collective-permute-done | bytes 147488 | tf_op jit(solution)/shard_map/ppermute | solution.py:36
  24.3 1.2 %copy-done.1 = bf16[8,512,128]{2,1,0:T(8,128)(2,1)S(1)} copy-done((bf16[8,512,128]{2,1,0:T(8,128)(2,1)S(1)}, bf16[8,512,128]{2,1,0:T(8,128)(2,1)}, u32[]{:S(2)}) %copy-start.1) | copy-done | bytes 1048600
  25.6 1.0 copy-done.3
  26.6 0.4 absorb.1
  27.0 0.6 collective-permute-start.10
  27.6 0.1 collective-permute-start.5
  27.8 0.4 collective-permute-start.3
  28.3 0.7 collective-permute-done.5.rest_5_
  29.0 0.2 collective-permute-done.3.rest_3_
  29.2 0.3 collective-permute-done.11.rest_11_
  29.5 0.2 collective-permute-start.13
  29.7 2.3 %collective-permute-start.14 = (bf16[448,1024]{1,0:T(8,128)(2,1)}, bf16[448,1024]{1,0:T(8,128)(2,1)S(1)}, u32[]{:S(2)}, u32[]{:S(2)}) collective-permute-start(bf16[448,1024]{1,0:T(8,128)(2,1)} %bitcast.24), channel_id=1, source_target_pairs={{0,16},{2,18},{4,20},{6,22},{8,24},{10,26},{12,28},{14,30},{17,1},... | collective-permute-start | bytes 2752520 | tf_op jit(solution)/shard_map/ppermute | solution.py:36
  32.0 0.7 collective-permute-start.22
  32.8 6.3 %attend.1.rest_0_ = bf16[128,1024]{1,0:T(8,128)(2,1)S(1)} custom-call(s32[8]{0:T(128)S(1)} %copy-done.5, bf16[1024,512]{1,0:T(8,128)(2,1)S(1)} %get-tuple-element.29.qc_ref, bf16[1024,64]{1,0:T(8,128)(2,1)S(1)} %get-tuple-element.25.qr_ref, bf16[8,512,128]{2,1,0:T(8,128)(2,1)S(1)} %copy-done, bf16[576,128]{1,0:T(8,128)(2,1)S(1)} %bitcast.34, ...), custom_call_target="tpu_custom_call" | custom-call | tf_op jit(solution)/shard_map/attend/pallas_call | solution.py:301
  39.1 1.4 %collective-permute-start.18 = (bf16[128,1024]{1,0:T(8,128)(2,1)S(1)}, bf16[128,1024]{1,0:T(8,128)(2,1)S(1)}, u32[]{:S(2)}, u32[]{:S(2)}) collective-permute-start(bf16[128,1024]{1,0:T(8,128)(2,1)S(1)} %attend.1.rest_0_), channel_id=1, source_target_pairs={{0,1},{1,0},{2,3},{3,2},{4,5},{5,4},{6,7},{7,6},{8,9},{9,8},{10,11... | collective-permute-start | bytes 786440 | tf_op jit(solution)/shard_map/ppermute | solution.py:36
  40.5 2.0 %collective-permute-start.15 = (bf16[128,1024]{1,0:T(8,128)(2,1)S(1)}, bf16[128,1024]{1,0:T(8,128)(2,1)S(1)}, u32[]{:S(2)}, u32[]{:S(2)}) collective-permute-start(bf16[128,1024]{1,0:T(8,128)(2,1)S(1)} %attend.1.rest_0_), channel_id=1, source_target_pairs={{0,64},{1,65},{2,66},{3,67},{4,68},{5,69},{6,70},{7,71},{8,72},{9,... | collective-permute-start | bytes 786440 | tf_op jit(solution)/shard_map/ppermute | solution.py:36
  42.5 4.6 %collective-permute-done.18.rest_4_ = bf16[128,1024]{1,0:T(8,128)(2,1)S(1)} collective-permute-done((bf16[128,1024]{1,0:T(8,128)(2,1)S(1)}, bf16[128,1024]{1,0:T(8,128)(2,1)S(1)}, u32[]{:S(2)}, u32[]{:S(2)}) %collective-permute-start.18) | collective-permute-done | bytes 262176 | tf_op jit(solution)/shard_map/ppermute | solution.py:36
  47.1 2.5 %collective-permute-done.17.rest_3_ = bf16[128,1024]{1,0:T(8,128)(2,1)S(1)} collective-permute-done((bf16[128,1024]{1,0:T(8,128)(2,1)S(1)}, bf16[128,1024]{1,0:T(8,128)(2,1)S(1)}, u32[]{:S(2)}, u32[]{:S(2)}) %collective-permute-start.17) | collective-permute-done | bytes 262176 | tf_op jit(solution)/shard_map/ppermute | solution.py:36
  49.7 1.5 %collective-permute-done.16.rest_2_ = bf16[128,1024]{1,0:T(8,128)(2,1)S(1)} collective-permute-done((bf16[128,1024]{1,0:T(8,128)(2,1)S(1)}, bf16[128,1024]{1,0:T(8,128)(2,1)S(1)}, u32[]{:S(2)}, u32[]{:S(2)}) %collective-permute-start.16) | collective-permute-done | bytes 262176 | tf_op jit(solution)/shard_map/ppermute | solution.py:36
  51.2 5.3 %collective-permute-done.15.rest_1_ = bf16[128,1024]{1,0:T(8,128)(2,1)S(1)} collective-permute-done((bf16[128,1024]{1,0:T(8,128)(2,1)S(1)}, bf16[128,1024]{1,0:T(8,128)(2,1)S(1)}, u32[]{:S(2)}, u32[]{:S(2)}) %collective-permute-start.15) | collective-permute-done | bytes 262176 | tf_op jit(solution)/shard_map/ppermute | solution.py:36
  56.5 1.5 %collective-permute-start.23 = (bf16[448,1024]{1,0:T(8,128)(2,1)S(1)}, bf16[448,1024]{1,0:T(8,128)(2,1)S(1)}, u32[]{:S(2)}, u32[]{:S(2)}) collective-permute-start(bf16[448,1024]{1,0:T(8,128)(2,1)S(1)} %collective-permute-done.22.rest_14_), channel_id=1, source_target_pairs={{1,17},{3,19},{5,21},{7,23},{9,25},{11,27},{13,29},{15,31},{16,0},... | collective-permute-start | bytes 2752520 | tf_op jit(solution)/shard_map/ppermute | solution.py:36
  58.0 0.9 collective-permute-start.21
  58.9 1.2 %collective-permute-start.19 = (bf16[128,1024]{1,0:T(8,128)(2,1)S(1)}, bf16[128,1024]{1,0:T(8,128)(2,1)S(1)}, u32[]{:S(2)}, u32[]{:S(2)}) collective-permute-start(bf16[128,1024]{1,0:T(8,128)(2,1)S(1)} %collective-permute-done.18.rest_4_), channel_id=1, source_target_pairs={{0,64},{1,65},{2,66},{3,67},{4,68},{5,69},{6,70},{7,71},{8,72},{9,... | collective-permute-start | bytes 786440 | tf_op jit(solution)/shard_map/ppermute | solution.py:36
  60.1 1.6 %collective-permute-start.20 = (bf16[128,1024]{1,0:T(8,128)(2,1)S(1)}, bf16[128,1024]{1,0:T(8,128)(2,1)S(1)}, u32[]{:S(2)}, u32[]{:S(2)}) collective-permute-start(bf16[128,1024]{1,0:T(8,128)(2,1)S(1)} %collective-permute-done.16.rest_2_), channel_id=1, source_target_pairs={{0,1},{1,0},{2,3},{3,2},{4,5},{5,4},{6,7},{7,6},{8,9},{9,8},{10,11... | collective-permute-start | bytes 786440 | tf_op jit(solution)/shard_map/ppermute | solution.py:36
  61.7 5.3 %collective-permute-done.21.rest_7_ = bf16[128,1024]{1,0:T(8,128)(2,1)S(1)} collective-permute-done((bf16[128,1024]{1,0:T(8,128)(2,1)S(1)}, bf16[128,1024]{1,0:T(8,128)(2,1)S(1)}, u32[]{:S(2)}, u32[]{:S(2)}) %collective-permute-start.21) | collective-permute-done | bytes 262176 | tf_op jit(solution)/shard_map/ppermute | solution.py:36
  67.0 0.9 collective-permute-done.19.rest_5_
  68.0 1.0 collective-permute-done.20.rest_6_
  68.9 3.0 %project.1 = (bf16[448,128]{1,0:T(8,128)(2,1)S(1)}, bf16[2,448,128]{2,1,0:T(8,128)(2,1)S(1)}, bf16[2,448,128]{2,1,0:T(8,128)(2,1)S(1)}, bf16[224,128]{1,0:T(8,12...) custom-call(bf16[128,1024]{1,0:T(8,128)(2,1)S(1)} %attend.1.rest_0_, ...), custom_call_target="tpu_custom_call" | custom-call | tf_op jit(solution)/shard_map/project/pallas_call | solution.py:336
  71.9 2.0 %collective-permute-start.24 = (bf16[2,448,128]{2,1,0:T(8,128)(2,1)S(1)}, bf16[2,448,128]{2,1,0:T(8,128)(2,1)S(1)}, u32[]{:S(2)}, u32[]{:S(2)}) collective-permute-start(bf16[2,448,128]{2,1,0:T(8,128)(2,1)S(1)} %get-tuple-element.35), channel_id=1, source_target_pairs={{0,2},{1,3},{2,4},{3,5},{4,6},{5,7},{6,8},{7,9},{8,10},{9,11},{10,... | collective-permute-start | bytes 688136 | tf_op jit(solution)/shard_map/ppermute | solution.py:36
  73.9 3.3 %collective-permute-start.26 = (bf16[224,128]{1,0:T(8,128)(2,1)S(1)}, bf16[224,128]{1,0:T(8,128)(2,1)S(1)}, u32[]{:S(2)}, u32[]{:S(2)}) collective-permute-start(bf16[224,128]{1,0:T(8,128)(2,1)S(1)} %get-tuple-element.40), channel_id=1, source_target_pairs={{0,4},{1,5},{2,6},{3,7},{4,8},{5,9},{6,10},{7,11},{8,12},{9,13},{1... | collective-permute-start | bytes 172040 | tf_op jit(solution)/shard_map/ppermute | solution.py:36
  77.1 1.3 %collective-permute-start.25 = (bf16[2,448,128]{2,1,0:T(8,128)(2,1)S(1)}, bf16[2,448,128]{2,1,0:T(8,128)(2,1)S(1)}, u32[]{:S(2)}, u32[]{:S(2)}) collective-permute-start(bf16[2,448,128]{2,1,0:T(8,128)(2,1)S(1)} %get-tuple-element.36), channel_id=1, source_target_pairs={{0,14},{1,15},{2,0},{3,1},{4,2},{5,3},{6,4},{7,5},{8,6},{9,7},{10,... | collective-permute-start | bytes 688136 | tf_op jit(solution)/shard_map/ppermute | solution.py:36
  78.5 2.4 %collective-permute-start.28 = (bf16[224,128]{1,0:T(8,128)(2,1)S(1)}, bf16[224,128]{1,0:T(8,128)(2,1)S(1)}, u32[]{:S(2)}, u32[]{:S(2)}) collective-permute-start(bf16[224,128]{1,0:T(8,128)(2,1)S(1)} %get-tuple-element.42), channel_id=1, source_target_pairs={{0,12},{1,13},{2,14},{3,15},{4,0},{5,1},{6,2},{7,3},{8,4},{9,5},{1... | collective-permute-start | bytes 172040 | tf_op jit(solution)/shard_map/ppermute | solution.py:36
  80.8 5.6 %collective-permute-done.26 = bf16[224,128]{1,0:T(8,128)(2,1)S(1)} collective-permute-done((bf16[224,128]{1,0:T(8,128)(2,1)S(1)}, bf16[224,128]{1,0:T(8,128)(2,1)S(1)}, u32[]{:S(2)}, u32[]{:S(2)}) %collective-permute-start.26) | collective-permute-done | bytes 57376 | tf_op jit(solution)/shard_map/ppermute | solution.py:36
  86.6 2.4 %collective-permute-done.28 = bf16[224,128]{1,0:T(8,128)(2,1)S(1)} collective-permute-done((bf16[224,128]{1,0:T(8,128)(2,1)S(1)}, bf16[224,128]{1,0:T(8,128)(2,1)S(1)}, u32[]{:S(2)}, u32[]{:S(2)}) %collective-permute-start.28) | collective-permute-done | bytes 57376 | tf_op jit(solution)/shard_map/ppermute | solution.py:36
  89.0 1.8 %collective-permute-start.29 = (bf16[448,128]{1,0:T(8,128)(2,1)S(1)}, bf16[448,128]{1,0:T(8,128)(2,1)S(1)}, u32[]{:S(2)}, u32[]{:S(2)}) collective-permute-start(bf16[448,128]{1,0:T(8,128)(2,1)S(1)} %fusion.1), channel_id=1, source_target_pairs={{0,12},{1,13},{2,14},{3,15},{4,0},{5,1},{6,2},{7,3},{8,4},{9,5},{1... | collective-permute-start | bytes 344072 | tf_op jit(solution)/shard_map/ppermute | solution.py:36
  90.8 4.4 %collective-permute-done.27 = bf16[448,128]{1,0:T(8,128)(2,1)S(1)} collective-permute-done((bf16[448,128]{1,0:T(8,128)(2,1)S(1)}, bf16[448,128]{1,0:T(8,128)(2,1)S(1)}, u32[]{:S(2)}, u32[]{:S(2)}) %collective-permute-start.27) | collective-permute-done | bytes 114720 | tf_op jit(solution)/shard_map/ppermute | solution.py:36
  95.2 0.8 collective-permute-done.29
  96.1 5.2 %collective-permute-start.30 = (bf16[448,128]{1,0:T(8,128)(2,1)S(1)}, bf16[448,128]{1,0:T(8,128)(2,1)S(1)}, u32[]{:S(2)}, u32[]{:S(2)}) collective-permute-start(bf16[448,128]{1,0:T(8,128)(2,1)S(1)} %fusion.6), channel_id=1, source_target_pairs={{0,0},{1,1},{2,2},{3,3},{4,64},{5,65},{6,66},{7,67},{8,128},{9,129... | collective-permute-start | bytes 344072 | tf_op jit(solution)/shard_map/ppermute | solution.py:36
  101.3 7.8 %collective-permute-done.30 = bf16[448,128]{1,0:T(8,128)(2,1)S(1)} collective-permute-done((bf16[448,128]{1,0:T(8,128)(2,1)S(1)}, bf16[448,128]{1,0:T(8,128)(2,1)S(1)}, u32[]{:S(2)}, u32[]{:S(2)}) %collective-permute-start.30) | collective-permute-done | bytes 114720 | tf_op jit(solution)/shard_map/ppermute | solution.py:36
  109.1 0.6 copy.8
  (33 shorter events, 0.4 us)
Async XLA Ops:
  0.0 32.8 %copy-start = (bf16[8,512,128]{2,1,0:T(8,128)(2,1)S(1)}, bf16[8,512,128]{2,1,0:T(8,128)(2,1)}, u32[]{:S(2)}) copy-start(bf16[8,512,128]{2,1,0:T(8,128)(2,1)} %w_uv_any.1) | copy-start | bytes 3145732
  0.0 29.5 %collective-permute-start = (bf16[448,1024]{1,0:T(8,128)(2,1)}, bf16[448,1024]{1,0:T(8,128)(2,1)S(1)}, u32[]{:S(2)}, u32[]{:S(2)}) collective-permute-start(bf16[448,1024]{1,0:T(8,128)(2,1)} %bitcast.23), channel_id=1, source_target_pairs={{0,48},{1,0},{2,50},{3,2},{4,52},{5,4},{6,54},{7,6},{8,56},{9,8},{... | collective-permute-start | bytes 2752520 | tf_op jit(solution)/shard_map/ppermute | solution.py:36
  2.5 7.0 %collective-permute-start.12 = (bf16[576,128]{1,0:T(8,128)(2,1)}, bf16[576,128]{1,0:T(8,128)(2,1)S(1)}, u32[]{:S(2)}, u32[]{:S(2)}) collective-permute-start(bf16[576,128]{1,0:T(8,128)(2,1)} %bitcast.27), channel_id=1, source_target_pairs={{48,193},{49,192},{50,195},{51,194},{52,197},{53,196},{54,199},{55... | collective-permute-start | bytes 442376 | tf_op jit(solution)/shard_map/ppermute | solution.py:36
  3.1 16.1 %collective-permute-start.9 = (bf16[576,128]{1,0:T(8,128)(2,1)}, bf16[576,128]{1,0:T(8,128)(2,1)S(1)}, u32[]{:S(2)}, u32[]{:S(2)}) collective-permute-start(bf16[576,128]{1,0:T(8,128)(2,1)} %bitcast.28), channel_id=1, source_target_pairs={{0,161},{1,160},{2,163},{3,162},{4,165},{5,164},{6,167},{7,166},{8... | collective-permute-start | bytes 442376 | tf_op jit(solution)/shard_map/ppermute | solution.py:36
  4.4 15.9 %collective-permute-start.8 = (bf16[576,128]{1,0:T(8,128)(2,1)}, bf16[576,128]{1,0:T(8,128)(2,1)S(1)}, u32[]{:S(2)}, u32[]{:S(2)}) collective-permute-start(bf16[576,128]{1,0:T(8,128)(2,1)} %bitcast.29), channel_id=1, source_target_pairs={{0,128},{1,129},{2,130},{3,131},{4,132},{5,133},{6,134},{7,135},{8... | collective-permute-start | bytes 442376 | tf_op jit(solution)/shard_map/ppermute | solution.py:36
  5.7 18.6 %collective-permute-start.6 = (bf16[576,128]{1,0:T(8,128)(2,1)}, bf16[576,128]{1,0:T(8,128)(2,1)S(1)}, u32[]{:S(2)}, u32[]{:S(2)}) collective-permute-start(bf16[576,128]{1,0:T(8,128)(2,1)} %bitcast.30), channel_id=1, source_target_pairs={{0,97},{1,96},{2,99},{3,98},{4,101},{5,100},{6,103},{7,102},{8,105... | collective-permute-start | bytes 442376 | tf_op jit(solution)/shard_map/ppermute | solution.py:36
  9.5 17.5 %collective-permute-start.4 = (bf16[576,128]{1,0:T(8,128)(2,1)}, bf16[576,128]{1,0:T(8,128)(2,1)S(1)}, u32[]{:S(2)}, u32[]{:S(2)}) collective-permute-start(bf16[576,128]{1,0:T(8,128)(2,1)} %bitcast.31), channel_id=1, source_target_pairs={{0,64},{1,65},{2,66},{3,67},{4,68},{5,69},{6,70},{7,71},{8,72},{9,... | collective-permute-start | bytes 442376 | tf_op jit(solution)/shard_map/ppermute | solution.py:36
  19.2 8.4 %collective-permute-start.2 = (bf16[576,128]{1,0:T(8,128)(2,1)}, bf16[576,128]{1,0:T(8,128)(2,1)S(1)}, u32[]{:S(2)}, u32[]{:S(2)}) collective-permute-start(bf16[576,128]{1,0:T(8,128)(2,1)} %bitcast.32), channel_id=1, source_target_pairs={{0,33},{1,32},{2,35},{3,34},{4,37},{5,36},{6,39},{7,38},{8,41},{9,... | collective-permute-start | bytes 442376 | tf_op jit(solution)/shard_map/ppermute | solution.py:36
  20.3 7.5 %collective-permute-start.1 = (bf16[576,128]{1,0:T(8,128)(2,1)}, bf16[576,128]{1,0:T(8,128)(2,1)S(1)}, u32[]{:S(2)}, u32[]{:S(2)}) collective-permute-start(bf16[576,128]{1,0:T(8,128)(2,1)} %bitcast.33), channel_id=1, source_target_pairs={{0,16},{1,17},{2,18},{3,19},{4,20},{5,21},{6,22},{7,23},{8,24},{9,... | collective-permute-start | bytes 442376 | tf_op jit(solution)/shard_map/ppermute | solution.py:36
  24.3 3.8 %collective-permute-start.7 = (bf16[576,128]{1,0:T(8,128)(2,1)S(1)}, bf16[576,128]{1,0:T(8,128)(2,1)S(1)}, u32[]{:S(2)}, u32[]{:S(2)}) collective-permute-start(bf16[576,128]{1,0:T(8,128)(2,1)S(1)} %collective-permute-done.6.rest_6_), channel_id=1, source_target_pairs={{0,16},{1,17},{2,18},{3,19},{4,20},{5,21},{6,22},{7,23},{8,24},{9,... | collective-permute-start | bytes 442376 | tf_op jit(solution)/shard_map/ppermute | solution.py:36
  24.3 1.2 %copy-start.1 = (bf16[8,512,128]{2,1,0:T(8,128)(2,1)S(1)}, bf16[8,512,128]{2,1,0:T(8,128)(2,1)}, u32[]{:S(2)}) copy-start(bf16[8,512,128]{2,1,0:T(8,128)(2,1)} %w_uk_ref.1) | copy-start | bytes 3145732
  25.6 1.0 copy-start.3
  26.6 6.2 %copy-start.4 = (bf16[128,576]{0,1:T(8,128)(2,1)S(1)}, bf16[128,576]{0,1:T(8,128)(2,1)}, u32[]{:S(2)}) copy-start(bf16[128,576]{0,1:T(8,128)(2,1)} %param.7) | copy-start | bytes 442372
  27.0 5.8 %copy-start.5 = (s32[8]{0:T(128)S(1)}, s32[8]{0:T(128)}, u32[]{:S(2)}) copy-start(s32[8]{0:T(128)} %lengths_ref.1) | copy-start | bytes 100
  27.0 41.9 %copy-start.2 = (bf16[1024,448]{0,1:T(8,128)(2,1)S(1)}, bf16[1024,448]{0,1:T(8,128)(2,1)}, u32[]{:S(2)}) copy-start(bf16[1024,448]{0,1:T(8,128)(2,1)} %param.10) | copy-start | bytes 2752516
  27.0 2.2 %collective-permute-start.10 = (bf16[576,128]{1,0:T(8,128)(2,1)S(1)}, bf16[576,128]{1,0:T(8,128)(2,1)S(1)}, u32[]{:S(2)}, u32[]{:S(2)}) collective-permute-start(bf16[576,128]{1,0:T(8,128)(2,1)S(1)} %collective-permute-done.8.rest_8_), channel_id=1, source_target_pairs={{0,16},{1,17},{2,18},{3,19},{4,20},{5,21},{6,22},{7,23},{8,24},{9,... | collective-permute-start | bytes 442376 | tf_op jit(solution)/shard_map/ppermute | solution.py:36
  27.6 1.4 %collective-permute-start.5 = (bf16[576,128]{1,0:T(8,128)(2,1)S(1)}, bf16[576,128]{1,0:T(8,128)(2,1)S(1)}, u32[]{:S(2)}, u32[]{:S(2)}) collective-permute-start(bf16[576,128]{1,0:T(8,128)(2,1)S(1)} %collective-permute-done.4.rest_4_), channel_id=1, source_target_pairs={{0,16},{1,17},{2,18},{3,19},{4,20},{5,21},{6,22},{7,23},{8,24},{9,... | collective-permute-start | bytes 442376 | tf_op jit(solution)/shard_map/ppermute | solution.py:36
  27.8 1.5 %collective-permute-start.3 = (bf16[576,128]{1,0:T(8,128)(2,1)S(1)}, bf16[576,128]{1,0:T(8,128)(2,1)S(1)}, u32[]{:S(2)}, u32[]{:S(2)}) collective-permute-start(bf16[576,128]{1,0:T(8,128)(2,1)S(1)} %collective-permute-done.2.rest_2_), channel_id=1, source_target_pairs={{0,16},{1,17},{2,18},{3,19},{4,20},{5,21},{6,22},{7,23},{8,24},{9,... | collective-permute-start | bytes 442376 | tf_op jit(solution)/shard_map/ppermute | solution.py:36
  28.2 1.4 %collective-permute-start.11 = (bf16[576,128]{1,0:T(8,128)(2,1)S(1)}, bf16[576,128]{1,0:T(8,128)(2,1)S(1)}, u32[]{:S(2)}, u32[]{:S(2)}) collective-permute-start(bf16[576,128]{1,0:T(8,128)(2,1)S(1)} %collective-permute-done.9.rest_10_), channel_id=1, source_target_pairs={{0,16},{1,17},{2,18},{3,19},{4,20},{5,21},{6,22},{7,23},{8,24},{9,... | collective-permute-start | bytes 442376 | tf_op jit(solution)/shard_map/ppermute | solution.py:36
  29.5 3.2 %collective-permute-start.13 = (bf16[448,1024]{1,0:T(8,128)(2,1)S(1)}, bf16[448,1024]{1,0:T(8,128)(2,1)S(1)}, u32[]{:S(2)}, u32[]{:S(2)}) collective-permute-start(bf16[448,1024]{1,0:T(8,128)(2,1)S(1)} %collective-permute-done.rest_9_.rest_15_), channel_id=1, source_target_pairs={{0,16},{1,17},{2,18},{3,19},{4,20},{5,21},{6,22},{7,23},{8,24},{9,... | collective-permute-start | bytes 2752520 | tf_op jit(solution)/shard_map/ppermute | solution.py:36
  29.7 9.4 %collective-permute-start.14 = (bf16[448,1024]{1,0:T(8,128)(2,1)}, bf16[448,1024]{1,0:T(8,128)(2,1)S(1)}, u32[]{:S(2)}, u32[]{:S(2)}) collective-permute-start(bf16[448,1024]{1,0:T(8,128)(2,1)} %bitcast.24), channel_id=1, source_target_pairs={{0,16},{2,18},{4,20},{6,22},{8,24},{10,26},{12,28},{14,30},{17,1},... | collective-permute-start | bytes 2752520 | tf_op jit(solution)/shard_map/ppermute | solution.py:36
  32.0 10.5 %collective-permute-start.22 = (bf16[448,1024]{1,0:T(8,128)(2,1)}, bf16[448,1024]{1,0:T(8,128)(2,1)S(1)}, u32[]{:S(2)}, u32[]{:S(2)}) collective-permute-start(bf16[448,1024]{1,0:T(8,128)(2,1)} %bitcast.25), channel_id=1, source_target_pairs={{1,48},{3,50},{5,52},{7,54},{9,56},{11,58},{13,60},{15,62},{16,33}... | collective-permute-start | bytes 2752520 | tf_op jit(solution)/shard_map/ppermute | solution.py:36
  39.1 8.0 %collective-permute-start.18 = (bf16[128,1024]{1,0:T(8,128)(2,1)S(1)}, bf16[128,1024]{1,0:T(8,128)(2,1)S(1)}, u32[]{:S(2)}, u32[]{:S(2)}) collective-permute-start(bf16[128,1024]{1,0:T(8,128)(2,1)S(1)} %attend.1.rest_0_), channel_id=1, source_target_pairs={{0,1},{1,0},{2,3},{3,2},{4,5},{5,4},{6,7},{7,6},{8,9},{9,8},{10,11... | collective-permute-start | bytes 786440 | tf_op jit(solution)/shard_map/ppermute | solution.py:36
  40.5 9.2 %collective-permute-start.17 = (bf16[128,1024]{1,0:T(8,128)(2,1)S(1)}, bf16[128,1024]{1,0:T(8,128)(2,1)S(1)}, u32[]{:S(2)}, u32[]{:S(2)}) collective-permute-start(bf16[128,1024]{1,0:T(8,128)(2,1)S(1)} %attend.1.rest_0_), channel_id=1, source_target_pairs={{0,192},{1,193},{2,194},{3,195},{4,196},{5,197},{6,198},{7,199},{8... | collective-permute-start | bytes 786440 | tf_op jit(solution)/shard_map/ppermute | solution.py:36
  40.5 10.7 %collective-permute-start.16 = (bf16[128,1024]{1,0:T(8,128)(2,1)S(1)}, bf16[128,1024]{1,0:T(8,128)(2,1)S(1)}, u32[]{:S(2)}, u32[]{:S(2)}) collective-permute-start(bf16[128,1024]{1,0:T(8,128)(2,1)S(1)} %attend.1.rest_0_), channel_id=1, source_target_pairs={{0,128},{1,129},{2,130},{3,131},{4,132},{5,133},{6,134},{7,135},{8... | collective-permute-start | bytes 786440 | tf_op jit(solution)/shard_map/ppermute | solution.py:36
  40.5 16.0 %collective-permute-start.15 = (bf16[128,1024]{1,0:T(8,128)(2,1)S(1)}, bf16[128,1024]{1,0:T(8,128)(2,1)S(1)}, u32[]{:S(2)}, u32[]{:S(2)}) collective-permute-start(bf16[128,1024]{1,0:T(8,128)(2,1)S(1)} %attend.1.rest_0_), channel_id=1, source_target_pairs={{0,64},{1,65},{2,66},{3,67},{4,68},{5,69},{6,70},{7,71},{8,72},{9,... | collective-permute-start | bytes 786440 | tf_op jit(solution)/shard_map/ppermute | solution.py:36
  56.5 12.4 %collective-permute-start.23 = (bf16[448,1024]{1,0:T(8,128)(2,1)S(1)}, bf16[448,1024]{1,0:T(8,128)(2,1)S(1)}, u32[]{:S(2)}, u32[]{:S(2)}) collective-permute-start(bf16[448,1024]{1,0:T(8,128)(2,1)S(1)} %collective-permute-done.22.rest_14_), channel_id=1, source_target_pairs={{1,17},{3,19},{5,21},{7,23},{9,25},{11,27},{13,29},{15,31},{16,0},... | collective-permute-start | bytes 2752520 | tf_op jit(solution)/shard_map/ppermute | solution.py:36
  58.0 9.0 %collective-permute-start.21 = (bf16[128,1024]{1,0:T(8,128)(2,1)S(1)}, bf16[128,1024]{1,0:T(8,128)(2,1)S(1)}, u32[]{:S(2)}, u32[]{:S(2)}) collective-permute-start(bf16[128,1024]{1,0:T(8,128)(2,1)S(1)} %collective-permute-done.18.rest_4_), channel_id=1, source_target_pairs={{0,192},{1,193},{2,194},{3,195},{4,196},{5,197},{6,198},{7,199},{8... | collective-permute-start | bytes 786440 | tf_op jit(solution)/shard_map/ppermute | solution.py:36
  58.9 9.1 %collective-permute-start.19 = (bf16[128,1024]{1,0:T(8,128)(2,1)S(1)}, bf16[128,1024]{1,0:T(8,128)(2,1)S(1)}, u32[]{:S(2)}, u32[]{:S(2)}) collective-permute-start(bf16[128,1024]{1,0:T(8,128)(2,1)S(1)} %collective-permute-done.18.rest_4_), channel_id=1, source_target_pairs={{0,64},{1,65},{2,66},{3,67},{4,68},{5,69},{6,70},{7,71},{8,72},{9,... | collective-permute-start | bytes 786440 | tf_op jit(solution)/shard_map/ppermute | solution.py:36
  60.1 8.8 %collective-permute-start.20 = (bf16[128,1024]{1,0:T(8,128)(2,1)S(1)}, bf16[128,1024]{1,0:T(8,128)(2,1)S(1)}, u32[]{:S(2)}, u32[]{:S(2)}) collective-permute-start(bf16[128,1024]{1,0:T(8,128)(2,1)S(1)} %collective-permute-done.16.rest_2_), channel_id=1, source_target_pairs={{0,1},{1,0},{2,3},{3,2},{4,5},{5,4},{6,7},{7,6},{8,9},{9,8},{10,11... | collective-permute-start | bytes 786440 | tf_op jit(solution)/shard_map/ppermute | solution.py:36
  71.9 14.6 %collective-permute-start.24 = (bf16[2,448,128]{2,1,0:T(8,128)(2,1)S(1)}, bf16[2,448,128]{2,1,0:T(8,128)(2,1)S(1)}, u32[]{:S(2)}, u32[]{:S(2)}) collective-permute-start(bf16[2,448,128]{2,1,0:T(8,128)(2,1)S(1)} %get-tuple-element.35), channel_id=1, source_target_pairs={{0,2},{1,3},{2,4},{3,5},{4,6},{5,7},{6,8},{7,9},{8,10},{9,11},{10,... | collective-permute-start | bytes 688136 | tf_op jit(solution)/shard_map/ppermute | solution.py:36
  73.9 12.6 %collective-permute-start.26 = (bf16[224,128]{1,0:T(8,128)(2,1)S(1)}, bf16[224,128]{1,0:T(8,128)(2,1)S(1)}, u32[]{:S(2)}, u32[]{:S(2)}) collective-permute-start(bf16[224,128]{1,0:T(8,128)(2,1)S(1)} %get-tuple-element.40), channel_id=1, source_target_pairs={{0,4},{1,5},{2,6},{3,7},{4,8},{5,9},{6,10},{7,11},{8,12},{9,13},{1... | collective-permute-start | bytes 172040 | tf_op jit(solution)/shard_map/ppermute | solution.py:36
  77.1 11.8 %collective-permute-start.25 = (bf16[2,448,128]{2,1,0:T(8,128)(2,1)S(1)}, bf16[2,448,128]{2,1,0:T(8,128)(2,1)S(1)}, u32[]{:S(2)}, u32[]{:S(2)}) collective-permute-start(bf16[2,448,128]{2,1,0:T(8,128)(2,1)S(1)} %get-tuple-element.36), channel_id=1, source_target_pairs={{0,14},{1,15},{2,0},{3,1},{4,2},{5,3},{6,4},{7,5},{8,6},{9,7},{10,... | collective-permute-start | bytes 688136 | tf_op jit(solution)/shard_map/ppermute | solution.py:36
  78.5 10.5 %collective-permute-start.28 = (bf16[224,128]{1,0:T(8,128)(2,1)S(1)}, bf16[224,128]{1,0:T(8,128)(2,1)S(1)}, u32[]{:S(2)}, u32[]{:S(2)}) collective-permute-start(bf16[224,128]{1,0:T(8,128)(2,1)S(1)} %get-tuple-element.42), channel_id=1, source_target_pairs={{0,12},{1,13},{2,14},{3,15},{4,0},{5,1},{6,2},{7,3},{8,4},{9,5},{1... | collective-permute-start | bytes 172040 | tf_op jit(solution)/shard_map/ppermute | solution.py:36
  86.5 8.7 %collective-permute-start.27 = (bf16[448,128]{1,0:T(8,128)(2,1)S(1)}, bf16[448,128]{1,0:T(8,128)(2,1)S(1)}, u32[]{:S(2)}, u32[]{:S(2)}) collective-permute-start(bf16[448,128]{1,0:T(8,128)(2,1)S(1)} %fusion.3), channel_id=1, source_target_pairs={{0,4},{1,5},{2,6},{3,7},{4,8},{5,9},{6,10},{7,11},{8,12},{9,13},{1... | collective-permute-start | bytes 344072 | tf_op jit(solution)/shard_map/ppermute | solution.py:36
  89.0 7.0 %collective-permute-start.29 = (bf16[448,128]{1,0:T(8,128)(2,1)S(1)}, bf16[448,128]{1,0:T(8,128)(2,1)S(1)}, u32[]{:S(2)}, u32[]{:S(2)}) collective-permute-start(bf16[448,128]{1,0:T(8,128)(2,1)S(1)} %fusion.1), channel_id=1, source_target_pairs={{0,12},{1,13},{2,14},{3,15},{4,0},{5,1},{6,2},{7,3},{8,4},{9,5},{1... | collective-permute-start | bytes 344072 | tf_op jit(solution)/shard_map/ppermute | solution.py:36
  96.1 13.0 %collective-permute-start.30 = (bf16[448,128]{1,0:T(8,128)(2,1)S(1)}, bf16[448,128]{1,0:T(8,128)(2,1)S(1)}, u32[]{:S(2)}, u32[]{:S(2)}) collective-permute-start(bf16[448,128]{1,0:T(8,128)(2,1)S(1)} %fusion.6), channel_id=1, source_target_pairs={{0,0},{1,1},{2,2},{3,3},{4,64},{5,65},{6,66},{7,67},{8,128},{9,129... | collective-permute-start | bytes 344072 | tf_op jit(solution)/shard_map/ppermute | solution.py:36

commit v4 on v3

--- a/solution.py
+++ b/solution.py
@@ -249,10 +249,6 @@
             return (3, 0, 0, tz, 1 - txl)
         return None
 
-    got = [mine, send(mine, from_y(0, True))]
-    for step in (1, 2):
-        got.extend([send(mine, from_y(step, False)), send(mine, from_y(step, True))])
-    far = send(mine, farthest)
     qc, qr = pl.pallas_call(
         absorb_kernel,
         out_shape=(
@@ -265,10 +261,14 @@
         name="absorb",
     )(queries, w_uk)
 
+    got = [mine, send(after(mine, (qc, qr)), from_y(0, True))]
+    for step in (1, 2):
+        got.extend([send(mine, from_y(step, False)), send(mine, from_y(step, True))])
+    far = send(mine, farthest)
     blocks = []
     for block in got[:4]:
         blocks.extend([block, send(block, other_core)])
-    for block in after(got[4:], (qc, qr)):
+    for block in got[4:]:
         blocks.extend([block, send(block, other_core)])
     blocks.append(far)
     units = len(got) + 1

time: 111 us -> 109 us (0.982)
  starting transfers between devices: 50.9 us -> 48 us
    ppermute x31, starting transfers between devices: 50.9 us -> 48 us  [send(): return lax.ppermute(value, AXES, pairs)]
  transfers between devices with their start and end apart: 31 -> 31, of which waited for: 16 -> 15; matrix products, arithmetic and copies ran while one was open for 0% -> 0% of each run, Pallas kernels for 6% -> 7%
where the time goes in v4:
time: 109 us; the launch traced here: 108 us
  starting transfers between devices  48 us (44%)
  waiting for transfers between devices  45.3 us (42%)
  Pallas kernels  10.8 us (10%)
  local copies, waits for them, and re-layouts  3.31 us (3%)
    ppermute x31, starting transfers between devices, send(): return lax.ppermute(value, AXES, pairs)  48 us
    ppermute x31, waiting for transfers between devices, send(): return lax.ppermute(value, AXES, pairs)  45.3 us
    pallas_call x1, Pallas kernels, body(): pl.pallas_call(attend_kernel, out_shape=jax.ShapeDtypeStruct((rows, heads...  7.37 us
    unnamed x13, local copies, waits for them, and re-layouts  3.31 us
    pallas_call x1, Pallas kernels, body(): pl.pallas_call(project_kernel, out_shape=[result(width, rows), result(2,...  3 us
  transfers between devices with their start and end apart: 31, of which 15 were waited for; matrix products, arithmetic and copies ran while one was open for 0% of the time, Pallas kernels for 7%

profile of v4, /device:TPU:16, one launch (start us, length us, event | category | flops | bytes accessed | tf_op | source)
XLA Modules:
  0.0 107.7 jit_solution(5459932555200821203)
XLA Ops:
  0.0 2.5 %collective-permute-start = (bf16[448,1024]{1,0:T(8,128)(2,1)}, bf16[448,1024]{1,0:T(8,128)(2,1)S(1)}, u32[]{:S(2)}, u32[]{:S(2)}) collective-permute-start(bf16[448,1024]{1,0:T(8,128)(2,1)} %bitcast.23), channel_id=1, source_target_pairs={{0,48},{1,0},{2,50},{3,2},{4,52},{5,4},{6,54},{7,6},{8,56},{9,8},{... | collective-permute-start | bytes 2752520 | tf_op jit(solution)/shard_map/ppermute | solution.py:36
  2.5 0.7 collective-permute-start.12
  3.1 1.3 %collective-permute-start.10 = (bf16[576,128]{1,0:T(8,128)(2,1)}, bf16[576,128]{1,0:T(8,128)(2,1)S(1)}, u32[]{:S(2)}, u32[]{:S(2)}) collective-permute-start(bf16[576,128]{1,0:T(8,128)(2,1)} %bitcast.28), channel_id=1, source_target_pairs={{0,161},{1,160},{2,163},{3,162},{4,165},{5,164},{6,167},{7,166},{8... | collective-permute-start | bytes 442376 | tf_op jit(solution)/shard_map/ppermute | solution.py:36
  4.4 1.3 %collective-permute-start.8 = (bf16[576,128]{1,0:T(8,128)(2,1)}, bf16[576,128]{1,0:T(8,128)(2,1)S(1)}, u32[]{:S(2)}, u32[]{:S(2)}) collective-permute-start(bf16[576,128]{1,0:T(8,128)(2,1)} %bitcast.29), channel_id=1, source_target_pairs={{0,128},{1,129},{2,130},{3,131},{4,132},{5,133},{6,134},{7,135},{8... | collective-permute-start | bytes 442376 | tf_op jit(solution)/shard_map/ppermute | solution.py:36
  5.7 3.8 %collective-permute-start.6 = (bf16[576,128]{1,0:T(8,128)(2,1)}, bf16[576,128]{1,0:T(8,128)(2,1)S(1)}, u32[]{:S(2)}, u32[]{:S(2)}) collective-permute-start(bf16[576,128]{1,0:T(8,128)(2,1)} %bitcast.30), channel_id=1, source_target_pairs={{0,97},{1,96},{2,99},{3,98},{4,101},{5,100},{6,103},{7,102},{8,105... | collective-permute-start | bytes 442376 | tf_op jit(solution)/shard_map/ppermute | solution.py:36
  9.5 1.2 %copy-done.1 = bf16[8,512,128]{2,1,0:T(8,128)(2,1)S(1)} copy-done((bf16[8,512,128]{2,1,0:T(8,128)(2,1)S(1)}, bf16[8,512,128]{2,1,0:T(8,128)(2,1)}, u32[]{:S(2)}) %copy-start.1) | copy-done | bytes 1048600
  10.7 1.0 copy-done.3
  11.7 0.4 absorb.1
  12.2 0.4 copy-done.4
  12.6 6.6 %collective-permute-start.4 = (bf16[576,128]{1,0:T(8,128)(2,1)S(1)}, bf16[576,128]{1,0:T(8,128)(2,1)S(1)}, u32[]{:S(2)}, u32[]{:S(2)}) collective-permute-start(bf16[576,128]{1,0:T(8,128)(2,1)S(1)} %bitcast.31), channel_id=1, source_target_pairs={{0,64},{1,65},{2,66},{3,67},{4,68},{5,69},{6,70},{7,71},{8,72},{9,... | collective-permute-start | bytes 442376 | tf_op jit(solution)/shard_map/ppermute | solution.py:36
  19.2 2.7 %collective-permute-start.1 = (bf16[576,128]{1,0:T(8,128)(2,1)S(1)}, bf16[576,128]{1,0:T(8,128)(2,1)S(1)}, u32[]{:S(2)}, u32[]{:S(2)}) collective-permute-start(bf16[576,128]{1,0:T(8,128)(2,1)S(1)} %bitcast.32), channel_id=1, source_target_pairs={{0,16},{1,17},{2,18},{3,19},{4,20},{5,21},{6,22},{7,23},{8,24},{9,... | collective-permute-start | bytes 442376 | tf_op jit(solution)/shard_map/ppermute | solution.py:36
  21.9 1.2 %collective-permute-done.6.rest_6_ = bf16[576,128]{1,0:T(8,128)(2,1)S(1)} collective-permute-done((bf16[576,128]{1,0:T(8,128)(2,1)}, bf16[576,128]{1,0:T(8,128)(2,1)S(1)}, u32[]{:S(2)}, u32[]{:S(2)}) %collective-permute-start.6) | collective-permute-done | bytes 147488 | tf_op jit(solution)/shard_map/ppermute | solution.py:36
  23.1 1.4 %collective-permute-done.4.rest_4_ = bf16[576,128]{1,0:T(8,128)(2,1)S(1)} collective-permute-done((bf16[576,128]{1,0:T(8,128)(2,1)S(1)}, bf16[576,128]{1,0:T(8,128)(2,1)S(1)}, u32[]{:S(2)}, u32[]{:S(2)}) %collective-permute-start.4) | collective-permute-done | bytes 147488 | tf_op jit(solution)/shard_map/ppermute | solution.py:36
  24.6 0.4 collective-permute-start.7
  25.0 3.8 %collective-permute-done.2.rest_2_ = bf16[576,128]{1,0:T(8,128)(2,1)S(1)} collective-permute-done((bf16[576,128]{1,0:T(8,128)(2,1)S(1)}, bf16[576,128]{1,0:T(8,128)(2,1)S(1)}, u32[]{:S(2)}, u32[]{:S(2)}) %collective-permute-start.2) | collective-permute-done | bytes 147488 | tf_op jit(solution)/shard_map/ppermute | solution.py:36
  28.9 0.5 collective-permute-start.3
  29.4 0.9 collective-permute-done.5.rest_5_
  30.2 0.2 collective-permute-done.3.rest_3_
  30.4 0.3 collective-permute-start.13
  30.8 2.2 %collective-permute-start.14 = (bf16[448,1024]{1,0:T(8,128)(2,1)}, bf16[448,1024]{1,0:T(8,128)(2,1)S(1)}, u32[]{:S(2)}, u32[]{:S(2)}) collective-permute-start(bf16[448,1024]{1,0:T(8,128)(2,1)} %bitcast.24), channel_id=1, source_target_pairs={{0,16},{2,18},{4,20},{6,22},{8,24},{10,26},{12,28},{14,30},{17,1},... | collective-permute-start | bytes 2752520 | tf_op jit(solution)/shard_map/ppermute | solution.py:36
  32.9 0.7 collective-permute-start.22
  33.7 7.4 %attend.1.rest_0_ = bf16[128,1024]{1,0:T(8,128)(2,1)S(1)} custom-call(s32[8]{0:T(128)S(1)} %copy-done.5, bf16[1024,512]{1,0:T(8,128)(2,1)S(1)} %get-tuple-element.27.qc_ref, bf16[1024,64]{1,0:T(8,128)(2,1)S(1)} %get-tuple-element.24.qr_ref, bf16[8,512,128]{2,1,0:T(8,128)(2,1)S(1)} %copy-done, bf16[576,128]{1,0:T(8,128)(2,1)S(1)} %bitcast.34, ...), custom_call_target="tpu_custom_call" | custom-call | tf_op jit(solution)/shard_map/attend/pallas_call | solution.py:301
  41.1 0.1 collective-permute-start.18
  41.2 0.1 collective-permute-start.17
  41.3 0.1 collective-permute-start.16
  41.4 1.9 %collective-permute-start.15 = (bf16[128,1024]{1,0:T(8,128)(2,1)S(1)}, bf16[128,1024]{1,0:T(8,128)(2,1)S(1)}, u32[]{:S(2)}, u32[]{:S(2)}) collective-permute-start(bf16[128,1024]{1,0:T(8,128)(2,1)S(1)} %attend.1.rest_0_), channel_id=1, source_target_pairs={{0,64},{1,65},{2,66},{3,67},{4,68},{5,69},{6,70},{7,71},{8,72},{9,... | collective-permute-start | bytes 786440 | tf_op jit(solution)/shard_map/ppermute | solution.py:36
  43.3 4.2 %collective-permute-done.18.rest_4_ = bf16[128,1024]{1,0:T(8,128)(2,1)S(1)} collective-permute-done((bf16[128,1024]{1,0:T(8,128)(2,1)S(1)}, bf16[128,1024]{1,0:T(8,128)(2,1)S(1)}, u32[]{:S(2)}, u32[]{:S(2)}) %collective-permute-start.18) | collective-permute-done | bytes 262176 | tf_op jit(solution)/shard_map/ppermute | solution.py:36
  47.5 4.3 %collective-permute-done.17.rest_3_ = bf16[128,1024]{1,0:T(8,128)(2,1)S(1)} collective-permute-done((bf16[128,1024]{1,0:T(8,128)(2,1)S(1)}, bf16[128,1024]{1,0:T(8,128)(2,1)S(1)}, u32[]{:S(2)}, u32[]{:S(2)}) %collective-permute-start.17) | collective-permute-done | bytes 262176 | tf_op jit(solution)/shard_map/ppermute | solution.py:36
  51.9 0.2 collective-permute-done.16.rest_2_
  52.1 2.0 %collective-permute-done.15.rest_1_ = bf16[128,1024]{1,0:T(8,128)(2,1)S(1)} collective-permute-done((bf16[128,1024]{1,0:T(8,128)(2,1)S(1)}, bf16[128,1024]{1,0:T(8,128)(2,1)S(1)}, u32[]{:S(2)}, u32[]{:S(2)}) %collective-permute-start.15) | collective-permute-done | bytes 262176 | tf_op jit(solution)/shard_map/ppermute | solution.py:36
  54.1 1.5 %collective-permute-start.23 = (bf16[448,1024]{1,0:T(8,128)(2,1)S(1)}, bf16[448,1024]{1,0:T(8,128)(2,1)S(1)}, u32[]{:S(2)}, u32[]{:S(2)}) collective-permute-start(bf16[448,1024]{1,0:T(8,128)(2,1)S(1)} %collective-permute-done.22.rest_14_), channel_id=1, source_target_pairs={{1,17},{3,19},{5,21},{7,23},{9,25},{11,27},{13,29},{15,31},{16,0},... | collective-permute-start | bytes 2752520 | tf_op jit(solution)/shard_map/ppermute | solution.py:36
  55.5 2.2 %collective-permute-start.21 = (bf16[128,1024]{1,0:T(8,128)(2,1)S(1)}, bf16[128,1024]{1,0:T(8,128)(2,1)S(1)}, u32[]{:S(2)}, u32[]{:S(2)}) collective-permute-start(bf16[128,1024]{1,0:T(8,128)(2,1)S(1)} %collective-permute-done.18.rest_4_), channel_id=1, source_target_pairs={{0,192},{1,193},{2,194},{3,195},{4,196},{5,197},{6,198},{7,199},{8... | collective-permute-start | bytes 786440 | tf_op jit(solution)/shard_map/ppermute | solution.py:36
  57.7 1.7 %collective-permute-start.20 = (bf16[128,1024]{1,0:T(8,128)(2,1)S(1)}, bf16[128,1024]{1,0:T(8,128)(2,1)S(1)}, u32[]{:S(2)}, u32[]{:S(2)}) collective-permute-start(bf16[128,1024]{1,0:T(8,128)(2,1)S(1)} %collective-permute-done.16.rest_2_), channel_id=1, source_target_pairs={{0,1},{1,0},{2,3},{3,2},{4,5},{5,4},{6,7},{7,6},{8,9},{9,8},{10,11... | collective-permute-start | bytes 786440 | tf_op jit(solution)/shard_map/ppermute | solution.py:36
  59.4 5.1 %collective-permute-done.21.rest_7_ = bf16[128,1024]{1,0:T(8,128)(2,1)S(1)} collective-permute-done((bf16[128,1024]{1,0:T(8,128)(2,1)S(1)}, bf16[128,1024]{1,0:T(8,128)(2,1)S(1)}, u32[]{:S(2)}, u32[]{:S(2)}) %collective-permute-start.21) | collective-permute-done | bytes 262176 | tf_op jit(solution)/shard_map/ppermute | solution.py:36
  64.6 2.2 %collective-permute-done.19.rest_5_ = bf16[128,1024]{1,0:T(8,128)(2,1)S(1)} collective-permute-done((bf16[128,1024]{1,0:T(8,128)(2,1)S(1)}, bf16[128,1024]{1,0:T(8,128)(2,1)S(1)}, u32[]{:S(2)}, u32[]{:S(2)}) %collective-permute-start.19) | collective-permute-done | bytes 262176 | tf_op jit(solution)/shard_map/ppermute | solution.py:36
  66.9 3.0 %project.1 = (bf16[448,128]{1,0:T(8,128)(2,1)S(1)}, bf16[2,448,128]{2,1,0:T(8,128)(2,1)S(1)}, bf16[2,448,128]{2,1,0:T(8,128)(2,1)S(1)}, bf16[224,128]{1,0:T(8,12...) custom-call(bf16[128,1024]{1,0:T(8,128)(2,1)S(1)} %attend.1.rest_0_, ...), custom_call_target="tpu_custom_call" | custom-call | tf_op jit(solution)/shard_map/project/pallas_call | solution.py:336
  69.9 2.0 %collective-permute-start.24 = (bf16[2,448,128]{2,1,0:T(8,128)(2,1)S(1)}, bf16[2,448,128]{2,1,0:T(8,128)(2,1)S(1)}, u32[]{:S(2)}, u32[]{:S(2)}) collective-permute-start(bf16[2,448,128]{2,1,0:T(8,128)(2,1)S(1)} %get-tuple-element.33), channel_id=1, source_target_pairs={{0,2},{1,3},{2,4},{3,5},{4,6},{5,7},{6,8},{7,9},{8,10},{9,11},{10,... | collective-permute-start | bytes 688136 | tf_op jit(solution)/shard_map/ppermute | solution.py:36
  71.9 3.3 %collective-permute-start.26 = (bf16[224,128]{1,0:T(8,128)(2,1)S(1)}, bf16[224,128]{1,0:T(8,128)(2,1)S(1)}, u32[]{:S(2)}, u32[]{:S(2)}) collective-permute-start(bf16[224,128]{1,0:T(8,128)(2,1)S(1)} %get-tuple-element.38), channel_id=1, source_target_pairs={{0,4},{1,5},{2,6},{3,7},{4,8},{5,9},{6,10},{7,11},{8,12},{9,13},{1... | collective-permute-start | bytes 172040 | tf_op jit(solution)/shard_map/ppermute | solution.py:36
  75.1 1.3 %collective-permute-start.25 = (bf16[2,448,128]{2,1,0:T(8,128)(2,1)S(1)}, bf16[2,448,128]{2,1,0:T(8,128)(2,1)S(1)}, u32[]{:S(2)}, u32[]{:S(2)}) collective-permute-start(bf16[2,448,128]{2,1,0:T(8,128)(2,1)S(1)} %get-tuple-element.34), channel_id=1, source_target_pairs={{0,14},{1,15},{2,0},{3,1},{4,2},{5,3},{6,4},{7,5},{8,6},{9,7},{10,... | collective-permute-start | bytes 688136 | tf_op jit(solution)/shard_map/ppermute | solution.py:36
  76.4 2.4 %collective-permute-start.28 = (bf16[224,128]{1,0:T(8,128)(2,1)S(1)}, bf16[224,128]{1,0:T(8,128)(2,1)S(1)}, u32[]{:S(2)}, u32[]{:S(2)}) collective-permute-start(bf16[224,128]{1,0:T(8,128)(2,1)S(1)} %get-tuple-element.40), channel_id=1, source_target_pairs={{0,12},{1,13},{2,14},{3,15},{4,0},{5,1},{6,2},{7,3},{8,4},{9,5},{1... | collective-permute-start | bytes 172040 | tf_op jit(solution)/shard_map/ppermute | solution.py:36
  78.8 5.8 %collective-permute-done.26 = bf16[224,128]{1,0:T(8,128)(2,1)S(1)} collective-permute-done((bf16[224,128]{1,0:T(8,128)(2,1)S(1)}, bf16[224,128]{1,0:T(8,128)(2,1)S(1)}, u32[]{:S(2)}, u32[]{:S(2)}) %collective-permute-start.26) | collective-permute-done | bytes 57376 | tf_op jit(solution)/shard_map/ppermute | solution.py:36
  84.7 0.1 collective-permute-start.27
  84.8 2.4 %collective-permute-done.28 = bf16[224,128]{1,0:T(8,128)(2,1)S(1)} collective-permute-done((bf16[224,128]{1,0:T(8,128)(2,1)S(1)}, bf16[224,128]{1,0:T(8,128)(2,1)S(1)}, u32[]{:S(2)}, u32[]{:S(2)}) %collective-permute-start.28) | collective-permute-done | bytes 57376 | tf_op jit(solution)/shard_map/ppermute | solution.py:36
  87.2 1.8 %collective-permute-start.29 = (bf16[448,128]{1,0:T(8,128)(2,1)S(1)}, bf16[448,128]{1,0:T(8,128)(2,1)S(1)}, u32[]{:S(2)}, u32[]{:S(2)}) collective-permute-start(bf16[448,128]{1,0:T(8,128)(2,1)S(1)} %fusion.1), channel_id=1, source_target_pairs={{0,12},{1,13},{2,14},{3,15},{4,0},{5,1},{6,2},{7,3},{8,4},{9,5},{1... | collective-permute-start | bytes 344072 | tf_op jit(solution)/shard_map/ppermute | solution.py:36
  89.0 4.4 %collective-permute-done.27 = bf16[448,128]{1,0:T(8,128)(2,1)S(1)} collective-permute-done((bf16[448,128]{1,0:T(8,128)(2,1)S(1)}, bf16[448,128]{1,0:T(8,128)(2,1)S(1)}, u32[]{:S(2)}, u32[]{:S(2)}) %collective-permute-start.27) | collective-permute-done | bytes 114720 | tf_op jit(solution)/shard_map/ppermute | solution.py:36
  93.5 6.6 %collective-permute-start.30 = (bf16[448,128]{1,0:T(8,128)(2,1)S(1)}, bf16[448,128]{1,0:T(8,128)(2,1)S(1)}, u32[]{:S(2)}, u32[]{:S(2)}) collective-permute-start(bf16[448,128]{1,0:T(8,128)(2,1)S(1)} %fusion.6), channel_id=1, source_target_pairs={{0,0},{1,1},{2,2},{3,3},{4,64},{5,65},{6,66},{7,67},{8,128},{9,129... | collective-permute-start | bytes 344072 | tf_op jit(solution)/shard_map/ppermute | solution.py:36
  100.1 7.0 %collective-permute-done.30 = bf16[448,128]{1,0:T(8,128)(2,1)S(1)} collective-permute-done((bf16[448,128]{1,0:T(8,128)(2,1)S(1)}, bf16[448,128]{1,0:T(8,128)(2,1)S(1)}, u32[]{:S(2)}, u32[]{:S(2)}) %collective-permute-start.30) | collective-permute-done | bytes 114720 | tf_op jit(solution)/shard_map/ppermute | solution.py:36
  107.1 0.6 copy.8
  (33 shorter events, 0.3 us)
Async XLA Ops:
  0.0 33.7 %copy-start = (bf16[8,512,128]{2,1,0:T(8,128)(2,1)S(1)}, bf16[8,512,128]{2,1,0:T(8,128)(2,1)}, u32[]{:S(2)}) copy-start(bf16[8,512,128]{2,1,0:T(8,128)(2,1)} %w_uv_any.1) | copy-start | bytes 3145732
  0.0 30.4 %collective-permute-start = (bf16[448,1024]{1,0:T(8,128)(2,1)}, bf16[448,1024]{1,0:T(8,128)(2,1)S(1)}, u32[]{:S(2)}, u32[]{:S(2)}) collective-permute-start(bf16[448,1024]{1,0:T(8,128)(2,1)} %bitcast.23), channel_id=1, source_target_pairs={{0,48},{1,0},{2,50},{3,2},{4,52},{5,4},{6,54},{7,6},{8,56},{9,8},{... | collective-permute-start | bytes 2752520 | tf_op jit(solution)/shard_map/ppermute | solution.py:36
  2.5 9.7 %collective-permute-start.12 = (bf16[576,128]{1,0:T(8,128)(2,1)}, bf16[576,128]{1,0:T(8,128)(2,1)S(1)}, u32[]{:S(2)}, u32[]{:S(2)}) collective-permute-start(bf16[576,128]{1,0:T(8,128)(2,1)} %bitcast.27), channel_id=1, source_target_pairs={{48,193},{49,192},{50,195},{51,194},{52,197},{53,196},{54,199},{55... | collective-permute-start | bytes 442376 | tf_op jit(solution)/shard_map/ppermute | solution.py:36
  3.1 16.1 %collective-permute-start.10 = (bf16[576,128]{1,0:T(8,128)(2,1)}, bf16[576,128]{1,0:T(8,128)(2,1)S(1)}, u32[]{:S(2)}, u32[]{:S(2)}) collective-permute-start(bf16[576,128]{1,0:T(8,128)(2,1)} %bitcast.28), channel_id=1, source_target_pairs={{0,161},{1,160},{2,163},{3,162},{4,165},{5,164},{6,167},{7,166},{8... | collective-permute-start | bytes 442376 | tf_op jit(solution)/shard_map/ppermute | solution.py:36
  4.4 17.5 %collective-permute-start.8 = (bf16[576,128]{1,0:T(8,128)(2,1)}, bf16[576,128]{1,0:T(8,128)(2,1)S(1)}, u32[]{:S(2)}, u32[]{:S(2)}) collective-permute-start(bf16[576,128]{1,0:T(8,128)(2,1)} %bitcast.29), channel_id=1, source_target_pairs={{0,128},{1,129},{2,130},{3,131},{4,132},{5,133},{6,134},{7,135},{8... | collective-permute-start | bytes 442376 | tf_op jit(solution)/shard_map/ppermute | solution.py:36
  5.7 17.3 %collective-permute-start.6 = (bf16[576,128]{1,0:T(8,128)(2,1)}, bf16[576,128]{1,0:T(8,128)(2,1)S(1)}, u32[]{:S(2)}, u32[]{:S(2)}) collective-permute-start(bf16[576,128]{1,0:T(8,128)(2,1)} %bitcast.30), channel_id=1, source_target_pairs={{0,97},{1,96},{2,99},{3,98},{4,101},{5,100},{6,103},{7,102},{8,105... | collective-permute-start | bytes 442376 | tf_op jit(solution)/shard_map/ppermute | solution.py:36
  9.5 1.2 %copy-start.1 = (bf16[8,512,128]{2,1,0:T(8,128)(2,1)S(1)}, bf16[8,512,128]{2,1,0:T(8,128)(2,1)}, u32[]{:S(2)}) copy-start(bf16[8,512,128]{2,1,0:T(8,128)(2,1)} %w_uk_ref.1) | copy-start | bytes 3145732
  10.7 1.0 copy-start.3
  11.7 0.9 copy-start.4
  12.2 21.5 %copy-start.5 = (s32[8]{0:T(128)S(1)}, s32[8]{0:T(128)}, u32[]{:S(2)}) copy-start(s32[8]{0:T(128)} %lengths_ref.1) | copy-start | bytes 100
  12.2 54.7 %copy-start.2 = (bf16[1024,448]{0,1:T(8,128)(2,1)S(1)}, bf16[1024,448]{0,1:T(8,128)(2,1)}, u32[]{:S(2)}) copy-start(bf16[1024,448]{0,1:T(8,128)(2,1)} %param.10) | copy-start | bytes 2752516
  12.6 11.9 %collective-permute-start.4 = (bf16[576,128]{1,0:T(8,128)(2,1)S(1)}, bf16[576,128]{1,0:T(8,128)(2,1)S(1)}, u32[]{:S(2)}, u32[]{:S(2)}) collective-permute-start(bf16[576,128]{1,0:T(8,128)(2,1)S(1)} %bitcast.31), channel_id=1, source_target_pairs={{0,64},{1,65},{2,66},{3,67},{4,68},{5,69},{6,70},{7,71},{8,72},{9,... | collective-permute-start | bytes 442376 | tf_op jit(solution)/shard_map/ppermute | solution.py:36
  19.2 5.4 %collective-permute-start.1 = (bf16[576,128]{1,0:T(8,128)(2,1)S(1)}, bf16[576,128]{1,0:T(8,128)(2,1)S(1)}, u32[]{:S(2)}, u32[]{:S(2)}) collective-permute-start(bf16[576,128]{1,0:T(8,128)(2,1)S(1)} %bitcast.32), channel_id=1, source_target_pairs={{0,16},{1,17},{2,18},{3,19},{4,20},{5,21},{6,22},{7,23},{8,24},{9,... | collective-permute-start | bytes 442376 | tf_op jit(solution)/shard_map/ppermute | solution.py:36
  21.9 7.0 %collective-permute-start.2 = (bf16[576,128]{1,0:T(8,128)(2,1)S(1)}, bf16[576,128]{1,0:T(8,128)(2,1)S(1)}, u32[]{:S(2)}, u32[]{:S(2)}) collective-permute-start(bf16[576,128]{1,0:T(8,128)(2,1)S(1)} %bitcast.33), channel_id=1, source_target_pairs={{0,33},{1,32},{2,35},{3,34},{4,37},{5,36},{6,39},{7,38},{8,41},{9,... | collective-permute-start | bytes 442376 | tf_op jit(solution)/shard_map/ppermute | solution.py:36
  23.1 5.8 %collective-permute-start.11 = (bf16[576,128]{1,0:T(8,128)(2,1)S(1)}, bf16[576,128]{1,0:T(8,128)(2,1)S(1)}, u32[]{:S(2)}, u32[]{:S(2)}) collective-permute-start(bf16[576,128]{1,0:T(8,128)(2,1)S(1)} %collective-permute-done.10.rest_10_), channel_id=1, source_target_pairs={{0,16},{1,17},{2,18},{3,19},{4,20},{5,21},{6,22},{7,23},{8,24},{9,... | collective-permute-start | bytes 442376 | tf_op jit(solution)/shard_map/ppermute | solution.py:36
  24.5 4.8 %collective-permute-start.9 = (bf16[576,128]{1,0:T(8,128)(2,1)S(1)}, bf16[576,128]{1,0:T(8,128)(2,1)S(1)}, u32[]{:S(2)}, u32[]{:S(2)}) collective-permute-start(bf16[576,128]{1,0:T(8,128)(2,1)S(1)} %collective-permute-done.8.rest_8_), channel_id=1, source_target_pairs={{0,16},{1,17},{2,18},{3,19},{4,20},{5,21},{6,22},{7,23},{8,24},{9,... | collective-permute-start | bytes 442376 | tf_op jit(solution)/shard_map/ppermute | solution.py:36
  24.6 4.8 %collective-permute-start.7 = (bf16[576,128]{1,0:T(8,128)(2,1)S(1)}, bf16[576,128]{1,0:T(8,128)(2,1)S(1)}, u32[]{:S(2)}, u32[]{:S(2)}) collective-permute-start(bf16[576,128]{1,0:T(8,128)(2,1)S(1)} %collective-permute-done.6.rest_6_), channel_id=1, source_target_pairs={{0,16},{1,17},{2,18},{3,19},{4,20},{5,21},{6,22},{7,23},{8,24},{9,... | collective-permute-start | bytes 442376 | tf_op jit(solution)/shard_map/ppermute | solution.py:36
  28.9 1.4 %collective-permute-start.5 = (bf16[576,128]{1,0:T(8,128)(2,1)S(1)}, bf16[576,128]{1,0:T(8,128)(2,1)S(1)}, u32[]{:S(2)}, u32[]{:S(2)}) collective-permute-start(bf16[576,128]{1,0:T(8,128)(2,1)S(1)} %collective-permute-done.4.rest_4_), channel_id=1, source_target_pairs={{0,16},{1,17},{2,18},{3,19},{4,20},{5,21},{6,22},{7,23},{8,24},{9,... | collective-permute-start | bytes 442376 | tf_op jit(solution)/shard_map/ppermute | solution.py:36
  28.9 1.6 %collective-permute-start.3 = (bf16[576,128]{1,0:T(8,128)(2,1)S(1)}, bf16[576,128]{1,0:T(8,128)(2,1)S(1)}, u32[]{:S(2)}, u32[]{:S(2)}) collective-permute-start(bf16[576,128]{1,0:T(8,128)(2,1)S(1)} %collective-permute-done.2.rest_2_), channel_id=1, source_target_pairs={{0,16},{1,17},{2,18},{3,19},{4,20},{5,21},{6,22},{7,23},{8,24},{9,... | collective-permute-start | bytes 442376 | tf_op jit(solution)/shard_map/ppermute | solution.py:36
  30.4 3.2 %collective-permute-start.13 = (bf16[448,1024]{1,0:T(8,128)(2,1)S(1)}, bf16[448,1024]{1,0:T(8,128)(2,1)S(1)}, u32[]{:S(2)}, u32[]{:S(2)}) collective-permute-start(bf16[448,1024]{1,0:T(8,128)(2,1)S(1)} %collective-permute-done.rest_9_.rest_15_), channel_id=1, source_target_pairs={{0,16},{1,17},{2,18},{3,19},{4,20},{5,21},{6,22},{7,23},{8,24},{9,... | collective-permute-start | bytes 2752520 | tf_op jit(solution)/shard_map/ppermute | solution.py:36
  30.8 10.3 %collective-permute-start.14 = (bf16[448,1024]{1,0:T(8,128)(2,1)}, bf16[448,1024]{1,0:T(8,128)(2,1)S(1)}, u32[]{:S(2)}, u32[]{:S(2)}) collective-permute-start(bf16[448,1024]{1,0:T(8,128)(2,1)} %bitcast.24), channel_id=1, source_target_pairs={{0,16},{2,18},{4,20},{6,22},{8,24},{10,26},{12,28},{14,30},{17,1},... | collective-permute-start | bytes 2752520 | tf_op jit(solution)/shard_map/ppermute | solution.py:36
  32.9 10.4 %collective-permute-start.22 = (bf16[448,1024]{1,0:T(8,128)(2,1)}, bf16[448,1024]{1,0:T(8,128)(2,1)S(1)}, u32[]{:S(2)}, u32[]{:S(2)}) collective-permute-start(bf16[448,1024]{1,0:T(8,128)(2,1)} %bitcast.25), channel_id=1, source_target_pairs={{1,48},{3,50},{5,52},{7,54},{9,56},{11,58},{13,60},{15,62},{16,33}... | collective-permute-start | bytes 2752520 | tf_op jit(solution)/shard_map/ppermute | solution.py:36
  41.1 6.5 %collective-permute-start.18 = (bf16[128,1024]{1,0:T(8,128)(2,1)S(1)}, bf16[128,1024]{1,0:T(8,128)(2,1)S(1)}, u32[]{:S(2)}, u32[]{:S(2)}) collective-permute-start(bf16[128,1024]{1,0:T(8,128)(2,1)S(1)} %attend.1.rest_0_), channel_id=1, source_target_pairs={{0,1},{1,0},{2,3},{3,2},{4,5},{5,4},{6,7},{7,6},{8,9},{9,8},{10,11... | collective-permute-start | bytes 786440 | tf_op jit(solution)/shard_map/ppermute | solution.py:36
  41.2 10.7 %collective-permute-start.17 = (bf16[128,1024]{1,0:T(8,128)(2,1)S(1)}, bf16[128,1024]{1,0:T(8,128)(2,1)S(1)}, u32[]{:S(2)}, u32[]{:S(2)}) collective-permute-start(bf16[128,1024]{1,0:T(8,128)(2,1)S(1)} %attend.1.rest_0_), channel_id=1, source_target_pairs={{0,192},{1,193},{2,194},{3,195},{4,196},{5,197},{6,198},{7,199},{8... | collective-permute-start | bytes 786440 | tf_op jit(solution)/shard_map/ppermute | solution.py:36
  41.3 10.8 %collective-permute-start.16 = (bf16[128,1024]{1,0:T(8,128)(2,1)S(1)}, bf16[128,1024]{1,0:T(8,128)(2,1)S(1)}, u32[]{:S(2)}, u32[]{:S(2)}) collective-permute-start(bf16[128,1024]{1,0:T(8,128)(2,1)S(1)} %attend.1.rest_0_), channel_id=1, source_target_pairs={{0,128},{1,129},{2,130},{3,131},{4,132},{5,133},{6,134},{7,135},{8... | collective-permute-start | bytes 786440 | tf_op jit(solution)/shard_map/ppermute | solution.py:36
  41.4 12.7 %collective-permute-start.15 = (bf16[128,1024]{1,0:T(8,128)(2,1)S(1)}, bf16[128,1024]{1,0:T(8,128)(2,1)S(1)}, u32[]{:S(2)}, u32[]{:S(2)}) collective-permute-start(bf16[128,1024]{1,0:T(8,128)(2,1)S(1)} %attend.1.rest_0_), channel_id=1, source_target_pairs={{0,64},{1,65},{2,66},{3,67},{4,68},{5,69},{6,70},{7,71},{8,72},{9,... | collective-permute-start | bytes 786440 | tf_op jit(solution)/shard_map/ppermute | solution.py:36
  54.1 12.8 %collective-permute-start.23 = (bf16[448,1024]{1,0:T(8,128)(2,1)S(1)}, bf16[448,1024]{1,0:T(8,128)(2,1)S(1)}, u32[]{:S(2)}, u32[]{:S(2)}) collective-permute-start(bf16[448,1024]{1,0:T(8,128)(2,1)S(1)} %collective-permute-done.22.rest_14_), channel_id=1, source_target_pairs={{1,17},{3,19},{5,21},{7,23},{9,25},{11,27},{13,29},{15,31},{16,0},... | collective-permute-start | bytes 2752520 | tf_op jit(solution)/shard_map/ppermute | solution.py:36
  55.5 9.0 %collective-permute-start.21 = (bf16[128,1024]{1,0:T(8,128)(2,1)S(1)}, bf16[128,1024]{1,0:T(8,128)(2,1)S(1)}, u32[]{:S(2)}, u32[]{:S(2)}) collective-permute-start(bf16[128,1024]{1,0:T(8,128)(2,1)S(1)} %collective-permute-done.18.rest_4_), channel_id=1, source_target_pairs={{0,192},{1,193},{2,194},{3,195},{4,196},{5,197},{6,198},{7,199},{8... | collective-permute-start | bytes 786440 | tf_op jit(solution)/shard_map/ppermute | solution.py:36
  57.7 9.1 %collective-permute-start.19 = (bf16[128,1024]{1,0:T(8,128)(2,1)S(1)}, bf16[128,1024]{1,0:T(8,128)(2,1)S(1)}, u32[]{:S(2)}, u32[]{:S(2)}) collective-permute-start(bf16[128,1024]{1,0:T(8,128)(2,1)S(1)} %collective-permute-done.18.rest_4_), channel_id=1, source_target_pairs={{0,64},{1,65},{2,66},{3,67},{4,68},{5,69},{6,70},{7,71},{8,72},{9,... | collective-permute-start | bytes 786440 | tf_op jit(solution)/shard_map/ppermute | solution.py:36
  57.7 9.1 %collective-permute-start.20 = (bf16[128,1024]{1,0:T(8,128)(2,1)S(1)}, bf16[128,1024]{1,0:T(8,128)(2,1)S(1)}, u32[]{:S(2)}, u32[]{:S(2)}) collective-permute-start(bf16[128,1024]{1,0:T(8,128)(2,1)S(1)} %collective-permute-done.16.rest_2_), channel_id=1, source_target_pairs={{0,1},{1,0},{2,3},{3,2},{4,5},{5,4},{6,7},{7,6},{8,9},{9,8},{10,11... | collective-permute-start | bytes 786440 | tf_op jit(solution)/shard_map/ppermute | solution.py:36
  69.9 14.8 %collective-permute-start.24 = (bf16[2,448,128]{2,1,0:T(8,128)(2,1)S(1)}, bf16[2,448,128]{2,1,0:T(8,128)(2,1)S(1)}, u32[]{:S(2)}, u32[]{:S(2)}) collective-permute-start(bf16[2,448,128]{2,1,0:T(8,128)(2,1)S(1)} %get-tuple-element.33), channel_id=1, source_target_pairs={{0,2},{1,3},{2,4},{3,5},{4,6},{5,7},{6,8},{7,9},{8,10},{9,11},{10,... | collective-permute-start | bytes 688136 | tf_op jit(solution)/shard_map/ppermute | solution.py:36
  71.9 12.8 %collective-permute-start.26 = (bf16[224,128]{1,0:T(8,128)(2,1)S(1)}, bf16[224,128]{1,0:T(8,128)(2,1)S(1)}, u32[]{:S(2)}, u32[]{:S(2)}) collective-permute-start(bf16[224,128]{1,0:T(8,128)(2,1)S(1)} %get-tuple-element.38), channel_id=1, source_target_pairs={{0,4},{1,5},{2,6},{3,7},{4,8},{5,9},{6,10},{7,11},{8,12},{9,13},{1... | collective-permute-start | bytes 172040 | tf_op jit(solution)/shard_map/ppermute | solution.py:36
  75.1 12.0 %collective-permute-start.25 = (bf16[2,448,128]{2,1,0:T(8,128)(2,1)S(1)}, bf16[2,448,128]{2,1,0:T(8,128)(2,1)S(1)}, u32[]{:S(2)}, u32[]{:S(2)}) collective-permute-start(bf16[2,448,128]{2,1,0:T(8,128)(2,1)S(1)} %get-tuple-element.34), channel_id=1, source_target_pairs={{0,14},{1,15},{2,0},{3,1},{4,2},{5,3},{6,4},{7,5},{8,6},{9,7},{10,... | collective-permute-start | bytes 688136 | tf_op jit(solution)/shard_map/ppermute | solution.py:36
  76.4 10.7 %collective-permute-start.28 = (bf16[224,128]{1,0:T(8,128)(2,1)S(1)}, bf16[224,128]{1,0:T(8,128)(2,1)S(1)}, u32[]{:S(2)}, u32[]{:S(2)}) collective-permute-start(bf16[224,128]{1,0:T(8,128)(2,1)S(1)} %get-tuple-element.40), channel_id=1, source_target_pairs={{0,12},{1,13},{2,14},{3,15},{4,0},{5,1},{6,2},{7,3},{8,4},{9,5},{1... | collective-permute-start | bytes 172040 | tf_op jit(solution)/shard_map/ppermute | solution.py:36
  84.7 8.7 %collective-permute-start.27 = (bf16[448,128]{1,0:T(8,128)(2,1)S(1)}, bf16[448,128]{1,0:T(8,128)(2,1)S(1)}, u32[]{:S(2)}, u32[]{:S(2)}) collective-permute-start(bf16[448,128]{1,0:T(8,128)(2,1)S(1)} %fusion.3), channel_id=1, source_target_pairs={{0,4},{1,5},{2,6},{3,7},{4,8},{5,9},{6,10},{7,11},{8,12},{9,13},{1... | collective-permute-start | bytes 344072 | tf_op jit(solution)/shard_map/ppermute | solution.py:36
  87.2 6.2 %collective-permute-start.29 = (bf16[448,128]{1,0:T(8,128)(2,1)S(1)}, bf16[448,128]{1,0:T(8,128)(2,1)S(1)}, u32[]{:S(2)}, u32[]{:S(2)}) collective-permute-start(bf16[448,128]{1,0:T(8,128)(2,1)S(1)} %fusion.1), channel_id=1, source_target_pairs={{0,12},{1,13},{2,14},{3,15},{4,0},{5,1},{6,2},{7,3},{8,4},{9,5},{1... | collective-permute-start | bytes 344072 | tf_op jit(solution)/shard_map/ppermute | solution.py:36
  93.5 13.6 %collective-permute-start.30 = (bf16[448,128]{1,0:T(8,128)(2,1)S(1)}, bf16[448,128]{1,0:T(8,128)(2,1)S(1)}, u32[]{:S(2)}, u32[]{:S(2)}) collective-permute-start(bf16[448,128]{1,0:T(8,128)(2,1)S(1)} %fusion.6), channel_id=1, source_target_pairs={{0,0},{1,1},{2,2},{3,3},{4,64},{5,65},{6,66},{7,67},{8,128},{9,129... | collective-permute-start | bytes 344072 | tf_op jit(solution)/shard_map/ppermute | solution.py:36

commit v5 on v4

--- a/solution.py
+++ b/solution.py
@@ -366,13 +366,21 @@
     far_up, far_down = after((far_up, far_down), (up, down))
     from_far_low = send(far_up, along(2))
     from_far_high = send(far_down, along(6))
-    up_sum = wide(up2) + wide(from_low[0]) + jnp.pad(wide(from_far_low), ((0, width // 2), (0, 0)))
-    down_sum = (
-        wide(down2) + wide(from_high[0]) + jnp.pad(wide(from_far_high), ((width // 2, 0), (0, 0)))
+    up_sum = jnp.concatenate(
+        [
+            wide(up2[: width // 2]) + wide(from_low[0, : width // 2]) + wide(from_far_low),
+            wide(up2[width // 2 :]) + wide(from_low[0, width // 2 :]),
+        ]
     )
-    total = wide(own) + wide(from_low[1]) + wide(from_high[1])
-    total = total + wide(send(up_sum.astype(jnp.bfloat16), along(2)))
-    total = total + wide(send(down_sum.astype(jnp.bfloat16), along(6)))
+    down_sum = jnp.concatenate(
+        [
+            wide(down2[: width // 2]) + wide(from_high[0, : width // 2]),
+            wide(down2[width // 2 :]) + wide(from_high[0, width // 2 :]) + wide(from_far_high),
+        ]
+    )
+    from_up = send(up_sum.astype(jnp.bfloat16), along(2))
+    from_down = send(down_sum.astype(jnp.bfloat16), along(6))
+    total = wide(own) + wide(from_low[1]) + wide(from_high[1]) + wide(from_up) + wide(from_down)
     total = total.astype(jnp.bfloat16)
 
     def final(ty, txh, tcore, tz, txl):

time: 109 us -> 110 us (level)
  waiting for transfers between devices: 45.3 us -> 49.1 us
  starting transfers between devices: 48 us -> 46.7 us
    ppermute x31, waiting for transfers between devices: 45.3 us -> 49.1 us  [send(): return lax.ppermute(value, AXES, pairs)]
    ppermute x31, starting transfers between devices: 48 us -> 46.7 us  [send(): return lax.ppermute(value, AXES, pairs)]
  transfers between devices with their start and end apart: 31 -> 31, of which waited for: 15 -> 17; matrix products, arithmetic and copies ran while one was open for 0% -> 0% of each run, Pallas kernels for 7% -> 6%
where the time goes in v5:
time: 110 us; the launch traced here: 109 us
  waiting for transfers between devices  49.1 us (45%)
  starting transfers between devices  46.7 us (42%)
  Pallas kernels  9.72 us (9%)
  local copies, waits for them, and re-layouts  3.31 us (3%)
    ppermute x31, waiting for transfers between devices, send(): return lax.ppermute(value, AXES, pairs)  49.1 us
    ppermute x31, starting transfers between devices, send(): return lax.ppermute(value, AXES, pairs)  46.7 us
    pallas_call x1, Pallas kernels, body(): pl.pallas_call(attend_kernel, out_shape=jax.ShapeDtypeStruct((rows, heads...  6.33 us
    unnamed x13, local copies, waits for them, and re-layouts  3.31 us
    pallas_call x1, Pallas kernels, body(): pl.pallas_call(project_kernel, out_shape=[result(width, rows), result(2,...  2.96 us
  transfers between devices with their start and end apart: 31, of which 17 were waited for; matrix products, arithmetic and copies ran while one was open for 0% of the time, Pallas kernels for 6%

profile of v5, /device:TPU:16, one launch (start us, length us, event | category | flops | bytes accessed | tf_op | source)
XLA Modules:
  0.0 109.3 jit_solution(15348660427560876108)
XLA Ops:
  0.0 2.5 %collective-permute-start = (bf16[448,1024]{1,0:T(8,128)(2,1)}, bf16[448,1024]{1,0:T(8,128)(2,1)S(1)}, u32[]{:S(2)}, u32[]{:S(2)}) collective-permute-start(bf16[448,1024]{1,0:T(8,128)(2,1)} %bitcast.33), channel_id=1, source_target_pairs={{0,48},{1,0},{2,50},{3,2},{4,52},{5,4},{6,54},{7,6},{8,56},{9,8},{... | collective-permute-start | bytes 2752520 | tf_op jit(solution)/shard_map/ppermute | solution.py:36
  2.5 0.7 collective-permute-start.12
  3.1 1.3 %collective-permute-start.10 = (bf16[576,128]{1,0:T(8,128)(2,1)}, bf16[576,128]{1,0:T(8,128)(2,1)S(1)}, u32[]{:S(2)}, u32[]{:S(2)}) collective-permute-start(bf16[576,128]{1,0:T(8,128)(2,1)} %bitcast.38), channel_id=1, source_target_pairs={{0,161},{1,160},{2,163},{3,162},{4,165},{5,164},{6,167},{7,166},{8... | collective-permute-start | bytes 442376 | tf_op jit(solution)/shard_map/ppermute | solution.py:36
  4.4 1.3 %collective-permute-start.8 = (bf16[576,128]{1,0:T(8,128)(2,1)}, bf16[576,128]{1,0:T(8,128)(2,1)S(1)}, u32[]{:S(2)}, u32[]{:S(2)}) collective-permute-start(bf16[576,128]{1,0:T(8,128)(2,1)} %bitcast.39), channel_id=1, source_target_pairs={{0,128},{1,129},{2,130},{3,131},{4,132},{5,133},{6,134},{7,135},{8... | collective-permute-start | bytes 442376 | tf_op jit(solution)/shard_map/ppermute | solution.py:36
  5.7 3.8 %collective-permute-start.6 = (bf16[576,128]{1,0:T(8,128)(2,1)}, bf16[576,128]{1,0:T(8,128)(2,1)S(1)}, u32[]{:S(2)}, u32[]{:S(2)}) collective-permute-start(bf16[576,128]{1,0:T(8,128)(2,1)} %bitcast.40), channel_id=1, source_target_pairs={{0,97},{1,96},{2,99},{3,98},{4,101},{5,100},{6,103},{7,102},{8,105... | collective-permute-start | bytes 442376 | tf_op jit(solution)/shard_map/ppermute | solution.py:36
  9.5 1.2 %copy-done.1 = bf16[8,512,128]{2,1,0:T(8,128)(2,1)S(1)} copy-done((bf16[8,512,128]{2,1,0:T(8,128)(2,1)S(1)}, bf16[8,512,128]{2,1,0:T(8,128)(2,1)}, u32[]{:S(2)}) %copy-start.1) | copy-done | bytes 1048600
  10.7 1.0 copy-done.3
  11.7 0.4 absorb.1
  12.2 0.4 copy-done.4
  12.6 6.6 %collective-permute-start.4 = (bf16[576,128]{1,0:T(8,128)(2,1)S(1)}, bf16[576,128]{1,0:T(8,128)(2,1)S(1)}, u32[]{:S(2)}, u32[]{:S(2)}) collective-permute-start(bf16[576,128]{1,0:T(8,128)(2,1)S(1)} %bitcast.41), channel_id=1, source_target_pairs={{0,64},{1,65},{2,66},{3,67},{4,68},{5,69},{6,70},{7,71},{8,72},{9,... | collective-permute-start | bytes 442376 | tf_op jit(solution)/shard_map/ppermute | solution.py:36
  19.2 2.7 %collective-permute-start.1 = (bf16[576,128]{1,0:T(8,128)(2,1)S(1)}, bf16[576,128]{1,0:T(8,128)(2,1)S(1)}, u32[]{:S(2)}, u32[]{:S(2)}) collective-permute-start(bf16[576,128]{1,0:T(8,128)(2,1)S(1)} %bitcast.42), channel_id=1, source_target_pairs={{0,16},{1,17},{2,18},{3,19},{4,20},{5,21},{6,22},{7,23},{8,24},{9,... | collective-permute-start | bytes 442376 | tf_op jit(solution)/shard_map/ppermute | solution.py:36
  21.9 1.2 %collective-permute-done.6.rest_6_ = bf16[576,128]{1,0:T(8,128)(2,1)S(1)} collective-permute-done((bf16[576,128]{1,0:T(8,128)(2,1)}, bf16[576,128]{1,0:T(8,128)(2,1)S(1)}, u32[]{:S(2)}, u32[]{:S(2)}) %collective-permute-start.6) | collective-permute-done | bytes 147488 | tf_op jit(solution)/shard_map/ppermute | solution.py:36
  23.1 1.4 %collective-permute-done.4.rest_4_ = bf16[576,128]{1,0:T(8,128)(2,1)S(1)} collective-permute-done((bf16[576,128]{1,0:T(8,128)(2,1)S(1)}, bf16[576,128]{1,0:T(8,128)(2,1)S(1)}, u32[]{:S(2)}, u32[]{:S(2)}) %collective-permute-start.4) | collective-permute-done | bytes 147488 | tf_op jit(solution)/shard_map/ppermute | solution.py:36
  24.6 0.4 collective-permute-start.7
  25.0 3.8 %collective-permute-done.2.rest_2_ = bf16[576,128]{1,0:T(8,128)(2,1)S(1)} collective-permute-done((bf16[576,128]{1,0:T(8,128)(2,1)S(1)}, bf16[576,128]{1,0:T(8,128)(2,1)S(1)}, u32[]{:S(2)}, u32[]{:S(2)}) %collective-permute-start.2) | collective-permute-done | bytes 147488 | tf_op jit(solution)/shard_map/ppermute | solution.py:36
  28.9 0.5 collective-permute-start.3
  29.4 0.9 collective-permute-done.5.rest_5_
  30.2 0.2 collective-permute-done.3.rest_3_
  30.4 0.3 collective-permute-start.13
  30.8 2.2 %collective-permute-start.14 = (bf16[448,1024]{1,0:T(8,128)(2,1)}, bf16[448,1024]{1,0:T(8,128)(2,1)S(1)}, u32[]{:S(2)}, u32[]{:S(2)}) collective-permute-start(bf16[448,1024]{1,0:T(8,128)(2,1)} %bitcast.34), channel_id=1, source_target_pairs={{0,16},{2,18},{4,20},{6,22},{8,24},{10,26},{12,28},{14,30},{17,1},... | collective-permute-start | bytes 2752520 | tf_op jit(solution)/shard_map/ppermute | solution.py:36
  32.9 0.7 collective-permute-start.22
  33.7 6.3 %attend.1.rest_0_ = bf16[128,1024]{1,0:T(8,128)(2,1)S(1)} custom-call(s32[8]{0:T(128)S(1)} %copy-done.5, bf16[1024,512]{1,0:T(8,128)(2,1)S(1)} %get-tuple-element.27.qc_ref, bf16[1024,64]{1,0:T(8,128)(2,1)S(1)} %get-tuple-element.24.qr_ref, bf16[8,512,128]{2,1,0:T(8,128)(2,1)S(1)} %copy-done, bf16[576,128]{1,0:T(8,128)(2,1)S(1)} %bitcast.44, ...), custom_call_target="tpu_custom_call" | custom-call | tf_op jit(solution)/shard_map/attend/pallas_call | solution.py:301
  40.0 0.1 collective-permute-start.18
  40.3 1.9 %collective-permute-start.15 = (bf16[128,1024]{1,0:T(8,128)(2,1)S(1)}, bf16[128,1024]{1,0:T(8,128)(2,1)S(1)}, u32[]{:S(2)}, u32[]{:S(2)}) collective-permute-start(bf16[128,1024]{1,0:T(8,128)(2,1)S(1)} %attend.1.rest_0_), channel_id=1, source_target_pairs={{0,64},{1,65},{2,66},{3,67},{4,68},{5,69},{6,70},{7,71},{8,72},{9,... | collective-permute-start | bytes 786440 | tf_op jit(solution)/shard_map/ppermute | solution.py:36
  42.2 6.9 %collective-permute-done.18.rest_4_ = bf16[128,1024]{1,0:T(8,128)(2,1)S(1)} collective-permute-done((bf16[128,1024]{1,0:T(8,128)(2,1)S(1)}, bf16[128,1024]{1,0:T(8,128)(2,1)S(1)}, u32[]{:S(2)}, u32[]{:S(2)}) %collective-permute-start.18) | collective-permute-done | bytes 262176 | tf_op jit(solution)/shard_map/ppermute | solution.py:36
  49.2 0.2 collective-permute-done.17.rest_3_
  49.4 1.7 %collective-permute-done.16.rest_2_ = bf16[128,1024]{1,0:T(8,128)(2,1)S(1)} collective-permute-done((bf16[128,1024]{1,0:T(8,128)(2,1)S(1)}, bf16[128,1024]{1,0:T(8,128)(2,1)S(1)}, u32[]{:S(2)}, u32[]{:S(2)}) %collective-permute-start.16) | collective-permute-done | bytes 262176 | tf_op jit(solution)/shard_map/ppermute | solution.py:36
  51.0 5.0 %collective-permute-done.15.rest_1_ = bf16[128,1024]{1,0:T(8,128)(2,1)S(1)} collective-permute-done((bf16[128,1024]{1,0:T(8,128)(2,1)S(1)}, bf16[128,1024]{1,0:T(8,128)(2,1)S(1)}, u32[]{:S(2)}, u32[]{:S(2)}) %collective-permute-start.15) | collective-permute-done | bytes 262176 | tf_op jit(solution)/shard_map/ppermute | solution.py:36
  56.1 1.5 %collective-permute-start.23 = (bf16[448,1024]{1,0:T(8,128)(2,1)S(1)}, bf16[448,1024]{1,0:T(8,128)(2,1)S(1)}, u32[]{:S(2)}, u32[]{:S(2)}) collective-permute-start(bf16[448,1024]{1,0:T(8,128)(2,1)S(1)} %collective-permute-done.22.rest_14_), channel_id=1, source_target_pairs={{1,17},{3,19},{5,21},{7,23},{9,25},{11,27},{13,29},{15,31},{16,0},... | collective-permute-start | bytes 2752520 | tf_op jit(solution)/shard_map/ppermute | solution.py:36
  57.5 1.1 %collective-permute-start.21 = (bf16[128,1024]{1,0:T(8,128)(2,1)S(1)}, bf16[128,1024]{1,0:T(8,128)(2,1)S(1)}, u32[]{:S(2)}, u32[]{:S(2)}) collective-permute-start(bf16[128,1024]{1,0:T(8,128)(2,1)S(1)} %collective-permute-done.18.rest_4_), channel_id=1, source_target_pairs={{0,192},{1,193},{2,194},{3,195},{4,196},{5,197},{6,198},{7,199},{8... | collective-permute-start | bytes 786440 | tf_op jit(solution)/shard_map/ppermute | solution.py:36
  58.6 1.0 collective-permute-start.19
  59.6 2.1 %collective-permute-start.20 = (bf16[128,1024]{1,0:T(8,128)(2,1)S(1)}, bf16[128,1024]{1,0:T(8,128)(2,1)S(1)}, u32[]{:S(2)}, u32[]{:S(2)}) collective-permute-start(bf16[128,1024]{1,0:T(8,128)(2,1)S(1)} %collective-permute-done.16.rest_2_), channel_id=1, source_target_pairs={{0,1},{1,0},{2,3},{3,2},{4,5},{5,4},{6,7},{7,6},{8,9},{9,8},{10,11... | collective-permute-start | bytes 786440 | tf_op jit(solution)/shard_map/ppermute | solution.py:36
  61.7 4.9 %collective-permute-done.21.rest_7_ = bf16[128,1024]{1,0:T(8,128)(2,1)S(1)} collective-permute-done((bf16[128,1024]{1,0:T(8,128)(2,1)S(1)}, bf16[128,1024]{1,0:T(8,128)(2,1)S(1)}, u32[]{:S(2)}, u32[]{:S(2)}) %collective-permute-start.21) | collective-permute-done | bytes 262176 | tf_op jit(solution)/shard_map/ppermute | solution.py:36
  66.6 1.2 %collective-permute-done.19.rest_5_ = bf16[128,1024]{1,0:T(8,128)(2,1)S(1)} collective-permute-done((bf16[128,1024]{1,0:T(8,128)(2,1)S(1)}, bf16[128,1024]{1,0:T(8,128)(2,1)S(1)}, u32[]{:S(2)}, u32[]{:S(2)}) %collective-permute-start.19) | collective-permute-done | bytes 262176 | tf_op jit(solution)/shard_map/ppermute | solution.py:36
  67.7 0.7 collective-permute-done.20.rest_6_
  68.5 3.0 %project.1 = (bf16[448,128]{1,0:T(8,128)(2,1)S(1)}, bf16[2,448,128]{2,1,0:T(8,128)(2,1)S(1)}, bf16[2,448,128]{2,1,0:T(8,128)(2,1)S(1)}, bf16[224,128]{1,0:T(8,12...) custom-call(bf16[128,1024]{1,0:T(8,128)(2,1)S(1)} %attend.1.rest_0_, ...), custom_call_target="tpu_custom_call" | custom-call | tf_op jit(solution)/shard_map/project/pallas_call | solution.py:336
  71.4 2.0 %collective-permute-start.24 = (bf16[2,448,128]{2,1,0:T(8,128)(2,1)S(1)}, bf16[2,448,128]{2,1,0:T(8,128)(2,1)S(1)}, u32[]{:S(2)}, u32[]{:S(2)}) collective-permute-start(bf16[2,448,128]{2,1,0:T(8,128)(2,1)S(1)} %get-tuple-element.33), channel_id=1, source_target_pairs={{0,2},{1,3},{2,4},{3,5},{4,6},{5,7},{6,8},{7,9},{8,10},{9,11},{10,... | collective-permute-start | bytes 688136 | tf_op jit(solution)/shard_map/ppermute | solution.py:36
  73.4 3.3 %collective-permute-start.26 = (bf16[224,128]{1,0:T(8,128)(2,1)S(1)}, bf16[224,128]{1,0:T(8,128)(2,1)S(1)}, u32[]{:S(2)}, u32[]{:S(2)}) collective-permute-start(bf16[224,128]{1,0:T(8,128)(2,1)S(1)} %get-tuple-element.38), channel_id=1, source_target_pairs={{0,4},{1,5},{2,6},{3,7},{4,8},{5,9},{6,10},{7,11},{8,12},{9,13},{1... | collective-permute-start | bytes 172040 | tf_op jit(solution)/shard_map/ppermute | solution.py:36
  76.7 1.3 %collective-permute-start.25 = (bf16[2,448,128]{2,1,0:T(8,128)(2,1)S(1)}, bf16[2,448,128]{2,1,0:T(8,128)(2,1)S(1)}, u32[]{:S(2)}, u32[]{:S(2)}) collective-permute-start(bf16[2,448,128]{2,1,0:T(8,128)(2,1)S(1)} %get-tuple-element.34), channel_id=1, source_target_pairs={{0,14},{1,15},{2,0},{3,1},{4,2},{5,3},{6,4},{7,5},{8,6},{9,7},{10,... | collective-permute-start | bytes 688136 | tf_op jit(solution)/shard_map/ppermute | solution.py:36
  78.0 2.4 %collective-permute-start.28 = (bf16[224,128]{1,0:T(8,128)(2,1)S(1)}, bf16[224,128]{1,0:T(8,128)(2,1)S(1)}, u32[]{:S(2)}, u32[]{:S(2)}) collective-permute-start(bf16[224,128]{1,0:T(8,128)(2,1)S(1)} %get-tuple-element.40), channel_id=1, source_target_pairs={{0,12},{1,13},{2,14},{3,15},{4,0},{5,1},{6,2},{7,3},{8,4},{9,5},{1... | collective-permute-start | bytes 172040 | tf_op jit(solution)/shard_map/ppermute | solution.py:36
  80.4 5.6 %collective-permute-done.26 = bf16[224,128]{1,0:T(8,128)(2,1)S(1)} collective-permute-done((bf16[224,128]{1,0:T(8,128)(2,1)S(1)}, bf16[224,128]{1,0:T(8,128)(2,1)S(1)}, u32[]{:S(2)}, u32[]{:S(2)}) %collective-permute-start.26) | collective-permute-done | bytes 57376 | tf_op jit(solution)/shard_map/ppermute | solution.py:36
  86.1 2.4 %collective-permute-done.28 = bf16[224,128]{1,0:T(8,128)(2,1)S(1)} collective-permute-done((bf16[224,128]{1,0:T(8,128)(2,1)S(1)}, bf16[224,128]{1,0:T(8,128)(2,1)S(1)}, u32[]{:S(2)}, u32[]{:S(2)}) %collective-permute-start.28) | collective-permute-done | bytes 57376 | tf_op jit(solution)/shard_map/ppermute | solution.py:36
  88.5 1.9 %collective-permute-start.29 = (bf16[448,128]{1,0:T(8,128)(2,1)S(1)}, bf16[448,128]{1,0:T(8,128)(2,1)S(1)}, u32[]{:S(2)}, u32[]{:S(2)}) collective-permute-start(bf16[448,128]{1,0:T(8,128)(2,1)S(1)} %pad_maximum_fusion.1), channel_id=1, source_target_pairs={{0,12},{1,13},{2,14},{3,15},{4,0},{5,1},{6,2},{7,3},{8,4},{9,5},{1... | collective-permute-start | bytes 344072 | tf_op jit(solution)/shard_map/ppermute | solution.py:36
  90.4 4.3 %collective-permute-done.27 = bf16[448,128]{1,0:T(8,128)(2,1)S(1)} collective-permute-done((bf16[448,128]{1,0:T(8,128)(2,1)S(1)}, bf16[448,128]{1,0:T(8,128)(2,1)S(1)}, u32[]{:S(2)}, u32[]{:S(2)}) %collective-permute-start.27) | collective-permute-done | bytes 114720 | tf_op jit(solution)/shard_map/ppermute | solution.py:36
  94.7 0.8 collective-permute-done.29
  95.6 5.1 %collective-permute-start.30 = (bf16[448,128]{1,0:T(8,128)(2,1)S(1)}, bf16[448,128]{1,0:T(8,128)(2,1)S(1)}, u32[]{:S(2)}, u32[]{:S(2)}) collective-permute-start(bf16[448,128]{1,0:T(8,128)(2,1)S(1)} %fusion.2), channel_id=1, source_target_pairs={{0,0},{1,1},{2,2},{3,3},{4,64},{5,65},{6,66},{7,67},{8,128},{9,129... | collective-permute-start | bytes 344072 | tf_op jit(solution)/shard_map/ppermute | solution.py:36
  100.7 7.9 %collective-permute-done.30 = bf16[448,128]{1,0:T(8,128)(2,1)S(1)} collective-permute-done((bf16[448,128]{1,0:T(8,128)(2,1)S(1)}, bf16[448,128]{1,0:T(8,128)(2,1)S(1)}, u32[]{:S(2)}, u32[]{:S(2)}) %collective-permute-start.30) | collective-permute-done | bytes 114720 | tf_op jit(solution)/shard_map/ppermute | solution.py:36
  108.6 0.6 copy.8
  (35 shorter events, 0.6 us)
Async XLA Ops:
  0.0 33.7 %copy-start = (bf16[8,512,128]{2,1,0:T(8,128)(2,1)S(1)}, bf16[8,512,128]{2,1,0:T(8,128)(2,1)}, u32[]{:S(2)}) copy-start(bf16[8,512,128]{2,1,0:T(8,128)(2,1)} %w_uv_any.1) | copy-start | bytes 3145732
  0.0 30.4 %collective-permute-start = (bf16[448,1024]{1,0:T(8,128)(2,1)}, bf16[448,1024]{1,0:T(8,128)(2,1)S(1)}, u32[]{:S(2)}, u32[]{:S(2)}) collective-permute-start(bf16[448,1024]{1,0:T(8,128)(2,1)} %bitcast.33), channel_id=1, source_target_pairs={{0,48},{1,0},{2,50},{3,2},{4,52},{5,4},{6,54},{7,6},{8,56},{9,8},{... | collective-permute-start | bytes 2752520 | tf_op jit(solution)/shard_map/ppermute | solution.py:36
  2.5 9.7 %collective-permute-start.12 = (bf16[576,128]{1,0:T(8,128)(2,1)}, bf16[576,128]{1,0:T(8,128)(2,1)S(1)}, u32[]{:S(2)}, u32[]{:S(2)}) collective-permute-start(bf16[576,128]{1,0:T(8,128)(2,1)} %bitcast.37), channel_id=1, source_target_pairs={{48,193},{49,192},{50,195},{51,194},{52,197},{53,196},{54,199},{55... | collective-permute-start | bytes 442376 | tf_op jit(solution)/shard_map/ppermute | solution.py:36
  3.1 16.1 %collective-permute-start.10 = (bf16[576,128]{1,0:T(8,128)(2,1)}, bf16[576,128]{1,0:T(8,128)(2,1)S(1)}, u32[]{:S(2)}, u32[]{:S(2)}) collective-permute-start(bf16[576,128]{1,0:T(8,128)(2,1)} %bitcast.38), channel_id=1, source_target_pairs={{0,161},{1,160},{2,163},{3,162},{4,165},{5,164},{6,167},{7,166},{8... | collective-permute-start | bytes 442376 | tf_op jit(solution)/shard_map/ppermute | solution.py:36
  4.4 17.5 %collective-permute-start.8 = (bf16[576,128]{1,0:T(8,128)(2,1)}, bf16[576,128]{1,0:T(8,128)(2,1)S(1)}, u32[]{:S(2)}, u32[]{:S(2)}) collective-permute-start(bf16[576,128]{1,0:T(8,128)(2,1)} %bitcast.39), channel_id=1, source_target_pairs={{0,128},{1,129},{2,130},{3,131},{4,132},{5,133},{6,134},{7,135},{8... | collective-permute-start | bytes 442376 | tf_op jit(solution)/shard_map/ppermute | solution.py:36
  5.7 17.3 %collective-permute-start.6 = (bf16[576,128]{1,0:T(8,128)(2,1)}, bf16[576,128]{1,0:T(8,128)(2,1)S(1)}, u32[]{:S(2)}, u32[]{:S(2)}) collective-permute-start(bf16[576,128]{1,0:T(8,128)(2,1)} %bitcast.40), channel_id=1, source_target_pairs={{0,97},{1,96},{2,99},{3,98},{4,101},{5,100},{6,103},{7,102},{8,105... | collective-permute-start | bytes 442376 | tf_op jit(solution)/shard_map/ppermute | solution.py:36
  9.5 1.2 %copy-start.1 = (bf16[8,512,128]{2,1,0:T(8,128)(2,1)S(1)}, bf16[8,512,128]{2,1,0:T(8,128)(2,1)}, u32[]{:S(2)}) copy-start(bf16[8,512,128]{2,1,0:T(8,128)(2,1)} %w_uk_ref.1) | copy-start | bytes 3145732
  10.7 1.0 copy-start.3
  11.7 0.9 copy-start.4
  12.2 21.5 %copy-start.5 = (s32[8]{0:T(128)S(1)}, s32[8]{0:T(128)}, u32[]{:S(2)}) copy-start(s32[8]{0:T(128)} %lengths_ref.1) | copy-start | bytes 100
  12.2 56.3 %copy-start.2 = (bf16[1024,448]{0,1:T(8,128)(2,1)S(1)}, bf16[1024,448]{0,1:T(8,128)(2,1)}, u32[]{:S(2)}) copy-start(bf16[1024,448]{0,1:T(8,128)(2,1)} %param.10) | copy-start | bytes 2752516
  12.6 11.9 %collective-permute-start.4 = (bf16[576,128]{1,0:T(8,128)(2,1)S(1)}, bf16[576,128]{1,0:T(8,128)(2,1)S(1)}, u32[]{:S(2)}, u32[]{:S(2)}) collective-permute-start(bf16[576,128]{1,0:T(8,128)(2,1)S(1)} %bitcast.41), channel_id=1, source_target_pairs={{0,64},{1,65},{2,66},{3,67},{4,68},{5,69},{6,70},{7,71},{8,72},{9,... | collective-permute-start | bytes 442376 | tf_op jit(solution)/shard_map/ppermute | solution.py:36
  19.2 5.4 %collective-permute-start.1 = (bf16[576,128]{1,0:T(8,128)(2,1)S(1)}, bf16[576,128]{1,0:T(8,128)(2,1)S(1)}, u32[]{:S(2)}, u32[]{:S(2)}) collective-permute-start(bf16[576,128]{1,0:T(8,128)(2,1)S(1)} %bitcast.42), channel_id=1, source_target_pairs={{0,16},{1,17},{2,18},{3,19},{4,20},{5,21},{6,22},{7,23},{8,24},{9,... | collective-permute-start | bytes 442376 | tf_op jit(solution)/shard_map/ppermute | solution.py:36
  21.9 7.0 %collective-permute-start.2 = (bf16[576,128]{1,0:T(8,128)(2,1)S(1)}, bf16[576,128]{1,0:T(8,128)(2,1)S(1)}, u32[]{:S(2)}, u32[]{:S(2)}) collective-permute-start(bf16[576,128]{1,0:T(8,128)(2,1)S(1)} %bitcast.43), channel_id=1, source_target_pairs={{0,33},{1,32},{2,35},{3,34},{4,37},{5,36},{6,39},{7,38},{8,41},{9,... | collective-permute-start | bytes 442376 | tf_op jit(solution)/shard_map/ppermute | solution.py:36
  23.1 5.8 %collective-permute-start.11 = (bf16[576,128]{1,0:T(8,128)(2,1)S(1)}, bf16[576,128]{1,0:T(8,128)(2,1)S(1)}, u32[]{:S(2)}, u32[]{:S(2)}) collective-permute-start(bf16[576,128]{1,0:T(8,128)(2,1)S(1)} %collective-permute-done.10.rest_10_), channel_id=1, source_target_pairs={{0,16},{1,17},{2,18},{3,19},{4,20},{5,21},{6,22},{7,23},{8,24},{9,... | collective-permute-start | bytes 442376 | tf_op jit(solution)/shard_map/ppermute | solution.py:36
  24.5 4.8 %collective-permute-start.9 = (bf16[576,128]{1,0:T(8,128)(2,1)S(1)}, bf16[576,128]{1,0:T(8,128)(2,1)S(1)}, u32[]{:S(2)}, u32[]{:S(2)}) collective-permute-start(bf16[576,128]{1,0:T(8,128)(2,1)S(1)} %collective-permute-done.8.rest_8_), channel_id=1, source_target_pairs={{0,16},{1,17},{2,18},{3,19},{4,20},{5,21},{6,22},{7,23},{8,24},{9,... | collective-permute-start | bytes 442376 | tf_op jit(solution)/shard_map/ppermute | solution.py:36
  24.6 4.8 %collective-permute-start.7 = (bf16[576,128]{1,0:T(8,128)(2,1)S(1)}, bf16[576,128]{1,0:T(8,128)(2,1)S(1)}, u32[]{:S(2)}, u32[]{:S(2)}) collective-permute-start(bf16[576,128]{1,0:T(8,128)(2,1)S(1)} %collective-permute-done.6.rest_6_), channel_id=1, source_target_pairs={{0,16},{1,17},{2,18},{3,19},{4,20},{5,21},{6,22},{7,23},{8,24},{9,... | collective-permute-start | bytes 442376 | tf_op jit(solution)/shard_map/ppermute | solution.py:36
  28.9 1.4 %collective-permute-start.5 = (bf16[576,128]{1,0:T(8,128)(2,1)S(1)}, bf16[576,128]{1,0:T(8,128)(2,1)S(1)}, u32[]{:S(2)}, u32[]{:S(2)}) collective-permute-start(bf16[576,128]{1,0:T(8,128)(2,1)S(1)} %collective-permute-done.4.rest_4_), channel_id=1, source_target_pairs={{0,16},{1,17},{2,18},{3,19},{4,20},{5,21},{6,22},{7,23},{8,24},{9,... | collective-permute-start | bytes 442376 | tf_op jit(solution)/shard_map/ppermute | solution.py:36
  28.9 1.6 %collective-permute-start.3 = (bf16[576,128]{1,0:T(8,128)(2,1)S(1)}, bf16[576,128]{1,0:T(8,128)(2,1)S(1)}, u32[]{:S(2)}, u32[]{:S(2)}) collective-permute-start(bf16[576,128]{1,0:T(8,128)(2,1)S(1)} %collective-permute-done.2.rest_2_), channel_id=1, source_target_pairs={{0,16},{1,17},{2,18},{3,19},{4,20},{5,21},{6,22},{7,23},{8,24},{9,... | collective-permute-start | bytes 442376 | tf_op jit(solution)/shard_map/ppermute | solution.py:36
  30.4 3.2 %collective-permute-start.13 = (bf16[448,1024]{1,0:T(8,128)(2,1)S(1)}, bf16[448,1024]{1,0:T(8,128)(2,1)S(1)}, u32[]{:S(2)}, u32[]{:S(2)}) collective-permute-start(bf16[448,1024]{1,0:T(8,128)(2,1)S(1)} %collective-permute-done.rest_9_.rest_15_), channel_id=1, source_target_pairs={{0,16},{1,17},{2,18},{3,19},{4,20},{5,21},{6,22},{7,23},{8,24},{9,... | collective-permute-start | bytes 2752520 | tf_op jit(solution)/shard_map/ppermute | solution.py:36
  30.8 9.3 %collective-permute-start.14 = (bf16[448,1024]{1,0:T(8,128)(2,1)}, bf16[448,1024]{1,0:T(8,128)(2,1)S(1)}, u32[]{:S(2)}, u32[]{:S(2)}) collective-permute-start(bf16[448,1024]{1,0:T(8,128)(2,1)} %bitcast.34), channel_id=1, source_target_pairs={{0,16},{2,18},{4,20},{6,22},{8,24},{10,26},{12,28},{14,30},{17,1},... | collective-permute-start | bytes 2752520 | tf_op jit(solution)/shard_map/ppermute | solution.py:36
  32.9 9.3 %collective-permute-start.22 = (bf16[448,1024]{1,0:T(8,128)(2,1)}, bf16[448,1024]{1,0:T(8,128)(2,1)S(1)}, u32[]{:S(2)}, u32[]{:S(2)}) collective-permute-start(bf16[448,1024]{1,0:T(8,128)(2,1)} %bitcast.35), channel_id=1, source_target_pairs={{1,48},{3,50},{5,52},{7,54},{9,56},{11,58},{13,60},{15,62},{16,33}... | collective-permute-start | bytes 2752520 | tf_op jit(solution)/shard_map/ppermute | solution.py:36
  40.0 9.1 %collective-permute-start.18 = (bf16[128,1024]{1,0:T(8,128)(2,1)S(1)}, bf16[128,1024]{1,0:T(8,128)(2,1)S(1)}, u32[]{:S(2)}, u32[]{:S(2)}) collective-permute-start(bf16[128,1024]{1,0:T(8,128)(2,1)S(1)} %attend.1.rest_0_), channel_id=1, source_target_pairs={{0,1},{1,0},{2,3},{3,2},{4,5},{5,4},{6,7},{7,6},{8,9},{9,8},{10,11... | collective-permute-start | bytes 786440 | tf_op jit(solution)/shard_map/ppermute | solution.py:36
  40.1 9.3 %collective-permute-start.17 = (bf16[128,1024]{1,0:T(8,128)(2,1)S(1)}, bf16[128,1024]{1,0:T(8,128)(2,1)S(1)}, u32[]{:S(2)}, u32[]{:S(2)}) collective-permute-start(bf16[128,1024]{1,0:T(8,128)(2,1)S(1)} %attend.1.rest_0_), channel_id=1, source_target_pairs={{0,192},{1,193},{2,194},{3,195},{4,196},{5,197},{6,198},{7,199},{8... | collective-permute-start | bytes 786440 | tf_op jit(solution)/shard_map/ppermute | solution.py:36
  40.2 10.8 %collective-permute-start.16 = (bf16[128,1024]{1,0:T(8,128)(2,1)S(1)}, bf16[128,1024]{1,0:T(8,128)(2,1)S(1)}, u32[]{:S(2)}, u32[]{:S(2)}) collective-permute-start(bf16[128,1024]{1,0:T(8,128)(2,1)S(1)} %attend.1.rest_0_), channel_id=1, source_target_pairs={{0,128},{1,129},{2,130},{3,131},{4,132},{5,133},{6,134},{7,135},{8... | collective-permute-start | bytes 786440 | tf_op jit(solution)/shard_map/ppermute | solution.py:36
  40.3 15.7 %collective-permute-start.15 = (bf16[128,1024]{1,0:T(8,128)(2,1)S(1)}, bf16[128,1024]{1,0:T(8,128)(2,1)S(1)}, u32[]{:S(2)}, u32[]{:S(2)}) collective-permute-start(bf16[128,1024]{1,0:T(8,128)(2,1)S(1)} %attend.1.rest_0_), channel_id=1, source_target_pairs={{0,64},{1,65},{2,66},{3,67},{4,68},{5,69},{6,70},{7,71},{8,72},{9,... | collective-permute-start | bytes 786440 | tf_op jit(solution)/shard_map/ppermute | solution.py:36
  56.1 12.4 %collective-permute-start.23 = (bf16[448,1024]{1,0:T(8,128)(2,1)S(1)}, bf16[448,1024]{1,0:T(8,128)(2,1)S(1)}, u32[]{:S(2)}, u32[]{:S(2)}) collective-permute-start(bf16[448,1024]{1,0:T(8,128)(2,1)S(1)} %collective-permute-done.22.rest_14_), channel_id=1, source_target_pairs={{1,17},{3,19},{5,21},{7,23},{9,25},{11,27},{13,29},{15,31},{16,0},... | collective-permute-start | bytes 2752520 | tf_op jit(solution)/shard_map/ppermute | solution.py:36
  57.5 9.0 %collective-permute-start.21 = (bf16[128,1024]{1,0:T(8,128)(2,1)S(1)}, bf16[128,1024]{1,0:T(8,128)(2,1)S(1)}, u32[]{:S(2)}, u32[]{:S(2)}) collective-permute-start(bf16[128,1024]{1,0:T(8,128)(2,1)S(1)} %collective-permute-done.18.rest_4_), channel_id=1, source_target_pairs={{0,192},{1,193},{2,194},{3,195},{4,196},{5,197},{6,198},{7,199},{8... | collective-permute-start | bytes 786440 | tf_op jit(solution)/shard_map/ppermute | solution.py:36
  58.6 9.1 %collective-permute-start.19 = (bf16[128,1024]{1,0:T(8,128)(2,1)S(1)}, bf16[128,1024]{1,0:T(8,128)(2,1)S(1)}, u32[]{:S(2)}, u32[]{:S(2)}) collective-permute-start(bf16[128,1024]{1,0:T(8,128)(2,1)S(1)} %collective-permute-done.18.rest_4_), channel_id=1, source_target_pairs={{0,64},{1,65},{2,66},{3,67},{4,68},{5,69},{6,70},{7,71},{8,72},{9,... | collective-permute-start | bytes 786440 | tf_op jit(solution)/shard_map/ppermute | solution.py:36
  59.6 8.8 %collective-permute-start.20 = (bf16[128,1024]{1,0:T(8,128)(2,1)S(1)}, bf16[128,1024]{1,0:T(8,128)(2,1)S(1)}, u32[]{:S(2)}, u32[]{:S(2)}) collective-permute-start(bf16[128,1024]{1,0:T(8,128)(2,1)S(1)} %collective-permute-done.16.rest_2_), channel_id=1, source_target_pairs={{0,1},{1,0},{2,3},{3,2},{4,5},{5,4},{6,7},{7,6},{8,9},{9,8},{10,11... | collective-permute-start | bytes 786440 | tf_op jit(solution)/shard_map/ppermute | solution.py:36
  71.4 14.5 %collective-permute-start.24 = (bf16[2,448,128]{2,1,0:T(8,128)(2,1)S(1)}, bf16[2,448,128]{2,1,0:T(8,128)(2,1)S(1)}, u32[]{:S(2)}, u32[]{:S(2)}) collective-permute-start(bf16[2,448,128]{2,1,0:T(8,128)(2,1)S(1)} %get-tuple-element.33), channel_id=1, source_target_pairs={{0,2},{1,3},{2,4},{3,5},{4,6},{5,7},{6,8},{7,9},{8,10},{9,11},{10,... | collective-permute-start | bytes 688136 | tf_op jit(solution)/shard_map/ppermute | solution.py:36
  73.4 12.5 %collective-permute-start.26 = (bf16[224,128]{1,0:T(8,128)(2,1)S(1)}, bf16[224,128]{1,0:T(8,128)(2,1)S(1)}, u32[]{:S(2)}, u32[]{:S(2)}) collective-permute-start(bf16[224,128]{1,0:T(8,128)(2,1)S(1)} %get-tuple-element.38), channel_id=1, source_target_pairs={{0,4},{1,5},{2,6},{3,7},{4,8},{5,9},{6,10},{7,11},{8,12},{9,13},{1... | collective-permute-start | bytes 172040 | tf_op jit(solution)/shard_map/ppermute | solution.py:36
  76.7 11.8 %collective-permute-start.25 = (bf16[2,448,128]{2,1,0:T(8,128)(2,1)S(1)}, bf16[2,448,128]{2,1,0:T(8,128)(2,1)S(1)}, u32[]{:S(2)}, u32[]{:S(2)}) collective-permute-start(bf16[2,448,128]{2,1,0:T(8,128)(2,1)S(1)} %get-tuple-element.34), channel_id=1, source_target_pairs={{0,14},{1,15},{2,0},{3,1},{4,2},{5,3},{6,4},{7,5},{8,6},{9,7},{10,... | collective-permute-start | bytes 688136 | tf_op jit(solution)/shard_map/ppermute | solution.py:36
  78.0 10.5 %collective-permute-start.28 = (bf16[224,128]{1,0:T(8,128)(2,1)S(1)}, bf16[224,128]{1,0:T(8,128)(2,1)S(1)}, u32[]{:S(2)}, u32[]{:S(2)}) collective-permute-start(bf16[224,128]{1,0:T(8,128)(2,1)S(1)} %get-tuple-element.40), channel_id=1, source_target_pairs={{0,12},{1,13},{2,14},{3,15},{4,0},{5,1},{6,2},{7,3},{8,4},{9,5},{1... | collective-permute-start | bytes 172040 | tf_op jit(solution)/shard_map/ppermute | solution.py:36
  86.0 8.7 %collective-permute-start.27 = (bf16[448,128]{1,0:T(8,128)(2,1)S(1)}, bf16[448,128]{1,0:T(8,128)(2,1)S(1)}, u32[]{:S(2)}, u32[]{:S(2)}) collective-permute-start(bf16[448,128]{1,0:T(8,128)(2,1)S(1)} %pad_maximum_fusion), channel_id=1, source_target_pairs={{0,4},{1,5},{2,6},{3,7},{4,8},{5,9},{6,10},{7,11},{8,12},{9,13},{1... | collective-permute-start | bytes 344072 | tf_op jit(solution)/shard_map/ppermute | solution.py:36
  88.5 7.0 %collective-permute-start.29 = (bf16[448,128]{1,0:T(8,128)(2,1)S(1)}, bf16[448,128]{1,0:T(8,128)(2,1)S(1)}, u32[]{:S(2)}, u32[]{:S(2)}) collective-permute-start(bf16[448,128]{1,0:T(8,128)(2,1)S(1)} %pad_maximum_fusion.1), channel_id=1, source_target_pairs={{0,12},{1,13},{2,14},{3,15},{4,0},{5,1},{6,2},{7,3},{8,4},{9,5},{1... | collective-permute-start | bytes 344072 | tf_op jit(solution)/shard_map/ppermute | solution.py:36
  95.6 13.0 %collective-permute-start.30 = (bf16[448,128]{1,0:T(8,128)(2,1)S(1)}, bf16[448,128]{1,0:T(8,128)(2,1)S(1)}, u32[]{:S(2)}, u32[]{:S(2)}) collective-permute-start(bf16[448,128]{1,0:T(8,128)(2,1)S(1)} %fusion.2), channel_id=1, source_target_pairs={{0,0},{1,1},{2,2},{3,3},{4,64},{5,65},{6,66},{7,67},{8,128},{9,129... | collective-permute-start | bytes 344072 | tf_op jit(solution)/shard_map/ppermute | solution.py:36
